TPU v7x, 512 devices: a whole 4x4x16 slice. The times are simulated.
512 devices in a mesh: row: 16 (over x, y), col: 32 (over z, core).
Axes of the slice: x: 4, y: 4, z: 16, core: 2. Of those that a mesh axis runs over, the one named last changes fastest.
Arguments:
- kernel: bfloat16 [16, 4, 32, 2, 256, 256], P('row', None, 'col'), as said below
Outputs:
- panels: float32 [16, 4, 2, 256, 256], P('row')
- schur: bfloat16 [16, 4, 32, 2, 256, 256], P('row', None, 'col')
Inputs may be any that keep to these rules, and one draw needn't show every extreme that they name: kernel describes a symmetric matrix whose leading 2 * 256 rows and columns form a positive definite block.
All inputs are finite; a program needn't handle non-finite values.
Results may differ from a plain program's by a relative error of at most 0.005.
Values may be sent and summed in bfloat16 or wider, within the bound.
A program may use at most 64 MiB of HBM per device.

v0:
```python
import jax
import jax.numpy as jnp
from jax import lax
from jax.sharding import PartitionSpec as P

PANELS = 2


def from_root(block, axis, source):
    block = jnp.where(lax.axis_index(axis) == source, block, jnp.zeros_like(block))
    return lax.psum(block, axis)


def factorize(block):
    lower_factor = jnp.linalg.cholesky(block)
    identity = jnp.eye(block.shape[0], dtype=jnp.float32)
    inverse = lax.linalg.triangular_solve(lower_factor, identity, left_side=True, lower=True)
    return (lower_factor, inverse)


def solve_rows(column, inverse):
    row_blocks = column.shape[0]
    block_width = column.shape[1]
    flat = column.astype(jnp.float32).reshape(row_blocks * block_width, block_width)
    solved = jnp.dot(flat, inverse.T, precision=lax.Precision.HIGHEST)
    return solved.reshape(row_blocks, block_width, block_width)


def per_device(kernel):
    row_count = lax.axis_size("row")
    col_count = lax.axis_size("col")
    my_row = lax.axis_index("row")
    my_col = lax.axis_index("col")
    blocks_here = kernel[0, :, 0]
    row_blocks = blocks_here.shape[0]
    col_blocks = blocks_here.shape[1]
    block_width = blocks_here.shape[2]
    stride = col_count // row_count
    row_ids = jnp.arange(row_blocks, dtype=jnp.int32) * row_count + my_row
    col_ids = jnp.arange(col_blocks, dtype=jnp.int32) * col_count + my_col
    panel_list = []
    for current in range(PANELS):
        below = (row_ids > current)[:, None, None]
        at_diagonal = (row_ids == current)[:, None, None]
        lower_factor, inverse = factorize(blocks_here[0, 0].astype(jnp.float32))
        inverse = from_root(inverse, "row", current)
        solved = solve_rows(blocks_here[:, 0], inverse)
        strict = jnp.where(below, solved, jnp.float32(0.0))
        panel_step = jnp.where(at_diagonal, lower_factor[None], strict)
        panel_step = from_root(panel_step, "col", current)
        rounded = jnp.where(below, panel_step, jnp.float32(0.0)).astype(jnp.bfloat16)
        grouped = rounded.reshape(col_blocks, stride, block_width, block_width)
        picked = lax.dynamic_index_in_dim(grouped, my_col // row_count, 1, keepdims=False)
        mirror = from_root(picked, "row", my_col % row_count)
        panel_list.append(panel_step)
        update = jnp.einsum("iab,jcb->ijac", rounded, mirror, preferred_element_type=jnp.float32)
        blocks_here = (blocks_here.astype(jnp.float32) - update).astype(jnp.bfloat16)
    keep = (row_ids[:, None] >= PANELS) & (col_ids[None, :] >= PANELS)
    schur = jnp.where(keep[:, :, None, None], blocks_here, jnp.zeros((), jnp.bfloat16))
    panels = jnp.stack(panel_list, axis=1)
    return (panels[None], schur[None, :, None])


def solution(mesh):
    in_specs = (P("row", None, "col", None, None, None),)
    out_specs = (P("row", None, None, None, None), P("row", None, "col", None, None, None))
    return jax.shard_map(
        per_device, mesh=mesh, in_specs=in_specs, out_specs=out_specs, check_vma=False
    )
```

profile of v0, /device:TPU:6, one launch (start us, length us, event | category | flops | bytes accessed | tf_op | source)
XLA Modules:
  0.0 1041.8 jit_solution(3783065233711324212)
XLA Ops:
  7.3 1.5 copy.12
  9.0 11.7 %cholesky.130 = f32[128,128]{1,0:T(8,128)S(1)} custom-call(f32[128,128]{1,0:T(8,128)S(1)} %cholesky.194), custom_call_target="Cholesky" | custom-call | tf_op jit(solution)/shard_map/jit(cholesky)/cholesky | solution.py:15
  20.7 9.8 custom-call.13
  31.0 11.7 %cholesky.147 = f32[128,128]{1,0:T(8,128)S(1)} custom-call(f32[128,128]{1,0:T(8,128)S(1)} %convolution_subtract_fusion.3), custom_call_target="Cholesky" | custom-call | tf_op jit(solution)/shard_map/jit(cholesky)/cholesky | solution.py:15
  44.9 0.7 fusion.16
  45.7 4.1 while.4
  46.4 1.3 bitcast_dynamic-update-slice_fusion.4
  48.4 1.3 bitcast_dynamic-update-slice_fusion.4
  49.8 19.9 %custom-call.14 = f32[2,128,128]{1,2,0:T(8,128)S(1)} custom-call(f32[2,128,128]{2,1,0:T(8,128)S(1)} %get-tuple-element.18), custom_call_target="InvertDiagBlocksLowerTriangular" | custom-call | tf_op jit(solution)/shard_map/triangular_solve/custom-call.0 | solution.py:17
  71.6 118.8 %all-reduce.8.cloned.1.call-done = f32[256,256]{1,0:T(8,128)} async-done(((f32[256,256]{1,0:T(8,128)}), f32[256,256]{1,0:T(8,128)}) %all-reduce.8.cloned.1.call-update) | async-done | bytes 262160 | tf_op jit(solution)/shard_map/psum | solution.py:11
  190.4 1.6 convolution_bitcast_fusion
  192.3 2.1 select_select_fusion
  194.5 210.1 %all-reduce.10.cloned.1.call-done = f32[4,256,256]{2,1,0:T(8,128)} async-done(((f32[4,256,256]{2,1,0:T(8,128)}), f32[4,256,256]{2,1,0:T(8,128)}) %all-reduce.10.cloned.1.call-update) | async-done | bytes 1048592 | tf_op jit(solution)/shard_map/psum | solution.py:11
  404.7 1.4 select_convert_fusion.1
  406.8 116.2 %all-reduce.12.cloned.1.call-done = bf16[2,256,256]{2,1,0:T(8,128)(2,1)} async-done(((bf16[2,256,256]{2,1,0:T(8,128)(2,1)}), bf16[2,256,256]{2,1,0:T(8,128)(2,1)}) %all-reduce.12.cloned.1.call-update) | async-done | bytes 262160 | tf_op jit(solution)/shard_map/psum | solution.py:11
  523.1 1.4 fusion.1
  524.7 11.7 %cholesky.164 = f32[128,128]{1,0:T(8,128)S(1)} custom-call(f32[128,128]{1,0:T(8,128)S(1)} %cholesky.197), custom_call_target="Cholesky" | custom-call | tf_op jit(solution)/shard_map/jit(cholesky)/cholesky | solution.py:15
  537.1 9.8 custom-call.15
  547.4 11.7 %cholesky.181 = f32[128,128]{1,0:T(8,128)S(1)} custom-call(f32[128,128]{1,0:T(8,128)S(1)} %convolution_subtract_fusion.2), custom_call_target="Cholesky" | custom-call | tf_op jit(solution)/shard_map/jit(cholesky)/cholesky | solution.py:15
  561.2 4.2 while.5
  562.0 1.4 bitcast_dynamic-update-slice_fusion.5
  564.0 1.4 bitcast_dynamic-update-slice_fusion.5
  565.4 19.7 %custom-call.16 = f32[2,128,128]{1,2,0:T(8,128)S(1)} custom-call(f32[2,128,128]{2,1,0:T(8,128)S(1)} %get-tuple-element.19), custom_call_target="InvertDiagBlocksLowerTriangular" | custom-call | tf_op jit(solution)/shard_map/triangular_solve/custom-call.0 | solution.py:17
  586.8 114.5 %all-reduce.14.cloned.1.call-done = f32[256,256]{1,0:T(8,128)} async-done(((f32[256,256]{1,0:T(8,128)}), f32[256,256]{1,0:T(8,128)}) %all-reduce.14.cloned.1.call-update) | async-done | bytes 262160 | tf_op jit(solution)/shard_map/psum | solution.py:11
  701.3 2.7 fusion.5
  704.1 210.1 %all-reduce.16.cloned.1.call-done = f32[4,256,256]{2,1,0:T(8,128)} async-done(((f32[4,256,256]{2,1,0:T(8,128)}), f32[4,256,256]{2,1,0:T(8,128)}) %all-reduce.16.cloned.1.call-update) | async-done | bytes 1048592 | tf_op jit(solution)/shard_map/psum | solution.py:11
  914.2 1.5 select_convert_fusion
  915.7 0.8 copy-done.2
  917.5 1.5 copy.22
  918.9 113.3 %all-reduce.18.cloned.1.call-done = bf16[2,256,256]{2,1,0:T(8,128)(2,1)} async-done(((bf16[2,256,256]{2,1,0:T(8,128)(2,1)}), bf16[2,256,256]{2,1,0:T(8,128)(2,1)}) %all-reduce.18.cloned.1.call-update) | async-done | bytes 262160 | tf_op jit(solution)/shard_map/psum | solution.py:11
  1032.2 1.4 fusion.3
  1033.6 1.3 copy.23
  (73 shorter events, 12.0 us)
Async XLA Ops:
  7.2 183.2 %all-reduce.8.cloned.1.call-start = ((), (), s32[]{:S(2)}) async-start(), calls=%async_computation | async-start | bytes 524288 | tf_op jit(solution)/shard_map/psum | solution.py:11
  71.3 333.4 %all-reduce.10.cloned.1.call-start = ((), (), s32[]{:S(2)}) async-start(), calls=%async_computation.1 | async-start | bytes 2097152 | tf_op jit(solution)/shard_map/psum | solution.py:11
  194.5 328.6 %all-reduce.12.cloned.1.call-start = ((), (), s32[]{:S(2)}) async-start(), calls=%async_computation.2 | async-start | bytes 524288 | tf_op jit(solution)/shard_map/psum | solution.py:11
  406.8 294.5 %all-reduce.14.cloned.1.call-start = ((), (), s32[]{:S(2)}) async-start(), calls=%async_computation.3 | async-start | bytes 524288 | tf_op jit(solution)/shard_map/psum | solution.py:11
  586.8 327.5 %all-reduce.16.cloned.1.call-start = ((), (), s32[]{:S(2)}) async-start(), calls=%async_computation.4 | async-start | bytes 2097152 | tf_op jit(solution)/shard_map/psum | solution.py:11
  704.0 213.3 %copy-start = (f32[4,256,256]{2,1,0:T(8,128)S(1)}, f32[4,256,256]{2,1,0:T(8,128)}, u32[]{:S(2)}) copy-start(f32[4,256,256]{2,1,0:T(8,128)} %all-reduce.10.cloned.1.call-done) | copy-start | bytes 3145732
  704.0 328.2 %all-reduce.18.cloned.1.call-start = ((), (), s32[]{:S(2)}) async-start(), calls=%async_computation.5 | async-start | bytes 524288 | tf_op jit(solution)/shard_map/psum | solution.py:11
  914.2 3.1 copy-start.1
  915.7 0.8 copy-start.2
  917.4 114.8 %copy-start.3 = (bf16[4,256,256]{2,1,0:T(8,128)(2,1)S(1)}, bf16[4,256,256]{2,1,0:T(8,128)(2,1)}, u32[]{:S(2)}) copy-start(bf16[4,256,256]{2,1,0:T(8,128)(2,1)} %copy-done.2) | copy-start | bytes 1572868
Sparse Core Ops, SparseCore 0:
  71.4 118.9 all-reduce.7
  194.6 210.0 all-reduce.9
  408.4 114.6 all-reduce.11
  586.9 114.3 all-reduce.13
  704.1 210.0 all-reduce.15
  917.6 114.5 all-reduce.17
where the time goes:
time: 1040 us
  waiting for transfers between devices  883 us (85%)
  other arithmetic  117 us (11%)
  between operations  17.1 us (2%)
  local copies, waits for them, and re-layouts  14 us (1%)
    psum x6, waiting for transfers between devices, from_root(): return lax.psum(block, axis)  883 us
    another operation x13, other arithmetic, factorize(): lower_factor = jnp.linalg.cholesky(block)  68.6 us
    another operation x5, other arithmetic, factorize(): lax.linalg.triangular_solve(lower_factor, identity, left_side=True, lower...  40.3 us
  transfers between devices with their start and end apart: 6, of which 6 were waited for; matrix products, arithmetic and copies ran while one was open for 0% of the time, Pallas kernels for 0%

commit v1 on v0

v1 whole, which is shorter than its diff:
```python
import functools

import jax
import jax.numpy as jnp
from jax import lax
from jax.experimental import pallas as pl
from jax.experimental.pallas import tpu as pltpu
from jax.sharding import PartitionSpec as P

MESH = pl.DeviceIdType.MESH
HI = lax.Precision.HIGHEST
GROUPS = ((0, 4), (4, 7), (7, 8))
SKIP = {0: 3, 3: 6, 6: 8, 13: 10, 10: 9}
BACK = {0: 13, 3: 2, 2: 1, 6: 5, 5: 4, 8: 7, 13: 14, 14: 15, 10: 11, 11: 12}


def lookup(key, pairs):
    value = jnp.int32(0)
    for k, v in pairs.items():
        value = jnp.where(key == k, jnp.int32(v), value)
    return value


def member(key, keys):
    hit = key == keys[0]
    for k in keys[1:]:
        hit = jnp.logical_or(hit, key == k)
    return hit


def eliminate(strips):
    row_iota = lax.broadcasted_iota(jnp.int32, (8, 128), 0)

    def row(v, i):
        return jnp.broadcast_to(v[i : i + 1, :], (8, 128))

    pivots = []
    for s in range(8):
        cols = []
        for t in range(s, 8):
            cols.append([jnp.broadcast_to(strips[t][:, 8 * s + i : 8 * s + i + 1], (8, 128)) for i in range(8)])
        head = strips[s]
        pivot = jnp.zeros((8, 128), jnp.float32)
        recips = []
        for i in range(8):
            own = cols[0][i]
            recip = 1.0 / row(own, i)
            pivot = jnp.where(row_iota == i, own, pivot)
            for j in range(i + 1, 8):
                factor = row(own, j) * recip
                for t in range(8 - s):
                    cols[t][j] = cols[t][j] - cols[t][i] * factor
            head = head - jnp.where(row_iota > i, own * recip, 0.0) * row(head, i)
            recips.append(recip)
        strips[s] = head
        pivots.append(pivot)
        heads = [row(head, i) * recips[i] for i in range(8)]
        for t in range(s + 1, 8):
            rest = strips[t]
            for i in range(8):
                rest = rest - cols[t - s][i] * heads[i]
            strips[t] = rest
    return strips, pivots


def dot32(a, b, dims):
    return lax.dot_general(a, b, (dims, ((), ())), precision=HI, preferred_element_type=jnp.float32)


def factor_two(q, g, xs):
    col_iota = lax.broadcasted_iota(jnp.int32, (8, 128), 1)
    row_iota = lax.broadcasted_iota(jnp.int32, (8, 128), 0)
    base = pl.multiple_of(q * 128, 128)
    for h in range(2):
        first = pl.multiple_of(base + 64 * h, 64)
        tile = g[pl.ds(first, 64), pl.ds(base, 128)]
        if h:
            tile = pltpu.roll(tile, 64, 1)
        strips = []
        for s in range(8):
            unit = jnp.where(col_iota == row_iota + 8 * s + 64, 1.0, 0.0)
            strips.append(jnp.where(col_iota < 64, tile[8 * s : 8 * s + 8, :], unit))
        strips, pivots = eliminate(strips)
        inverse = jnp.concatenate([a * lax.rsqrt(b) for a, b in zip(strips, pivots)], axis=0)[:, 64:]
        xs[2 * q + h] = jnp.concatenate([inverse[32:], inverse[:32]], axis=1)
        u = dot32(inverse, g[pl.ds(first, 64), :], ((1,), (0,)))
        g[...] = g[...] - dot32(u, u, ((0,), (0,)))


def gather_kernel(
    kern, acol, brow, gcol, xs,
    gbuf, g, p_send, p_recv, p_sib_send, p_sib_recv, m_send, m_recv,
    g_send, g_recv, g_sib_send, g_sib_recv, x_send, x_recv, lead_send, lead_recv, loc,
):
    r = lax.axis_index("row")
    c = lax.axis_index("col")
    x, y = lax.div(r, 4), lax.rem(r, 4)
    z, k = lax.div(c, 2), lax.rem(c, 2)
    sibling = c + 1 - 2 * k
    root = jnp.logical_and(r == 0, c == 0)
    head = z == 0
    skip_to = lookup(z, SKIP)
    back_to = lookup(z, BACK)
    has_skip = member(z, list(SKIP))
    has_back = member(z, list(BACK))
    parent = lookup(z, {v: q for q, v in list(SKIP.items()) + list(BACK.items())})

    def remote(src, dst, send, recv, row, col):
        return pltpu.make_async_remote_copy(
            src_ref=src, dst_ref=dst, send_sem=send, recv_sem=recv, device_id=(row, col), device_id_type=MESH
        )

    barrier = pltpu.get_barrier_semaphore()

    def signal(row, col):
        pl.semaphore_signal(barrier, inc=1, device_id=(row, col), device_id_type=MESH)

    own_panel = pltpu.make_async_copy(kern.at[0, :, 0, 0], acol.at[:, k], loc.at[0])
    own_rows = pltpu.make_async_copy(kern.at[0, 0, 0], brow.at[lax.rem(r, 2)], loc.at[1])
    own_piece = pltpu.make_async_copy(kern.at[0, 0, 0, 0, pl.ds(0, 32)], gcol.at[k, pl.ds(0, 32)], loc.at[2])
    own_lead = pltpu.make_async_copy(kern.at[0, 0, 0, 0], gbuf.at[0], loc.at[3])
    at_first = jnp.logical_and(r == 0, head)

    @pl.when(head)
    def _():
        own_panel.start()

    @pl.when(r < 2)
    def _():
        own_rows.start()

    @pl.when(at_first)
    def _():
        own_piece.start()

    @pl.when(root)
    def _():
        own_lead.start()
        signal(jnp.int32(1), jnp.int32(1))

    def greet(d, carry):
        signal(lax.rem(r + d, 16), c)
        return carry

    lax.fori_loop(1, 16, greet, 0)
    signal(r, sibling)

    @pl.when(jnp.logical_not(head))
    def _():
        signal(r, k)

        @pl.when(parent != 0)
        def _():
            signal(r, 2 * parent + k)

    @pl.when(jnp.logical_and(jnp.logical_and(head, k == 1), r != 0))
    def _():
        signal(jnp.int32(0), jnp.int32(0))

    children = has_skip.astype(jnp.int32) + has_back.astype(jnp.int32)
    lead_one = jnp.logical_and(r == 0, c == 1)
    lead_two = jnp.logical_and(r == 1, c == 1)
    count = 16 + jnp.where(head, 15, children) + jnp.where(root, 15, 0) + jnp.where(lead_two, 1, 0)
    pl.semaphore_wait(barrier, count)

    @pl.when(head)
    def _():
        own_panel.wait()

    @pl.when(r < 2)
    def _():
        own_rows.wait()

    @pl.when(at_first)
    def _():
        own_piece.wait()

    def panel_copies(i):
        block = acol.at[i, k]
        return (
            (has_skip, remote(block, block, p_send.at[i, 0], p_recv.at[i], r, 2 * skip_to + k)),
            (has_back, remote(block, block, p_send.at[i, 1], p_recv.at[i], r, 2 * back_to + k)),
            (None, remote(block, block, p_sib_send.at[i], p_sib_recv.at[i], r, sibling)),
        )

    def start_all(copies):
        for cond, copy in copies:
            if cond is None:
                copy.start()
            else:

                @pl.when(cond)
                def _(copy=copy):
                    copy.start()

    def finish_all(copies):
        for cond, copy in copies:
            if cond is None:
                copy.wait_send()
            else:

                @pl.when(cond)
                def _(copy=copy):
                    copy.wait_send()

    def panel_step(i):
        @pl.when(jnp.logical_not(head))
        def _():
            panel_copies(i)[0][1].wait_recv()

        start_all(panel_copies(i))

    def mirror_copies(s, j):
        block = brow.at[s, j]
        right, left = lax.rem(x + 1, 4), lax.rem(x + 3, 4)
        up, down = lax.rem(y + 1, 4), lax.rem(y + 3, 4)
        at_x = x == 0
        at_y = y == s
        if s == 0:
            ring_up, ring_down = y == 0, jnp.logical_or(y == 0, y == 3)
        else:
            ring_up, ring_down = jnp.logical_or(y == 1, y == 2), y == 1
        if s == 0:
            line_up, line_down = jnp.logical_or(x == 0, x == 1), x == 0
        else:
            line_up, line_down = x == 0, jnp.logical_or(x == 0, x == 3)
        if j == 0:
            ring_up = jnp.logical_and(ring_up, at_x)
            ring_down = jnp.logical_and(ring_down, at_x)
        else:
            line_up = jnp.logical_and(line_up, at_y)
            line_down = jnp.logical_and(line_down, at_y)
        targets = (
            (ring_up, x * 4 + up),
            (ring_down, x * 4 + down),
            (line_up, right * 4 + y),
            (line_down, left * 4 + y),
        )
        out = []
        for n, (cond, row) in enumerate(targets):
            out.append((cond, remote(block, block, m_send.at[2 * s + j, n], m_recv.at[2 * s + j], row, c)))
        return out

    def mirror_step(s, j):
        @pl.when(r != s)
        def _():
            mirror_copies(s, j)[0][1].wait_recv()

        start_all(mirror_copies(s, j))

    def piece(owner):
        return gcol.at[k, pl.ds(pl.multiple_of(32 * owner, 32), 32)]

    def scatter(i):
        owner = 8 * r + i
        return remote(
            kern.at[0, 0, 0, 0, pl.ds(32 * i, 32)], piece(owner), g_send.at[i], g_recv.at[owner], owner, c
        )

    def piece_down(d):
        return remote(piece(r), piece(r), g_send.at[d + 7], g_recv.at[r], r, 2 * d + k)

    def piece_across(d):
        return remote(piece(r), piece(r), g_send.at[d + 22], g_recv.at[r], lax.rem(r + d, 16), c)

    def piece_from(owner):
        return remote(piece(owner), piece(owner), g_send.at[0], g_recv.at[owner], r, sibling)

    leading_pair = remote(gcol.at[k], gcol.at[k], g_sib_send, g_sib_recv, r, sibling)

    def loop(lo, hi, body):
        def step(d, carry):
            body(d)
            return carry

        lax.fori_loop(lo, hi, step, 0)

    scattering = jnp.logical_and(head, r < 2)
    first_piece = jnp.where(r == 0, 1, 0)

    def leading_scatter():
        @pl.when(scattering)
        def _():
            loop(first_piece, 8, lambda i: scatter(i).start())

    def leading_spread():
        @pl.when(jnp.logical_not(at_first))
        def _():
            piece_from(r).wait_recv()

        @pl.when(head)
        def _():
            loop(1, 16, lambda d: piece_down(d).start())

        loop(1, 16, lambda d: piece_across(d).start())

    def leading_finish():
        loop(1, 16, lambda d: piece_from(lax.rem(r + d, 16)).wait_recv())
        leading_pair.start()

    def inverse_copy(n, slot, row, col):
        lo, hi = GROUPS[n]
        block = xs.at[pl.ds(lo, hi - lo)]
        return remote(block, block, x_send.at[n, slot], x_recv.at[n], row, col)

    def inverse_first(n, act):
        loop(1, 16, lambda d: act(inverse_copy(n, 14 + d, lax.rem(d + 8, 15) + 1, jnp.int32(0))))
        loop(1, 16, lambda d: act(inverse_copy(n, 29 + d, lax.rem(d + 8, 15) + 1, jnp.int32(1))))
        act(inverse_copy(n, 45, jnp.int32(0), jnp.int32(1)))

    def inverse_down(n, act):
        loop(1, 16, lambda d: act(inverse_copy(n, d - 1, r, 2 * (lax.rem(d + 6, 15) + 1) + k)))

    start = lambda copy: copy.start()
    done = lambda copy: copy.wait_send()

    def lead_copy(n):
        zero = jnp.int32(0)
        return remote(kern.at[0, 0, 0, 0], gbuf.at[n + 1], lead_send.at[n], lead_recv.at[n], zero, zero)

    @pl.when(lead_one)
    def _():
        lead_copy(0).start()

    @pl.when(lead_two)
    def _():
        lead_copy(1).start()

    leading_scatter()

    @pl.when(root)
    def _():
        for i in range(4):
            panel_step(i)
        mirror_step(0, 0)
        mirror_step(0, 1)
        leading_spread()
        own_lead.wait()
        lead_copy(0).wait_recv()
        lead_copy(1).wait_recv()
        g[0:256, 0:256] = gbuf[0].astype(jnp.float32)
        g[0:256, 256:512] = gbuf[1].astype(jnp.float32)
        g[256:512, 256:512] = gbuf[2].astype(jnp.float32)
        g[256:512, 0:256] = jnp.zeros((256, 256), jnp.float32)

        def two(q, carry):
            factor_two(q, g, xs)
            return carry

        lax.fori_loop(0, 2, two, 0)
        inverse_first(0, start)
        inverse_down(0, start)
        lax.fori_loop(2, 4, two, 0)
        for n in (1, 2):
            inverse_first(n, start)
            inverse_down(n, start)
        mirror_step(1, 0)
        mirror_step(1, 1)
        leading_finish()
        leading_pair.wait_recv()

    @pl.when(jnp.logical_not(root))
    def _():
        for s, j in ((0, 0), (1, 0), (0, 1), (1, 1)):
            mirror_step(s, j)
        leading_spread()
        for i in range(4):
            panel_step(i)
        leading_finish()
        leading_pair.wait_recv()
        for n in range(3):
            inverse_copy(n, 0, r, sibling).wait_recv()

            @pl.when(head)
            def _(n=n):
                inverse_down(n, start)

    for i in range(4):
        panel_copies(i)[2][1].wait_recv()
    for i in range(4):
        finish_all(panel_copies(i))
    for s in range(2):
        for j in range(2):
            finish_all(mirror_copies(s, j))

    @pl.when(lead_one)
    def _():
        lead_copy(0).wait_send()

    @pl.when(lead_two)
    def _():
        lead_copy(1).wait_send()

    @pl.when(scattering)
    def _():
        loop(first_piece, 8, lambda i: scatter(i).wait_send())

    @pl.when(head)
    def _():
        loop(1, 16, lambda d: piece_down(d).wait_send())
        for n in range(3):
            inverse_down(n, done)

    @pl.when(root)
    def _():
        for n in range(3):
            inverse_first(n, done)

    loop(1, 16, lambda d: piece_across(d).wait_send())
    leading_pair.wait_send()


def gather(kernel):
    bf16 = jnp.bfloat16
    return pl.pallas_call(
        gather_kernel,
        out_shape=(
            jax.ShapeDtypeStruct((4, 2, 256, 256), bf16),
            jax.ShapeDtypeStruct((2, 2, 256, 256), bf16),
            jax.ShapeDtypeStruct((2, 512, 256), bf16),
            jax.ShapeDtypeStruct((8, 32, 128), jnp.float32),
        ),
        in_specs=[pl.BlockSpec(memory_space=pl.ANY)],
        out_specs=(
            pl.BlockSpec(memory_space=pl.ANY),
            pl.BlockSpec(memory_space=pl.ANY),
            pl.BlockSpec(memory_space=pl.ANY),
            pl.BlockSpec(memory_space=pltpu.VMEM),
        ),
        scratch_shapes=[
            pltpu.VMEM((3, 256, 256), bf16),
            pltpu.VMEM((512, 512), jnp.float32),
            pltpu.SemaphoreType.DMA((4, 2)),
            pltpu.SemaphoreType.DMA((4,)),
            pltpu.SemaphoreType.DMA((4,)),
            pltpu.SemaphoreType.DMA((4,)),
            pltpu.SemaphoreType.DMA((4, 4)),
            pltpu.SemaphoreType.DMA((4,)),
            pltpu.SemaphoreType.DMA((38,)),
            pltpu.SemaphoreType.DMA((16,)),
            pltpu.SemaphoreType.DMA,
            pltpu.SemaphoreType.DMA,
            pltpu.SemaphoreType.DMA((3, 46)),
            pltpu.SemaphoreType.DMA((3,)),
            pltpu.SemaphoreType.DMA((2,)),
            pltpu.SemaphoreType.DMA((2,)),
            pltpu.SemaphoreType.DMA((4,)),
        ],
        compiler_params=pltpu.CompilerParams(
            collective_id=0, has_side_effects=True, vmem_limit_bytes=24 * 1024 * 1024
        ),
        name="gather_and_factor",
    )(kernel)


def split(a):
    high = a.astype(jnp.bfloat16)
    rest = a - high.astype(jnp.float32)
    middle = rest.astype(jnp.bfloat16)
    low = (rest - middle.astype(jnp.float32)).astype(jnp.bfloat16)
    return high, middle, low


def update_kernel(kern, acol, brow, gcol, xs, panels, schur, aug, parts):
    r = lax.axis_index("row")
    c = lax.axis_index("col")
    aug[:, 0:256] = gcol[0].astype(jnp.float32)
    aug[:, 256:512] = gcol[1].astype(jnp.float32)
    rows = lax.broadcasted_iota(jnp.int32, (512, 512), 0)
    cols = lax.broadcasted_iota(jnp.int32, (512, 512), 1)
    aug[:, 512:1024] = jnp.where(rows == cols, 1.0, 0.0)
    for s in range(8):
        packed = xs[s]
        inverse = jnp.concatenate([packed[:, 64:128], packed[:, 0:64]], axis=0)
        lines = dot32(inverse, aug[64 * s : 64 * s + 64, :], ((1,), (0,)))
        aug[64 * s : 64 * s + 64, :] = lines
        if s < 7:
            rest = pl.ds(64 * (s + 1), 512 - 64 * (s + 1))
            aug[rest, :] = aug[rest, :] - dot32(lines[:, 64 * (s + 1) : 512], lines, ((0,), (0,)))
    for n, part in enumerate(split(aug[:, 512:1024])):
        parts[n] = part

    mirror = []
    for j in range(2):
        total = jnp.zeros((512, 256), jnp.float32)
        for n in range(3):
            for s in range(2):
                total = total + jnp.dot(
                    parts[n, :, 256 * s : 256 * s + 256], brow[s, j], preferred_element_type=jnp.float32
                )
        mirror.append(total.astype(jnp.bfloat16))
    tri = lax.broadcasted_iota(jnp.int32, (256, 256), 0) >= lax.broadcasted_iota(jnp.int32, (256, 256), 1)
    for i in range(4):
        total = jnp.zeros((256, 512), jnp.float32)
        for n in range(3):
            for s in range(2):
                total = total + lax.dot_general(
                    acol[i, s], parts[n, :, 256 * s : 256 * s + 256],
                    (((1,), (1,)), ((), ())), preferred_element_type=jnp.float32,
                )
        first, second = total[:, 0:256], total[:, 256:512]
        if i == 0:
            first = jnp.where(jnp.logical_or(r != 0, tri), first, 0.0)
            second = jnp.where(jnp.logical_or(r > 1, jnp.logical_and(r == 1, tri)), second, 0.0)
        panels[0, i, 0] = first
        panels[0, i, 1] = second
        left = total.astype(jnp.bfloat16)
        for j in range(2):
            change = jnp.dot(left, mirror[j], preferred_element_type=jnp.float32)
            out = (kern[0, i, 0, j].astype(jnp.float32) - change).astype(jnp.bfloat16)
            if i == 0:
                out = jnp.where(r >= 2, out, jnp.zeros_like(out))
            if j == 0:
                out = jnp.where(c >= 2, out, jnp.zeros_like(out))
            schur[0, i, 0, j] = out


def update(kernel, acol, brow, gcol, xs):
    return pl.pallas_call(
        update_kernel,
        out_shape=(
            jax.ShapeDtypeStruct((1, 4, 2, 256, 256), jnp.float32),
            jax.ShapeDtypeStruct((1, 4, 1, 2, 256, 256), jnp.bfloat16),
        ),
        in_specs=[pl.BlockSpec(memory_space=pltpu.VMEM)] * 5,
        out_specs=(pl.BlockSpec(memory_space=pltpu.VMEM), pl.BlockSpec(memory_space=pltpu.VMEM)),
        scratch_shapes=[pltpu.VMEM((512, 1024), jnp.float32), pltpu.VMEM((3, 512, 512), jnp.bfloat16)],
        compiler_params=pltpu.CompilerParams(vmem_limit_bytes=48 * 1024 * 1024),
        name="solve_and_update",
    )(kernel, acol, brow, gcol, xs)


def per_device(kernel):
    return update(kernel, *gather(kernel))


def solution(mesh):
    in_specs = (P("row", None, "col", None, None, None),)
    out_specs = (P("row", None, None, None, None), P("row", None, "col", None, None, None))
    return jax.shard_map(per_device, mesh=mesh, in_specs=in_specs, out_specs=out_specs, check_vma=False)
```

time: 1040 us -> 125 us (0.12)
  the two profiles are of different devices: /device:TPU:6 before, /device:TPU:9 now
where the time goes in v1:
time: 125 us
  Pallas kernels  122 us (98%)
  local copies, waits for them, and re-layouts  2.44 us (2%)
    pallas_call x1, Pallas kernels, gather(): pl.pallas_call(gather_kernel, out_shape=(jax.ShapeDtypeStruct((4, 2, 256,...  108 us
    pallas_call x1, Pallas kernels, update(): pl.pallas_call(update_kernel, out_shape=(jax.ShapeDtypeStruct((1, 4, 2, 2...  13.7 us

profile of v1, /device:TPU:9, one launch (start us, length us, event | category | flops | bytes accessed | tf_op | source)
XLA Modules:
  0.0 124.9 jit_solution(13097977481696427589)
XLA Ops:
  0.6 0.0 copy-start
  0.6 1.2 copy-done
  1.9 108.1 %gather_and_factor.1 = (bf16[4,2,256,256]{3,2,1,0:T(8,128)(2,1)S(1)}, bf16[2,2,256,256]{3,2,1,0:T(8,128)(2,1)S(1)}, bf16[2,512,256]{2,1,0:T(8,128)(2,1)S(1)}, f32[8,32,128]{2,1,0:T(8,128)S(1)}) custom-call(bf16[1,4,1,2,256,256]{5,4,3,2,1,0:T(8,128)(2,1)S(1)} %copy-done), custom_call_target="tpu_custom_call" | custom-call | tf_op jit(solution)/shard_map/gather_and_factor/pallas_call | solution.py:415
  110.0 0.0 copy-start.1
  110.0 1.2 copy-done.1
  111.2 13.7 %solve_and_update.1 = (f32[1,4,2,256,256]{4,3,2,1,0:T(8,128)}, bf16[1,4,1,2,256,256]{5,4,3,2,1,0:T(8,128)(2,1)}) custom-call(bf16[1,4,1,2,256,256]{5,4,3,2,1,0:T(8,128)(2,1)S(1)} %copy-done.1, bf16[4,2,256,256]{3,2,1,0:T(8,128)(2,1)S(1)} %get-tuple-element.6.acol, bf16[2,2,256,256]{3,2,1,0:T(8,128)(2,1)S(1)} %get-tuple-element.7.brow, ...), custom_call_target="tpu_custom_call" | custom-call | tf_op jit(solution)/shard_map/solve_and_update/pallas_call | solution.py:519
Async XLA Ops:
  0.6 1.2 copy-start
  110.0 1.2 copy-start.1

commit v2 on v0

v2 whole, which is shorter than its diff:
```python
import functools

import jax
import jax.numpy as jnp
from jax import lax
from jax.experimental import pallas as pl
from jax.experimental.pallas import tpu as pltpu
from jax.sharding import PartitionSpec as P

MESH = pl.DeviceIdType.MESH
HI = lax.Precision.HIGHEST
GROUPS = ((0, 2), (2, 3), (3, 4))
HEAD = 1
SKIP = {0: 3, 3: 6, 6: 8, 13: 10, 10: 9}
BACK = {0: 13, 3: 2, 2: 1, 6: 5, 5: 4, 8: 7, 13: 14, 14: 15, 10: 11, 11: 12}


def lookup(key, pairs):
    value = jnp.int32(0)
    for k, v in pairs.items():
        value = jnp.where(key == k, jnp.int32(v), value)
    return value


def member(key, keys):
    hit = key == keys[0]
    for k in keys[1:]:
        hit = jnp.logical_or(hit, key == k)
    return hit


def eliminate(strips):
    row_iota = lax.broadcasted_iota(jnp.int32, (8, 128), 0)

    def row(v, i):
        return jnp.broadcast_to(v[i : i + 1, :], (8, 128))

    pivots = []
    for s in range(8):
        cols = []
        for t in range(s, 8):
            cols.append([jnp.broadcast_to(strips[t][:, 8 * s + i : 8 * s + i + 1], (8, 128)) for i in range(8)])
        head = strips[s]
        pivot = jnp.zeros((8, 128), jnp.float32)
        recips = []
        for i in range(8):
            own = cols[0][i]
            recip = 1.0 / row(own, i)
            pivot = jnp.where(row_iota == i, own, pivot)
            for j in range(i + 1, 8):
                factor = row(own, j) * recip
                for t in range(8 - s):
                    cols[t][j] = cols[t][j] - cols[t][i] * factor
            head = head - jnp.where(row_iota > i, own * recip, 0.0) * row(head, i)
            recips.append(recip)
        strips[s] = head
        pivots.append(pivot)
        heads = [row(head, i) * recips[i] for i in range(8)]
        for t in range(s + 1, 8):
            rest = strips[t]
            for i in range(8):
                rest = rest - cols[t - s][i] * heads[i]
            strips[t] = rest
    return strips, pivots


def dot32(a, b, dims):
    return lax.dot_general(a, b, (dims, ((), ())), precision=HI, preferred_element_type=jnp.float32)


def factor_block(q, h, g, store):
    col_iota = lax.broadcasted_iota(jnp.int32, (8, 128), 1)
    row_iota = lax.broadcasted_iota(jnp.int32, (8, 128), 0)
    base = pl.multiple_of(q * 128, 128)
    first = pl.multiple_of(base + 64 * h, 64)
    tile = g[pl.ds(first, 64), pl.ds(base, 128)]
    if h:
        tile = pltpu.roll(tile, 64, 1)
    strips = []
    for s in range(8):
        unit = jnp.where(col_iota == row_iota + 8 * s + 64, 1.0, 0.0)
        strips.append(jnp.where(col_iota < 64, tile[8 * s : 8 * s + 8, :], unit))
    strips, pivots = eliminate(strips)
    inverse = jnp.concatenate([a * lax.rsqrt(b) for a, b in zip(strips, pivots)], axis=0)[:, 64:]
    store(jnp.concatenate([inverse[32:], inverse[:32]], axis=1))
    lines = dot32(inverse, g[pl.ds(first, 64), :], ((1,), (0,)))
    rows = lax.broadcasted_iota(jnp.int32, (256, 512), 0)
    g[...] = g[...] - jnp.where(rows >= first + 64, dot32(lines[:, 0:256], lines, ((0,), (0,))), 0.0)
    g[pl.ds(first, 64), :] = lines


def set_identity(g):
    rows = lax.broadcasted_iota(jnp.int32, (256, 256), 0)
    cols = lax.broadcasted_iota(jnp.int32, (256, 256), 1)
    g[:, 256:512] = jnp.where(rows == cols, 1.0, 0.0)


def gather_kernel(
    kern, acol, brow, lead, xa, xs,
    gbuf, g, x_src, xa_src, a00, lead_stage, xa_stage, xs_stage,
    p_send, p_recv, p_sib_send, p_sib_recv, m_send, m_recv, m_sib_send, m_sib_recv,
    lead_send, lead_recv, a_send, a_recv, gs_send, gh_recv, gd_send, gd_recv, ga_send, ga_recv, gx_send, gx_recv,
    xr_send, xh_recv, xd_send, xd_recv, xx_send, xx_recv, loc,
):
    r = lax.axis_index("row")
    c = lax.axis_index("col")
    x, y = lax.div(r, 4), lax.rem(r, 4)
    z, k = lax.div(c, 2), lax.rem(c, 2)
    zero = jnp.int32(0)
    sibling = c + 1 - 2 * k
    both = jnp.logical_and
    core0, core1 = k == 0, k == 1
    top = z == 0
    inner = jnp.logical_not(top)
    root = both(r == 0, c == 0)
    aide = both(r == 0, c == 1)
    helper = both(r == 1, c == 1)
    head = both(z == HEAD, core0)
    runner = both(core0, inner)
    skip_to = lookup(z, SKIP)
    back_to = lookup(z, BACK)
    has_skip = member(z, list(SKIP))
    has_back = member(z, list(BACK))
    parent = lookup(z, {v: q for q, v in list(SKIP.items()) + list(BACK.items())})
    children = has_skip.astype(jnp.int32) + has_back.astype(jnp.int32)
    barrier = pltpu.get_barrier_semaphore()

    def remote(src, dst, send, recv, row, col):
        return pltpu.make_async_remote_copy(
            src_ref=src, dst_ref=dst, send_sem=send, recv_sem=recv, device_id=(row, col), device_id_type=MESH
        )

    def signal(row, col):
        pl.semaphore_signal(barrier, inc=1, device_id=(row, col), device_id_type=MESH)

    def loop(lo, hi, body):
        def step(d, carry):
            body(d)
            return carry

        lax.fori_loop(lo, hi, step, 0)

    def when(cond, body):
        @pl.when(cond)
        def _():
            body()

    def start(copy):
        copy.start()

    def sent(copy):
        copy.wait_send()

    own_panel = pltpu.make_async_copy(kern.at[0, :, 0, 0], acol.at[:, k], loc.at[0])
    own_rows = pltpu.make_async_copy(kern.at[0, 0, 0], brow.at[lax.rem(r, 2), :, k], loc.at[1])
    own_lead = pltpu.make_async_copy(kern.at[0, 0, 0, 0], gbuf.at[0], loc.at[2])
    when(root, lambda: own_lead.start())
    when(top, lambda: own_panel.start())
    when(r < 2, lambda: own_rows.start())

    signal(r, sibling)

    def greet_panel():
        signal(r, 2 * parent)
        when(parent == 0, lambda: signal(r, jnp.int32(1)))

    when(runner, greet_panel)

    def greet_plane():
        loop(1, 16, lambda d: signal(lax.rem(r + d, 16), c))
        when(z != HEAD, lambda: signal(r, jnp.int32(2 * HEAD)))

    when(core1, greet_plane)

    def greet_sources():
        signal(zero, zero)
        signal(zero, jnp.int32(1))
        signal(jnp.int32(1), jnp.int32(1))

    when(head, greet_sources)
    when(root, lambda: signal(jnp.int32(1), jnp.int32(1)))

    def arrive():
        plane = jnp.where(core1, 15, 0)
        line = jnp.where(top, 2, jnp.where(core0, children, 0))
        more = jnp.where(head, 15, 0) + jnp.where(root, 16, 0) + jnp.where(aide, 16, 0) + jnp.where(helper, 17, 0)
        pl.semaphore_wait(barrier, 1 + plane + line + more)
        when(top, lambda: own_panel.wait())
        when(r < 2, lambda: own_rows.wait())

    def panel_chunk(n):
        i, half, col = lax.div(n, 4), lax.rem(lax.div(n, 2), 2), lax.rem(n, 2)
        return acol.at[i, col, pl.ds(pl.multiple_of(128 * half, 128), 128)]

    def panel_skip(n):
        return remote(panel_chunk(n), panel_chunk(n), p_send.at[n, 0], p_recv.at[n], r, 2 * skip_to)

    def panel_back(n):
        return remote(panel_chunk(n), panel_chunk(n), p_send.at[n, 1], p_recv.at[n], r, 2 * back_to)

    def panel_pair(n):
        return remote(panel_chunk(n), panel_chunk(n), p_sib_send.at[n], p_sib_recv.at[n], r, sibling)

    def panel_top(act):
        def step(m):
            n = 2 * m + k
            act(panel_skip(n))
            act(panel_back(n))

        loop(0, 8, step)
        loop(0, 8, lambda m: act(panel_pair(2 * m + k)))

    def panel_line(n):
        panel_skip(n).wait_recv()
        when(has_skip, lambda: panel_skip(n).start())
        when(has_back, lambda: panel_back(n).start())
        panel_pair(n).start()

    def panel_line_sent(n):
        when(has_skip, lambda: panel_skip(n).wait_send())
        when(has_back, lambda: panel_back(n).wait_send())
        panel_pair(n).wait_send()

    def mirror_chunk(s, m):
        j, kc, half = lax.div(m, 4), lax.rem(lax.div(m, 2), 2), lax.rem(m, 2)
        return brow.at[s, j, kc, pl.ds(pl.multiple_of(128 * half, 128), 128)]

    def mirror_copy(s, m, way, row):
        return remote(mirror_chunk(s, m), mirror_chunk(s, m), m_send.at[8 * s + m, way], m_recv.at[8 * s + m], row, c)

    def mirror_pair(s, m):
        n = 8 * s + m
        return remote(mirror_chunk(s, m), mirror_chunk(s, m), m_sib_send.at[n], m_sib_recv.at[n], r, sibling)

    def mirror_feed(j, half):
        m = 4 * j + half
        n = 8 * r + m
        return remote(mirror_chunk(r, m), mirror_chunk(r, m), m_sib_send.at[n], m_recv.at[n], r, sibling)

    def mirror_each(s, m, act):
        j, kc = lax.div(m, 4), lax.rem(lax.div(m, 2), 2)
        rel = lax.rem(y + 4 - s, 4)
        ring = jnp.logical_or(j == 1, x == 0)
        line = jnp.logical_or(j == 0, rel == 0)
        ring_up = both(ring, jnp.logical_or(rel == 0, both(s == 1, rel == 1)))
        ring_down = both(ring, jnp.logical_or(rel == 0, both(s == 0, rel == 3)))
        line_up = both(line, jnp.logical_or(x == 0, both(s == 0, x == 1)))
        line_down = both(line, jnp.logical_or(x == 0, both(s == 1, x == 3)))
        when(ring_up, lambda: act(mirror_copy(s, m, 0, x * 4 + lax.rem(y + 1, 4))))
        when(ring_down, lambda: act(mirror_copy(s, m, 1, x * 4 + lax.rem(y + 3, 4))))
        when(line_up, lambda: act(mirror_copy(s, m, 2, lax.rem(x + 1, 4) * 4 + y)))
        when(line_down, lambda: act(mirror_copy(s, m, 3, lax.rem(x + 3, 4) * 4 + y)))
        when(both(kc == 0, r != s), lambda: act(mirror_pair(s, m)))

    def mirror_step(n):
        nearer = jnp.where(jnp.logical_or(y == 0, y == 3), 0, 1)
        s = lax.rem(lax.div(n, 8) + nearer, 2)
        m = lax.rem(n, 8)
        kc = lax.rem(lax.div(m, 2), 2)
        when(jnp.logical_or(r != s, kc == 0), lambda: mirror_copy(s, m, 0, r).wait_recv())
        mirror_each(s, m, start)

    def mirror_sent(n):
        mirror_each(lax.div(n, 8), lax.rem(n, 8), sent)

    def feeds(act):
        for j in range(2):
            for half in range(2):
                act(mirror_feed(j, half))

    def mirror_take():
        for s in range(2):

            def take(s=s):
                for j in range(2):
                    for half in range(2):
                        mirror_pair(s, 4 * j + half).wait_recv()

            when(r != s, take)

    def lead_from(src, n, p):
        rows = pl.ds(pl.multiple_of(16 * p, 16), 16)
        return remote(src.at[rows], lead_stage.at[n], gs_send.at[n, p], gh_recv.at[n], p, jnp.int32(2 * HEAD))

    own_block = kern.at[0, 0, 0, 0]

    def lead_scatter(src, n, act):
        loop(0, 16, lambda p: act(lead_from(src, n, p)))

    def down(buf, which, d):
        to = lax.rem(HEAD + d, 16)
        stage = lead_stage if which == 0 else xa_stage
        return remote(stage, buf.at[r], gd_send.at[which, d], gd_recv.at[which], r, 2 * to + 1)

    def across(buf, which, d):
        return remote(
            buf.at[r], buf.at[r], ga_send.at[which, d], ga_recv.at[which, r], lax.rem(r + d, 16), c
        )

    def piece_from(buf, which, p):
        return remote(buf.at[p], buf.at[p], ga_send.at[which, 0], ga_recv.at[which, p], r, sibling)

    def pair(buf, which):
        return remote(buf, buf, gx_send.at[which], gx_recv.at[which], r, sibling)

    def head_down(buf, which):
        loop(0, 16, lambda d: down(buf, which, lax.rem(d + 8, 16)).start())

    def spread(buf, which):
        down(buf, which, 0).wait_recv()
        loop(1, 16, lambda d: across(buf, which, lax.rem(d + 9, 15) + 1).start())

    def collect(buf, which):
        loop(1, 16, lambda d: piece_from(buf, which, lax.rem(r + d, 16)).wait_recv())
        pair(buf, which).start()

    def inverse_piece(p):
        return remote(xa_src.at[p], xa_stage, xr_send.at[0, p], xh_recv.at[0], p, jnp.int32(2 * HEAD))

    def inverse_block(n):
        lo, hi = GROUPS[n]
        return pl.ds(lo, hi - lo)

    def inverse_first(n, p):
        rows = inverse_block(n)
        return remote(x_src.at[rows], xs_stage.at[rows], xr_send.at[1 + n, p], xh_recv.at[1 + n], p, jnp.int32(2 * HEAD))

    def inverse_down(n, d):
        rows = inverse_block(n)
        to = lax.rem(HEAD + d, 16)
        return remote(xs_stage.at[rows], xs.at[rows], xd_send.at[n, d], xd_recv.at[n], r, 2 * to + 1)

    def inverse_pair(n):
        block = xs.at[inverse_block(n)]
        return remote(block, block, xx_send.at[n], xx_recv.at[n], r, sibling)

    def first_all(n, act):
        loop(0, 16, lambda p: act(inverse_first(n, lax.rem(p + 10, 16))))

    def down_all(n, act):
        loop(0, 16, lambda d: act(inverse_down(n, lax.rem(d + 8, 16))))

    def send_lead():
        return remote(own_block, a00, a_send, a_recv, r, sibling)

    def lead_copy(n):
        return remote(own_block, gbuf.at[n + 1], lead_send.at[n], lead_recv.at[n], zero, zero)

    def root_main():
        own_lead.wait()
        g[:, 0:256] = gbuf[0].astype(jnp.float32)
        set_identity(g)

        def second_half():
            lead_copy(0).wait_recv()
            lead_copy(1).wait_recv()
            side = dot32(g[:, 256:512], gbuf[1].astype(jnp.float32), ((1,), (0,)))
            g[:, 0:256] = gbuf[2].astype(jnp.float32) - dot32(side, side, ((0,), (0,)))
            set_identity(g)

        def bulk():
            arrive()
            send_lead().start()
            feeds(start)
            panel_top(start)

        def store_at(slot):
            def store(packed):
                x_src[slot] = packed
                for part in range(4):
                    xa_src[4 * slot + part] = packed[8 * part : 8 * part + 8]

            return store

        def step(it):
            when(it == 1, bulk)
            when(it == 2, second_half)
            q = lax.rem(it, 2)
            slot = 2 * q
            factor_block(q, 0, g, store_at(slot))
            when(it == 3, lambda: first_all(1, start))
            factor_block(q, 1, g, store_at(slot + 1))
            def after_first():
                loop(0, 16, lambda p: inverse_piece(p).start())
                loop(0, 16, lambda p: inverse_piece(p).wait_send())

            when(it == 1, after_first)
            when(it == 2, lambda: first_all(0, start))

        loop(0, 4, step)
        first_all(2, start)

    when(root, root_main)
    when(jnp.logical_not(root), arrive)

    def zero_top():
        when(aide, lambda: lead_copy(0).start())
        when(helper, lambda: lead_copy(1).start())
        panel_top(start)
        when(both(core0, r < 2), lambda: feeds(start))

    when(both(top, jnp.logical_not(root)), zero_top)
    when(both(both(core0, r < 2), inner), lambda: feeds(start))

    def aide_main():
        lead_scatter(own_block, 1, start)
        send_lead().wait_recv()
        lead_scatter(a00, 0, start)

    when(aide, aide_main)
    when(helper, lambda: lead_scatter(own_block, 2, start))

    def core1_main():
        loop(0, 16, mirror_step)
        spread(lead, 0)
        collect(lead, 0)
        spread(xa, 1)
        collect(xa, 1)
        for n in range(3):
            inverse_down(n, 0).wait_recv()
            inverse_pair(n).start()

    when(core1, core1_main)

    def head_main():
        for n in range(3):
            lead_from(own_block, n, 0).wait_recv()
        head_down(lead, 0)
        inverse_piece(0).wait_recv()
        head_down(xa, 1)
        for n in range(3):
            inverse_first(n, 0).wait_recv()
            down_all(n, start)

    when(head, head_main)
    when(runner, lambda: loop(0, 16, panel_line))

    def core0_take():
        mirror_take()
        pair(lead, 0).wait_recv()
        pair(xa, 1).wait_recv()
        for n in range(3):
            inverse_pair(n).wait_recv()

    when(core0, core0_take)
    when(both(core1, inner), lambda: loop(0, 16, lambda n: panel_pair(n).wait_recv()))
    when(top, lambda: loop(0, 8, lambda m: panel_pair(2 * m + 1 - k).wait_recv()))

    when(runner, lambda: loop(0, 16, panel_line_sent))
    when(top, lambda: panel_top(sent))
    when(both(core0, r < 2), lambda: feeds(sent))

    def core1_drain():
        loop(0, 16, mirror_sent)
        for which, buf in ((0, lead), (1, xa)):
            loop(1, 16, lambda d, which=which, buf=buf: across(buf, which, d).wait_send())
            pair(buf, which).wait_send()
        for n in range(3):
            inverse_pair(n).wait_send()

    when(core1, core1_drain)

    def head_drain():
        for which, buf in ((0, lead), (1, xa)):
            loop(0, 16, lambda d, which=which, buf=buf: down(buf, which, d).wait_send())
        for n in range(3):
            down_all(n, sent)

    when(head, head_drain)

    def aide_drain():
        lead_copy(0).wait_send()
        lead_scatter(own_block, 1, sent)
        lead_scatter(a00, 0, sent)

    when(aide, aide_drain)

    def helper_drain():
        lead_copy(1).wait_send()
        lead_scatter(own_block, 2, sent)

    when(helper, helper_drain)

    def root_drain():
        send_lead().wait_send()
        for n in range(3):
            first_all(n, sent)

    when(root, root_drain)


def gather(kernel):
    bf16, f32 = jnp.bfloat16, jnp.float32
    dma = pltpu.SemaphoreType.DMA
    return pl.pallas_call(
        gather_kernel,
        out_shape=(
            jax.ShapeDtypeStruct((4, 2, 256, 256), bf16),
            jax.ShapeDtypeStruct((2, 2, 2, 256, 256), bf16),
            jax.ShapeDtypeStruct((16, 3, 16, 256), bf16),
            jax.ShapeDtypeStruct((16, 8, 128), f32),
            jax.ShapeDtypeStruct((4, 32, 128), f32),
        ),
        in_specs=[pl.BlockSpec(memory_space=pltpu.HBM)],
        out_specs=(pl.BlockSpec(memory_space=pl.ANY),) * 5,
        scratch_shapes=[
            pltpu.VMEM((3, 256, 256), bf16),
            pltpu.VMEM((256, 512), f32),
            pltpu.VMEM((4, 32, 128), f32),
            pltpu.VMEM((16, 8, 128), f32),
            pltpu.VMEM((256, 256), bf16),
            pltpu.VMEM((3, 16, 256), bf16),
            pltpu.VMEM((8, 128), f32),
            pltpu.VMEM((4, 32, 128), f32),
            dma((16, 2)), dma((16,)), dma((16,)), dma((16,)),
            dma((16, 4)), dma((16,)), dma((16,)), dma((16,)),
            dma((2,)), dma((2,)), dma, dma,
            dma((3, 16)), dma((3,)), dma((2, 16)), dma((2,)), dma((2, 16)), dma((2, 16)), dma((2,)), dma((2,)),
            dma((4, 16)), dma((4,)), dma((3, 16)), dma((3,)), dma((3,)), dma((3,)), dma((3,)),
        ],
        compiler_params=pltpu.CompilerParams(
            collective_id=0, has_side_effects=True, vmem_limit_bytes=24 * 1024 * 1024
        ),
        name="gather_and_factor",
    )(kernel)


def split(a):
    high = a.astype(jnp.bfloat16)
    rest = a - high.astype(jnp.float32)
    middle = rest.astype(jnp.bfloat16)
    low = (rest - middle.astype(jnp.float32)).astype(jnp.bfloat16)
    return high, middle, low


def assemble(start, packs, g):
    g[:, 0:256] = start
    set_identity(g)
    for n in range(4):
        packed = packs[n]
        inverse = jnp.concatenate([packed[:, 64:128], packed[:, 0:64]], axis=0)
        lo, hi = 64 * n, 64 * n + 64
        lines = dot32(inverse, g[lo:hi, :], ((1,), (0,)))
        g[lo:hi, :] = lines
        if n < 3:
            g[hi:256, :] = g[hi:256, :] - dot32(lines[:, hi:256], lines, ((0,), (0,)))
    return g[:, 256:512]


def update_kernel(kern, acol, brow, lead, xa, xs, panels, schur, g, inv, parts):
    r = lax.axis_index("row")
    c = lax.axis_index("col")
    k = lax.rem(c, 2)

    def block(n):
        return jnp.concatenate([lead[p, n] for p in range(16)], axis=0).astype(jnp.float32)

    first_packs = [jnp.concatenate([xa[4 * n + p] for p in range(4)], axis=0) for n in range(4)]
    inv[...] = jnp.zeros((512, 512), jnp.float32)
    inv[0:256, 0:256] = assemble(block(0), first_packs, g)
    side = dot32(inv[0:256, 0:256], block(1), ((1,), (0,)))
    inv[256:512, 256:512] = assemble(block(2) - dot32(side, side, ((0,), (0,))), [xs[n] for n in range(4)], g)
    low = dot32(side, inv[0:256, 0:256], ((0,), (0,)))
    inv[256:512, 0:256] = -dot32(inv[256:512, 256:512], low, ((1,), (0,)))
    for n, part in enumerate(split(inv[...])):
        parts[n] = part

    mirror = []
    for j in range(2):
        total = jnp.zeros((512, 256), jnp.float32)
        for n in range(3):
            for s in range(2):
                total = total + jnp.dot(
                    parts[n, :, 256 * s : 256 * s + 256], brow[s, j, k], preferred_element_type=jnp.float32
                )
        mirror.append(total.astype(jnp.bfloat16))
    tri = lax.broadcasted_iota(jnp.int32, (256, 256), 0) >= lax.broadcasted_iota(jnp.int32, (256, 256), 1)
    for i in range(4):
        total = jnp.zeros((256, 512), jnp.float32)
        for n in range(3):
            for s in range(2):
                total = total + lax.dot_general(
                    acol[i, s], parts[n, :, 256 * s : 256 * s + 256],
                    (((1,), (1,)), ((), ())), preferred_element_type=jnp.float32,
                )
        first, second = total[:, 0:256], total[:, 256:512]
        if i == 0:
            first = jnp.where(jnp.logical_or(r != 0, tri), first, 0.0)
            second = jnp.where(jnp.logical_or(r > 1, jnp.logical_and(r == 1, tri)), second, 0.0)
        panels[0, i, 0] = first
        panels[0, i, 1] = second
        left = total.astype(jnp.bfloat16)
        for j in range(2):
            change = jnp.dot(left, mirror[j], preferred_element_type=jnp.float32)
            out = (kern[0, i, 0, j].astype(jnp.float32) - change).astype(jnp.bfloat16)
            if i == 0:
                out = jnp.where(r >= 2, out, jnp.zeros_like(out))
            if j == 0:
                out = jnp.where(c >= 2, out, jnp.zeros_like(out))
            schur[0, i, 0, j] = out


def update(kernel, *gathered):
    return pl.pallas_call(
        update_kernel,
        out_shape=(
            jax.ShapeDtypeStruct((1, 4, 2, 256, 256), jnp.float32),
            jax.ShapeDtypeStruct((1, 4, 1, 2, 256, 256), jnp.bfloat16),
        ),
        in_specs=[pl.BlockSpec(memory_space=pltpu.VMEM)] * 6,
        out_specs=(pl.BlockSpec(memory_space=pltpu.VMEM), pl.BlockSpec(memory_space=pltpu.VMEM)),
        scratch_shapes=[
            pltpu.VMEM((256, 512), jnp.float32),
            pltpu.VMEM((512, 512), jnp.float32),
            pltpu.VMEM((3, 512, 512), jnp.bfloat16),
        ],
        compiler_params=pltpu.CompilerParams(vmem_limit_bytes=48 * 1024 * 1024),
        name="solve_and_update",
    )(kernel, *gathered)


def per_device(kernel):
    return update(kernel, *gather(kernel))


def solution(mesh):
    in_specs = (P("row", None, "col", None, None, None),)
    out_specs = (P("row", None, None, None, None), P("row", None, "col", None, None, None))
    return jax.shard_map(per_device, mesh=mesh, in_specs=in_specs, out_specs=out_specs, check_vma=False)
```

time: 1040 us -> 71.7 us (0.07)
  the two profiles are of different devices: /device:TPU:6 before, /device:TPU:13 now
where the time goes in v2:
time: 71.7 us; the launch traced here: 71.5 us
  Pallas kernels  68.4 us (95%)
  local copies, waits for them, and re-layouts  2.44 us (3%)
    pallas_call x1, Pallas kernels, gather(): pl.pallas_call(gather_kernel, out_shape=(jax.ShapeDtypeStruct((4, 2, 256,...  55.5 us
    pallas_call x1, Pallas kernels, update(): pl.pallas_call(update_kernel, out_shape=(jax.ShapeDtypeStruct((1, 4, 2, 2...  12.9 us
    unnamed x4, local copies, waits for them, and re-layouts  2.44 us

profile of v2, /device:TPU:13, one launch (start us, length us, event | category | flops | bytes accessed | tf_op | source)
XLA Modules:
  0.0 71.5 jit_solution(12431299960264014046)
XLA Ops:
  0.6 0.0 copy-start
  0.6 1.2 %copy-done = bf16[1,4,1,2,256,256]{5,4,3,2,1,0:T(8,128)(2,1)S(1)} copy-done((bf16[1,4,1,2,256,256]{5,4,3,2,1,0:T(8,128)(2,1)S(1)}, bf16[1,4,1,2,256,256]{5,4,3,2,1,0:T(8,128)(2,1)}, u32[]{:S(2)}) %copy-start) | copy-done | bytes 1048600
  1.9 55.5 %gather_and_factor.1 = (bf16[4,2,256,256]{3,2,1,0:T(8,128)(2,1)S(1)}, bf16[2,2,2,256,256]{4,3,2,1,0:T(8,128)(2,1)S(1)}, bf16[16,3,16,256]{3,2,1,0:T(8,128)(2,1)S...) custom-call(bf16[1,4,1,2,256,256]{5,4,3,2,1,0:T(8,128)(2,1)S(1)} %copy-done), custom_call_target="tpu_custom_call" | custom-call | tf_op jit(solution)/shard_map/gather_and_factor/pallas_call | solution.py:495
  57.4 0.0 copy-start.1
  57.4 1.2 %copy-done.1 = bf16[1,4,1,2,256,256]{5,4,3,2,1,0:T(8,128)(2,1)S(1)} copy-done((bf16[1,4,1,2,256,256]{5,4,3,2,1,0:T(8,128)(2,1)S(1)}, bf16[1,4,1,2,256,256]{5,4,3,2,1,0:T(8,128)(2,1)}, u32[]{:S(2)}) %copy-start.1) | copy-done | bytes 1048600
  58.6 12.9 %solve_and_update.1 = (f32[1,4,2,256,256]{4,3,2,1,0:T(8,128)}, bf16[1,4,1,2,256,256]{5,4,3,2,1,0:T(8,128)(2,1)}) custom-call(bf16[1,4,1,2,256,256]{5,4,3,2,1,0:T(8,128)(2,1)S(1)} %copy-done.1, bf16[4,2,256,256]{3,2,1,0:T(8,128)(2,1)S(1)} %get-tuple-element.7.acol, bf16[2,2,2,256,256]{4,3,2,1,0:T(8,128)(2,1)S(1)} %get-tuple-element.8.brow, ...), custom_call_target="tpu_custom_call" | custom-call | tf_op jit(solution)/shard_map/solve_and_update/pallas_call | solution.py:604
Async XLA Ops:
  0.6 1.2 %copy-start = (bf16[1,4,1,2,256,256]{5,4,3,2,1,0:T(8,128)(2,1)S(1)}, bf16[1,4,1,2,256,256]{5,4,3,2,1,0:T(8,128)(2,1)}, u32[]{:S(2)}) copy-start(bf16[1,4,1,2,256,256]{5,4,3,2,1,0:T(8,128)(2,1)} %kern.3) | copy-start | bytes 3145732
  57.4 1.2 %copy-start.1 = (bf16[1,4,1,2,256,256]{5,4,3,2,1,0:T(8,128)(2,1)S(1)}, bf16[1,4,1,2,256,256]{5,4,3,2,1,0:T(8,128)(2,1)}, u32[]{:S(2)}) copy-start(bf16[1,4,1,2,256,256]{5,4,3,2,1,0:T(8,128)(2,1)} %kern.3) | copy-start | bytes 3145732

commit v3 on v2

--- a/solution.py
+++ b/solution.py
@@ -29,77 +29,121 @@
     return hit
 
 
-def eliminate(strips):
+def dot32(a, b, dims):
+    return lax.dot_general(a, b, (dims, ((), ())), precision=HI, preferred_element_type=jnp.float32)
+
+
+def row(v, i):
+    return jnp.broadcast_to(v[i : i + 1, :], (8, 128))
+
+def lane(v, i):
+    return jnp.broadcast_to(v[:, i : i + 1], (8, 128))
+
+
+def eliminate(strips, off):
     row_iota = lax.broadcasted_iota(jnp.int32, (8, 128), 0)
-
-    def row(v, i):
-        return jnp.broadcast_to(v[i : i + 1, :], (8, 128))
-
+    strips = list(strips)
+    diag = [lane(strips[0], off + i) for i in range(8)]
     pivots = []
     for s in range(8):
-        cols = []
-        for t in range(s, 8):
-            cols.append([jnp.broadcast_to(strips[t][:, 8 * s + i : 8 * s + i + 1], (8, 128)) for i in range(8)])
+        later = range(s + 1, 8)
+        cols = {t: [lane(strips[t], off + 8 * s + i) for i in range(8)] for t in later}
+        if s < 7:
+            raw = [lane(strips[s + 1], off + 8 * (s + 1) + i) for i in range(8)]
         head = strips[s]
         pivot = jnp.zeros((8, 128), jnp.float32)
         recips = []
         for i in range(8):
-            own = cols[0][i]
+            own = diag[i]
             recip = 1.0 / row(own, i)
+            recips.append(recip)
             pivot = jnp.where(row_iota == i, own, pivot)
             for j in range(i + 1, 8):
-                factor = row(own, j) * recip
-                for t in range(8 - s):
+                line = row(own, j)
+                diag[j] = diag[j] - (own * line) * recip
+                factor = line * recip
+                for t in later:
                     cols[t][j] = cols[t][j] - cols[t][i] * factor
             head = head - jnp.where(row_iota > i, own * recip, 0.0) * row(head, i)
-            recips.append(recip)
         strips[s] = head
         pivots.append(pivot)
+        if s < 7:
+            near = cols[s + 1]
+            scaled = [near[i] * recips[i] for i in range(8)]
+            diag = []
+            for j in range(8):
+                terms = [scaled[i] * row(near[i], j) for i in range(8)]
+                while len(terms) > 1:
+                    terms = [terms[a] + terms[a + 1] for a in range(0, len(terms), 2)]
+                diag.append(raw[j] - terms[0])
         heads = [row(head, i) * recips[i] for i in range(8)]
-        for t in range(s + 1, 8):
-            rest = strips[t]
-            for i in range(8):
-                rest = rest - cols[t - s][i] * heads[i]
-            strips[t] = rest
+        for t in later:
+            terms = [cols[t][i] * heads[i] for i in range(8)]
+            while len(terms) > 1:
+                terms = [terms[a] + terms[a + 1] for a in range(0, len(terms), 2)]
+            strips[t] = strips[t] - terms[0]
     return strips, pivots
 
 
-def dot32(a, b, dims):
-    return lax.dot_general(a, b, (dims, ((), ())), precision=HI, preferred_element_type=jnp.float32)
-
-
-def factor_block(q, h, g, store):
+def factor_phase(g, store):
     col_iota = lax.broadcasted_iota(jnp.int32, (8, 128), 1)
     row_iota = lax.broadcasted_iota(jnp.int32, (8, 128), 0)
-    base = pl.multiple_of(q * 128, 128)
-    first = pl.multiple_of(base + 64 * h, 64)
-    tile = g[pl.ds(first, 64), pl.ds(base, 128)]
-    if h:
-        tile = pltpu.roll(tile, 64, 1)
-    strips = []
-    for s in range(8):
-        unit = jnp.where(col_iota == row_iota + 8 * s + 64, 1.0, 0.0)
-        strips.append(jnp.where(col_iota < 64, tile[8 * s : 8 * s + 8, :], unit))
-    strips, pivots = eliminate(strips)
-    inverse = jnp.concatenate([a * lax.rsqrt(b) for a, b in zip(strips, pivots)], axis=0)[:, 64:]
-    store(jnp.concatenate([inverse[32:], inverse[:32]], axis=1))
-    lines = dot32(inverse, g[pl.ds(first, 64), :], ((1,), (0,)))
-    rows = lax.broadcasted_iota(jnp.int32, (256, 512), 0)
-    g[...] = g[...] - jnp.where(rows >= first + 64, dot32(lines[:, 0:256], lines, ((0,), (0,))), 0.0)
-    g[pl.ds(first, 64), :] = lines
+    for b in range(4):
+        odd = b % 2
+        lo = 64 + 64 * b
+        win = 128 * (b // 2)
+        off = 64 * odd
+        strips = []
+        tile = g[lo:lo+64, win:win+128]
+        for s in range(8):
+            if odd:
+                unit = jnp.where(col_iota == row_iota + 8 * s, 1.0, 0.0)
+                strips.append(jnp.where(col_iota >= 64, tile[8*s:8*s+8], unit))
+            else:
+                unit = jnp.where(col_iota == row_iota + 8 * s + 64, 1.0, 0.0)
+                strips.append(jnp.where(col_iota < 64, tile[8*s:8*s+8], unit))
+        strips, pivots = eliminate(strips, off)
+        keep = (col_iota < 64) if odd else (col_iota >= 64)
+        wide = jnp.concatenate([jnp.where(keep, a * lax.rsqrt(p), 0.0) for a, p in zip(strips, pivots)], axis=0)
+        turned = pltpu.roll(wide, 64, 1)
+        low = wide if odd else turned
+        high = turned if odd else wide
+        store(b, jnp.where(lax.broadcasted_iota(jnp.int32,(32,128),1) < 64, low[32:], high[:32]))
+        base = lo if odd else lo - 64
+        if b < 3:
+            nwin = 128 * ((b + 1) // 2)
+            u = dot32(wide, g[base:base+128, nwin:nwin+128], ((1,), (0,)))
+            nxt = lo + 64
+            noff = 64 * (1 - odd)
+            if odd:
+                g[nxt:nxt+64, nwin:nwin+128] = g[nxt:nxt+64, nwin:nwin+128] - dot32(u[:, 0:64], u, ((0,), (0,)))
+            else:
+                g[nxt:nxt+64, nwin:nwin+128] = g[nxt:nxt+64, nwin:nwin+128] - dot32(u, u, ((0,), (0,)))[64:128]
+        lines = dot32(wide, g[base : base + 128, :], ((1,), (0,)))
+        g[lo:lo+64, :] = lines
+        if b < 3:
+            first = 64 * (b + 1)
+            change = dot32(lines[:, 0:256], lines, ((0,), (0,)))
+            nxt = lo + 64
+            nwin = 128 * ((b + 1) // 2)
+            for lo_c, hi_c in ((0, nwin), (nwin + 128, 512)):
+                if hi_c > lo_c:
+                    g[nxt:nxt+64, lo_c:hi_c] = g[nxt:nxt+64, lo_c:hi_c] - change[first:first+64, lo_c:hi_c]
+            if b < 2:
+                g[nxt+64:320, :] = g[nxt+64:320, :] - change[first+64:256, :]
 
 
 def set_identity(g):
     rows = lax.broadcasted_iota(jnp.int32, (256, 256), 0)
     cols = lax.broadcasted_iota(jnp.int32, (256, 256), 1)
-    g[:, 256:512] = jnp.where(rows == cols, 1.0, 0.0)
+    g[64:320, 256:512] = jnp.where(rows == cols, 1.0, 0.0)
 
 
 def gather_kernel(
-    kern, acol, brow, lead, xa, xs,
-    gbuf, g, x_src, xa_src, a00, lead_stage, xa_stage, xs_stage,
+    kern, acol, brow, parts,
+    lead, inv0, xs, gbuf, g, x_src, inv_src, lead_stage, inv_stage, xs_stage, work,
     p_send, p_recv, p_sib_send, p_sib_recv, m_send, m_recv, m_sib_send, m_sib_recv,
-    lead_send, lead_recv, a_send, a_recv, gs_send, gh_recv, gd_send, gd_recv, ga_send, ga_recv, gx_send, gx_recv,
+    lead_send, lead_recv, gs_send, gh_recv, gd_send, gd_recv, ga_send, ga_recv, gx_send, gx_recv,
     xr_send, xh_recv, xd_send, xd_recv, xx_send, xx_recv, loc,
 ):
     r = lax.axis_index("row")
@@ -289,7 +333,7 @@
 
     def down(buf, which, d):
         to = lax.rem(HEAD + d, 16)
-        stage = lead_stage if which == 0 else xa_stage
+        stage = lead_stage if which == 0 else inv_stage
         return remote(stage, buf.at[r], gd_send.at[which, d], gd_recv.at[which], r, 2 * to + 1)
 
     def across(buf, which, d):
@@ -315,7 +359,7 @@
         pair(buf, which).start()
 
     def inverse_piece(p):
-        return remote(xa_src.at[p], xa_stage, xr_send.at[0, p], xh_recv.at[0], p, jnp.int32(2 * HEAD))
+        return remote(inv_src.at[p], inv_stage, xr_send.at[0, p], xh_recv.at[0], p, jnp.int32(2 * HEAD))
 
     def inverse_block(n):
         lo, hi = GROUPS[n]
@@ -340,55 +384,41 @@
     def down_all(n, act):
         loop(0, 16, lambda d: act(inverse_down(n, lax.rem(d + 8, 16))))
 
-    def send_lead():
-        return remote(own_block, a00, a_send, a_recv, r, sibling)
-
     def lead_copy(n):
         return remote(own_block, gbuf.at[n + 1], lead_send.at[n], lead_recv.at[n], zero, zero)
 
     def root_main():
         own_lead.wait()
-        g[:, 0:256] = gbuf[0].astype(jnp.float32)
+        g[0:64, :] = jnp.zeros((64, 512), jnp.float32)
+        g[320:384, :] = jnp.zeros((64, 512), jnp.float32)
+        g[64:320, 0:256] = gbuf[0].astype(jnp.float32)
         set_identity(g)
 
         def second_half():
+            arrive()
+            feeds(start)
+            panel_top(start)
+            for p in range(16):
+                inv_src[p] = g[64 + 16 * p : 80 + 16 * p, 256:512]
+            loop(0, 16, lambda p: inverse_piece(p).start())
             lead_copy(0).wait_recv()
             lead_copy(1).wait_recv()
-            side = dot32(g[:, 256:512], gbuf[1].astype(jnp.float32), ((1,), (0,)))
-            g[:, 0:256] = gbuf[2].astype(jnp.float32) - dot32(side, side, ((0,), (0,)))
+            side = dot32(g[64:320, 256:512], gbuf[1].astype(jnp.float32), ((1,), (0,)))
+            g[64:320, 0:256] = gbuf[2].astype(jnp.float32) - dot32(side, side, ((0,), (0,)))
             set_identity(g)
 
-        def bulk():
-            arrive()
-            send_lead().start()
-            feeds(start)
-            panel_top(start)
-
-        def store_at(slot):
-            def store(packed):
-                x_src[slot] = packed
-                for part in range(4):
-                    xa_src[4 * slot + part] = packed[8 * part : 8 * part + 8]
-
-            return store
-
-        def step(it):
-            when(it == 1, bulk)
-            when(it == 2, second_half)
-            q = lax.rem(it, 2)
-            slot = 2 * q
-            factor_block(q, 0, g, store_at(slot))
-            when(it == 3, lambda: first_all(1, start))
-            factor_block(q, 1, g, store_at(slot + 1))
-            def after_first():
-                loop(0, 16, lambda p: inverse_piece(p).start())
-                loop(0, 16, lambda p: inverse_piece(p).wait_send())
-
-            when(it == 1, after_first)
-            when(it == 2, lambda: first_all(0, start))
-
-        loop(0, 4, step)
-        first_all(2, start)
+        def phase(it):
+            when(it == 1, second_half)
+
+            def store(n, packed):
+                x_src[n] = packed
+                for which, (lo, hi) in enumerate(GROUPS):
+                    if hi == n + 1:
+                        when(it == 1, lambda which=which: first_all(which, start))
+
+            factor_phase(g, store)
+
+        loop(0, 2, phase)
 
     when(root, root_main)
     when(jnp.logical_not(root), arrive)
@@ -402,32 +432,24 @@
     when(both(top, jnp.logical_not(root)), zero_top)
     when(both(both(core0, r < 2), inner), lambda: feeds(start))
 
-    def aide_main():
-        lead_scatter(own_block, 1, start)
-        send_lead().wait_recv()
-        lead_scatter(a00, 0, start)
-
-    when(aide, aide_main)
-    when(helper, lambda: lead_scatter(own_block, 2, start))
+    when(aide, lambda: lead_scatter(own_block, 0, start))
+    when(helper, lambda: lead_scatter(own_block, 1, start))
 
     def core1_main():
         loop(0, 16, mirror_step)
         spread(lead, 0)
+        spread(inv0, 1)
         collect(lead, 0)
-        spread(xa, 1)
-        collect(xa, 1)
-        for n in range(3):
-            inverse_down(n, 0).wait_recv()
-            inverse_pair(n).start()
+        collect(inv0, 1)
 
     when(core1, core1_main)
 
     def head_main():
-        for n in range(3):
+        for n in range(2):
             lead_from(own_block, n, 0).wait_recv()
         head_down(lead, 0)
         inverse_piece(0).wait_recv()
-        head_down(xa, 1)
+        head_down(inv0, 1)
         for n in range(3):
             inverse_first(n, 0).wait_recv()
             down_all(n, start)
@@ -436,13 +458,50 @@
     when(runner, lambda: loop(0, 16, panel_line))
 
     def core0_take():
-        mirror_take()
         pair(lead, 0).wait_recv()
-        pair(xa, 1).wait_recv()
-        for n in range(3):
-            inverse_pair(n).wait_recv()
+        pair(inv0, 1).wait_recv()
 
     when(core0, core0_take)
+    take = {lo: n for n, (lo, hi) in enumerate(GROUPS)}
+
+    def inverse_take(n):
+        def first():
+            inverse_down(n, 0).wait_recv()
+            inverse_pair(n).start()
+
+        when(core1, first)
+        when(core0, lambda: inverse_pair(n).wait_recv())
+
+    def put(lo, hi, left, values):
+        high = values.astype(jnp.bfloat16)
+        parts[0, lo:hi, left : left + 256] = high
+        parts[1, lo:hi, left : left + 256] = (values - high.astype(jnp.float32)).astype(jnp.bfloat16)
+
+    def block(n):
+        return jnp.concatenate([lead[p, n] for p in range(16)], axis=0).astype(jnp.float32)
+
+    first_inverse = jnp.concatenate([inv0[p] for p in range(16)], axis=0)
+    put(0, 256, 0, first_inverse)
+    put(0, 256, 256, jnp.zeros((256, 256), jnp.float32))
+    side = dot32(first_inverse, block(0), ((1,), (0,)))
+    work[:, 0:256] = block(1) - dot32(side, side, ((0,), (0,)))
+    work[:, 256:512] = -dot32(side, first_inverse, ((0,), (0,)))
+    rows = lax.broadcasted_iota(jnp.int32, (256, 256), 0)
+    cols = lax.broadcasted_iota(jnp.int32, (256, 256), 1)
+    work[:, 512:768] = jnp.where(rows == cols, 1.0, 0.0)
+    for n in range(4):
+        if n in take:
+            inverse_take(take[n])
+        packed = xs[n]
+        inverse = jnp.concatenate([packed[:, 64:128], packed[:, 0:64]], axis=0)
+        lo, hi = 64 * n, 64 * n + 64
+        lines = dot32(inverse, work[lo:hi, :], ((1,), (0,)))
+        put(256 + lo, 256 + hi, 0, lines[:, 256:512])
+        put(256 + lo, 256 + hi, 256, lines[:, 512:768])
+        if n < 3:
+            work[hi:256, :] = work[hi:256, :] - dot32(lines[:, hi:256], lines, ((0,), (0,)))
+
+    when(core0, mirror_take)
     when(both(core1, inner), lambda: loop(0, 16, lambda n: panel_pair(n).wait_recv()))
     when(top, lambda: loop(0, 8, lambda m: panel_pair(2 * m + 1 - k).wait_recv()))
 
@@ -452,7 +511,7 @@
 
     def core1_drain():
         loop(0, 16, mirror_sent)
-        for which, buf in ((0, lead), (1, xa)):
+        for which, buf in ((0, lead), (1, inv0)):
             loop(1, 16, lambda d, which=which, buf=buf: across(buf, which, d).wait_send())
             pair(buf, which).wait_send()
         for n in range(3):
@@ -461,7 +520,7 @@
     when(core1, core1_drain)
 
     def head_drain():
-        for which, buf in ((0, lead), (1, xa)):
+        for which, buf in ((0, lead), (1, inv0)):
             loop(0, 16, lambda d, which=which, buf=buf: down(buf, which, d).wait_send())
         for n in range(3):
             down_all(n, sent)
@@ -470,19 +529,18 @@
 
     def aide_drain():
         lead_copy(0).wait_send()
-        lead_scatter(own_block, 1, sent)
-        lead_scatter(a00, 0, sent)
+        lead_scatter(own_block, 0, sent)
 
     when(aide, aide_drain)
 
     def helper_drain():
         lead_copy(1).wait_send()
-        lead_scatter(own_block, 2, sent)
+        lead_scatter(own_block, 1, sent)
 
     when(helper, helper_drain)
 
     def root_drain():
-        send_lead().wait_send()
+        loop(0, 16, lambda p: inverse_piece(p).wait_send())
         for n in range(3):
             first_all(n, sent)
 
@@ -497,25 +555,30 @@
         out_shape=(
             jax.ShapeDtypeStruct((4, 2, 256, 256), bf16),
             jax.ShapeDtypeStruct((2, 2, 2, 256, 256), bf16),
-            jax.ShapeDtypeStruct((16, 3, 16, 256), bf16),
-            jax.ShapeDtypeStruct((16, 8, 128), f32),
-            jax.ShapeDtypeStruct((4, 32, 128), f32),
+            jax.ShapeDtypeStruct((2, 512, 512), bf16),
         ),
         in_specs=[pl.BlockSpec(memory_space=pltpu.HBM)],
-        out_specs=(pl.BlockSpec(memory_space=pl.ANY),) * 5,
+        out_specs=(
+            pl.BlockSpec(memory_space=pl.ANY),
+            pl.BlockSpec(memory_space=pl.ANY),
+            pl.BlockSpec(memory_space=pltpu.VMEM),
+        ),
         scratch_shapes=[
+            pltpu.VMEM((16, 2, 16, 256), bf16),
+            pltpu.VMEM((16, 16, 256), f32),
+            pltpu.VMEM((4, 32, 128), f32),
             pltpu.VMEM((3, 256, 256), bf16),
-            pltpu.VMEM((256, 512), f32),
+            pltpu.VMEM((384, 512), f32),
             pltpu.VMEM((4, 32, 128), f32),
-            pltpu.VMEM((16, 8, 128), f32),
-            pltpu.VMEM((256, 256), bf16),
-            pltpu.VMEM((3, 16, 256), bf16),
-            pltpu.VMEM((8, 128), f32),
+            pltpu.VMEM((16, 16, 256), f32),
+            pltpu.VMEM((2, 16, 256), bf16),
+            pltpu.VMEM((16, 256), f32),
             pltpu.VMEM((4, 32, 128), f32),
+            pltpu.VMEM((256, 768), f32),
             dma((16, 2)), dma((16,)), dma((16,)), dma((16,)),
             dma((16, 4)), dma((16,)), dma((16,)), dma((16,)),
-            dma((2,)), dma((2,)), dma, dma,
-            dma((3, 16)), dma((3,)), dma((2, 16)), dma((2,)), dma((2, 16)), dma((2, 16)), dma((2,)), dma((2,)),
+            dma((2,)), dma((2,)),
+            dma((2, 16)), dma((2,)), dma((2, 16)), dma((2,)), dma((2, 16)), dma((2, 16)), dma((2,)), dma((2,)),
             dma((4, 16)), dma((4,)), dma((3, 16)), dma((3,)), dma((3,)), dma((3,)), dma((3,)),
         ],
         compiler_params=pltpu.CompilerParams(
@@ -525,96 +588,83 @@
     )(kernel)
 
 
-def split(a):
-    high = a.astype(jnp.bfloat16)
-    rest = a - high.astype(jnp.float32)
-    middle = rest.astype(jnp.bfloat16)
-    low = (rest - middle.astype(jnp.float32)).astype(jnp.bfloat16)
-    return high, middle, low
-
-
-def assemble(start, packs, g):
-    g[:, 0:256] = start
-    set_identity(g)
-    for n in range(4):
-        packed = packs[n]
-        inverse = jnp.concatenate([packed[:, 64:128], packed[:, 0:64]], axis=0)
-        lo, hi = 64 * n, 64 * n + 64
-        lines = dot32(inverse, g[lo:hi, :], ((1,), (0,)))
-        g[lo:hi, :] = lines
-        if n < 3:
-            g[hi:256, :] = g[hi:256, :] - dot32(lines[:, hi:256], lines, ((0,), (0,)))
-    return g[:, 256:512]
-
-
-def update_kernel(kern, acol, brow, lead, xa, xs, panels, schur, g, inv, parts):
+def update_kernel(kern, acol, brow, parts, panels, schur, old, pan, new, sems):
     r = lax.axis_index("row")
     c = lax.axis_index("col")
     k = lax.rem(c, 2)
-
-    def block(n):
-        return jnp.concatenate([lead[p, n] for p in range(16)], axis=0).astype(jnp.float32)
-
-    first_packs = [jnp.concatenate([xa[4 * n + p] for p in range(4)], axis=0) for n in range(4)]
-    inv[...] = jnp.zeros((512, 512), jnp.float32)
-    inv[0:256, 0:256] = assemble(block(0), first_packs, g)
-    side = dot32(inv[0:256, 0:256], block(1), ((1,), (0,)))
-    inv[256:512, 256:512] = assemble(block(2) - dot32(side, side, ((0,), (0,))), [xs[n] for n in range(4)], g)
-    low = dot32(side, inv[0:256, 0:256], ((0,), (0,)))
-    inv[256:512, 0:256] = -dot32(inv[256:512, 256:512], low, ((1,), (0,)))
-    for n, part in enumerate(split(inv[...])):
-        parts[n] = part
-
+    load = pltpu.make_async_copy(kern.at[0, :, 0], old, sems.at[0])
+    load.start()
     mirror = []
     for j in range(2):
-        total = jnp.zeros((512, 256), jnp.float32)
-        for n in range(3):
-            for s in range(2):
-                total = total + jnp.dot(
-                    parts[n, :, 256 * s : 256 * s + 256], brow[s, j, k], preferred_element_type=jnp.float32
-                )
-        mirror.append(total.astype(jnp.bfloat16))
+        halves = []
+        for n in range(2):
+            total = None
+            for s in range(n + 1):
+                for t in range(2):
+                    term = jnp.dot(
+                        parts[t, 256 * n : 256 * n + 256, 256 * s : 256 * s + 256],
+                        brow[s, j, k],
+                        preferred_element_type=jnp.float32,
+                    )
+                    total = term if total is None else total + term
+            halves.append(total.astype(jnp.bfloat16))
+        mirror.append(jnp.concatenate(halves, axis=0))
     tri = lax.broadcasted_iota(jnp.int32, (256, 256), 0) >= lax.broadcasted_iota(jnp.int32, (256, 256), 1)
+    stores = []
+    load.wait()
     for i in range(4):
-        total = jnp.zeros((256, 512), jnp.float32)
-        for n in range(3):
-            for s in range(2):
-                total = total + lax.dot_general(
-                    acol[i, s], parts[n, :, 256 * s : 256 * s + 256],
-                    (((1,), (1,)), ((), ())), preferred_element_type=jnp.float32,
-                )
-        first, second = total[:, 0:256], total[:, 256:512]
+        solved = []
+        for n in range(2):
+            total = None
+            for s in range(n + 1):
+                for t in range(2):
+                    term = lax.dot_general(
+                        acol[i, s],
+                        parts[t, 256 * n : 256 * n + 256, 256 * s : 256 * s + 256],
+                        (((1,), (1,)), ((), ())),
+                        preferred_element_type=jnp.float32,
+                    )
+                    total = term if total is None else total + term
+            solved.append(total)
+        left = jnp.concatenate([a.astype(jnp.bfloat16) for a in solved], axis=1)
         if i == 0:
-            first = jnp.where(jnp.logical_or(r != 0, tri), first, 0.0)
-            second = jnp.where(jnp.logical_or(r > 1, jnp.logical_and(r == 1, tri)), second, 0.0)
-        panels[0, i, 0] = first
-        panels[0, i, 1] = second
-        left = total.astype(jnp.bfloat16)
+            solved[0] = jnp.where(jnp.logical_or(r != 0, tri), solved[0], 0.0)
+            solved[1] = jnp.where(jnp.logical_or(r > 1, jnp.logical_and(r == 1, tri)), solved[1], 0.0)
+        for n in range(2):
+            pan[i, n] = solved[n]
+        stores.append(pltpu.make_async_copy(pan.at[i], panels.at[0, i], sems.at[1 + 2 * i]))
+        stores[-1].start()
         for j in range(2):
             change = jnp.dot(left, mirror[j], preferred_element_type=jnp.float32)
-            out = (kern[0, i, 0, j].astype(jnp.float32) - change).astype(jnp.bfloat16)
+            out = (old[i, j].astype(jnp.float32) - change).astype(jnp.bfloat16)
             if i == 0:
                 out = jnp.where(r >= 2, out, jnp.zeros_like(out))
             if j == 0:
                 out = jnp.where(c >= 2, out, jnp.zeros_like(out))
-            schur[0, i, 0, j] = out
+            new[i, j] = out
+        stores.append(pltpu.make_async_copy(new.at[i], schur.at[0, i, 0], sems.at[2 + 2 * i]))
+        stores[-1].start()
+    for store in stores:
+        store.wait()
 
 
 def update(kernel, *gathered):
+    hbm = pl.BlockSpec(memory_space=pltpu.HBM)
     return pl.pallas_call(
         update_kernel,
         out_shape=(
             jax.ShapeDtypeStruct((1, 4, 2, 256, 256), jnp.float32),
             jax.ShapeDtypeStruct((1, 4, 1, 2, 256, 256), jnp.bfloat16),
         ),
-        in_specs=[pl.BlockSpec(memory_space=pltpu.VMEM)] * 6,
-        out_specs=(pl.BlockSpec(memory_space=pltpu.VMEM), pl.BlockSpec(memory_space=pltpu.VMEM)),
+        in_specs=[hbm] + [pl.BlockSpec(memory_space=pltpu.VMEM)] * 3,
+        out_specs=(hbm, hbm),
         scratch_shapes=[
-            pltpu.VMEM((256, 512), jnp.float32),
-            pltpu.VMEM((512, 512), jnp.float32),
-            pltpu.VMEM((3, 512, 512), jnp.bfloat16),
+            pltpu.VMEM((4, 2, 256, 256), jnp.bfloat16),
+            pltpu.VMEM((4, 2, 256, 256), jnp.float32),
+            pltpu.VMEM((4, 2, 256, 256), jnp.bfloat16),
+            pltpu.SemaphoreType.DMA((9,)),
         ],
-        compiler_params=pltpu.CompilerParams(vmem_limit_bytes=48 * 1024 * 1024),
+        compiler_params=pltpu.CompilerParams(vmem_limit_bytes=32 * 1024 * 1024),
         name="solve_and_update",
     )(kernel, *gathered)
 

time: 71.7 us -> 57 us (0.79)
  Pallas kernels: 68.4 us -> 53.5 us
    pallas_call x1, Pallas kernels: 12.9 us -> 4.02 us  [update(): pl.pallas_call(update_kernel, out_shape=(jax.ShapeDtypeStruct((1, 4, 2, 2...]
    pallas_call x1, Pallas kernels: 55.5 us -> 49.5 us  [gather(): pl.pallas_call(gather_kernel, out_shape=(jax.ShapeDtypeStruct((4, 2, 256,...]
where the time goes in v3:
time: 57 us; the launch traced here: 56.8 us
  Pallas kernels  53.5 us (94%)
  local copies, waits for them, and re-layouts  2.44 us (4%)
  between operations  0.81 us (1%)
    pallas_call x1, Pallas kernels, gather(): pl.pallas_call(gather_kernel, out_shape=(jax.ShapeDtypeStruct((4, 2, 256,...  49.5 us
    pallas_call x1, Pallas kernels, update(): pl.pallas_call(update_kernel, out_shape=(jax.ShapeDtypeStruct((1, 4, 2, 2...  4.02 us
    unnamed x4, local copies, waits for them, and re-layouts  2.44 us

profile of v3, /device:TPU:13, one launch (start us, length us, event | category | flops | bytes accessed | tf_op | source)
XLA Modules:
  0.0 56.8 jit_solution(9419913330096668332)
XLA Ops:
  0.6 0.0 copy-start
  0.6 1.2 %copy-done = bf16[1,4,1,2,256,256]{5,4,3,2,1,0:T(8,128)(2,1)S(1)} copy-done((bf16[1,4,1,2,256,256]{5,4,3,2,1,0:T(8,128)(2,1)S(1)}, bf16[1,4,1,2,256,256]{5,4,3,2,1,0:T(8,128)(2,1)}, u32[]{:S(2)}) %copy-start) | copy-done | bytes 1048600
  1.9 49.5 %gather_and_factor.1 = (bf16[4,2,256,256]{3,2,1,0:T(8,128)(2,1)S(1)}, bf16[2,2,2,256,256]{4,3,2,1,0:T(8,128)(2,1)S(1)}, bf16[2,512,512]{2,1,0:T(8,128)(2,1)S(1)}) custom-call(bf16[1,4,1,2,256,256]{5,4,3,2,1,0:T(8,128)(2,1)S(1)} %copy-done), custom_call_target="tpu_custom_call" | custom-call | tf_op jit(solution)/shard_map/gather_and_factor/pallas_call | solution.py:553
  51.3 0.0 copy-start.1
  51.4 1.2 %copy-done.1 = bf16[1,4,1,2,256,256]{5,4,3,2,1,0:T(8,128)(2,1)S(1)} copy-done((bf16[1,4,1,2,256,256]{5,4,3,2,1,0:T(8,128)(2,1)S(1)}, bf16[1,4,1,2,256,256]{5,4,3,2,1,0:T(8,128)(2,1)}, u32[]{:S(2)}) %copy-start.1) | copy-done | bytes 1048600
  52.6 4.0 %solve_and_update.1 = (f32[1,4,2,256,256]{4,3,2,1,0:T(8,128)}, bf16[1,4,1,2,256,256]{5,4,3,2,1,0:T(8,128)(2,1)}) custom-call(bf16[1,4,1,2,256,256]{5,4,3,2,1,0:T(8,128)(2,1)S(1)} %copy-done.1, bf16[4,2,256,256]{3,2,1,0:T(8,128)(2,1)S(1)} %get-tuple-element.5.acol, bf16[2,2,2,256,256]{4,3,2,1,0:T(8,128)(2,1)S(1)} %get-tuple-element.6.brow, ...), custom_call_target="tpu_custom_call" | custom-call | tf_op jit(solution)/shard_map/solve_and_update/pallas_call | solution.py:653
Async XLA Ops:
  0.6 1.2 %copy-start = (bf16[1,4,1,2,256,256]{5,4,3,2,1,0:T(8,128)(2,1)S(1)}, bf16[1,4,1,2,256,256]{5,4,3,2,1,0:T(8,128)(2,1)}, u32[]{:S(2)}) copy-start(bf16[1,4,1,2,256,256]{5,4,3,2,1,0:T(8,128)(2,1)} %kern.3) | copy-start | bytes 3145732
  51.3 1.2 %copy-start.1 = (bf16[1,4,1,2,256,256]{5,4,3,2,1,0:T(8,128)(2,1)S(1)}, bf16[1,4,1,2,256,256]{5,4,3,2,1,0:T(8,128)(2,1)}, u32[]{:S(2)}) copy-start(bf16[1,4,1,2,256,256]{5,4,3,2,1,0:T(8,128)(2,1)} %kern.3) | copy-start | bytes 3145732

commit v4 on v3

--- a/solution.py
+++ b/solution.py
@@ -10,7 +10,8 @@
 MESH = pl.DeviceIdType.MESH
 HI = lax.Precision.HIGHEST
 GROUPS = ((0, 2), (2, 3), (3, 4))
-HEAD = 1
+PLANE = sorted(((a, b) for a in range(4) for b in range(4) if a or b), key=lambda d: -min(d[0], 4 - d[0]) - min(d[1], 4 - d[1]))
+LINE = sorted(range(1, 16), key=lambda d: -min(d, 16 - d))
 SKIP = {0: 3, 3: 6, 6: 8, 13: 10, 10: 9}
 BACK = {0: 13, 3: 2, 2: 1, 6: 5, 5: 4, 8: 7, 13: 14, 14: 15, 10: 11, 11: 12}
 
@@ -85,7 +86,7 @@
     return strips, pivots
 
 
-def factor_phase(g, store):
+def factor_phase(g, store, middle):
     col_iota = lax.broadcasted_iota(jnp.int32, (8, 128), 1)
     row_iota = lax.broadcasted_iota(jnp.int32, (8, 128), 0)
     for b in range(4):
@@ -108,6 +109,8 @@
         turned = pltpu.roll(wide, 64, 1)
         low = wide if odd else turned
         high = turned if odd else wide
+        if b == 1:
+            middle()
         store(b, jnp.where(lax.broadcasted_iota(jnp.int32,(32,128),1) < 64, low[32:], high[:32]))
         base = lo if odd else lo - 64
         if b < 3:
@@ -150,17 +153,22 @@
     c = lax.axis_index("col")
     x, y = lax.div(r, 4), lax.rem(r, 4)
     z, k = lax.div(c, 2), lax.rem(c, 2)
-    zero = jnp.int32(0)
+    zero, one = jnp.int32(0), jnp.int32(1)
     sibling = c + 1 - 2 * k
-    both = jnp.logical_and
-    core0, core1 = k == 0, k == 1
+    both, neither = jnp.logical_and, jnp.logical_not
     top = z == 0
-    inner = jnp.logical_not(top)
+    inner = neither(top)
+
+    def hub_core(row):
+        return jnp.where(both(top, row != 0), 0, 1)
+
+    hub = k == hub_core(r)
+    mate = neither(hub)
     root = both(r == 0, c == 0)
     aide = both(r == 0, c == 1)
     helper = both(r == 1, c == 1)
-    head = both(z == HEAD, core0)
-    runner = both(core0, inner)
+    head = both(c == 1, r != 0)
+    runner = both(k == 0, inner)
     skip_to = lookup(z, SKIP)
     back_to = lookup(z, BACK)
     has_skip = member(z, list(SKIP))
@@ -195,10 +203,18 @@
     def sent(copy):
         copy.wait_send()
 
+    def peer(d):
+        return lax.rem(x + d[0], 4) * 4 + lax.rem(y + d[1], 4)
+
+    own_block = kern.at[0, 0, 0, 0]
     own_panel = pltpu.make_async_copy(kern.at[0, :, 0, 0], acol.at[:, k], loc.at[0])
     own_rows = pltpu.make_async_copy(kern.at[0, 0, 0], brow.at[lax.rem(r, 2), :, k], loc.at[1])
-    own_lead = pltpu.make_async_copy(kern.at[0, 0, 0, 0], gbuf.at[0], loc.at[2])
+    own_lead = pltpu.make_async_copy(own_block, gbuf.at[0], loc.at[2])
+    aide_piece = pltpu.make_async_copy(own_block.at[pl.ds(0, 16)], lead.at[0, 0], loc.at[2])
+    helper_piece = pltpu.make_async_copy(own_block.at[pl.ds(16, 16)], lead_stage.at[1], loc.at[2])
     when(root, lambda: own_lead.start())
+    when(aide, lambda: aide_piece.start())
+    when(helper, lambda: helper_piece.start())
     when(top, lambda: own_panel.start())
     when(r < 2, lambda: own_rows.start())
 
@@ -206,34 +222,38 @@
 
     def greet_panel():
         signal(r, 2 * parent)
-        when(parent == 0, lambda: signal(r, jnp.int32(1)))
+        when(parent == 0, lambda: signal(r, one))
 
     when(runner, greet_panel)
 
     def greet_plane():
-        loop(1, 16, lambda d: signal(lax.rem(r + d, 16), c))
-        when(z != HEAD, lambda: signal(r, jnp.int32(2 * HEAD)))
-
-    when(core1, greet_plane)
+        for d in PLANE:
+            signal(peer(d), 2 * z + hub_core(peer(d)))
+        when(inner, lambda: signal(r, one))
+
+    when(hub, greet_plane)
 
     def greet_sources():
         signal(zero, zero)
-        signal(zero, jnp.int32(1))
-        signal(jnp.int32(1), jnp.int32(1))
+        signal(zero, one)
+        when(r != 1, lambda: signal(one, one))
 
     when(head, greet_sources)
-    when(root, lambda: signal(jnp.int32(1), jnp.int32(1)))
+    when(jnp.logical_or(root, aide), lambda: signal(one, one))
 
     def arrive():
-        plane = jnp.where(core1, 15, 0)
-        line = jnp.where(top, 2, jnp.where(core0, children, 0))
-        more = jnp.where(head, 15, 0) + jnp.where(root, 16, 0) + jnp.where(aide, 16, 0) + jnp.where(helper, 17, 0)
-        pl.semaphore_wait(barrier, 1 + plane + line + more)
+        plane = jnp.where(hub, 15, 0)
+        line = jnp.where(top, 2, jnp.where(k == 0, children, 0))
+        down = jnp.where(c == 1, 15, 0)
+        more = jnp.where(root, 15, 0) + jnp.where(aide, 15, 0) + jnp.where(helper, 16, 0)
+        pl.semaphore_wait(barrier, 1 + plane + line + down + more)
         when(top, lambda: own_panel.wait())
         when(r < 2, lambda: own_rows.wait())
+        when(aide, lambda: aide_piece.wait())
+        when(helper, lambda: helper_piece.wait())
 
     def panel_chunk(n):
-        i, half, col = lax.div(n, 4), lax.rem(lax.div(n, 2), 2), lax.rem(n, 2)
+        col, i, half = lax.div(n, 8), lax.rem(lax.div(n, 2), 4), lax.rem(n, 2)
         return acol.at[i, col, pl.ds(pl.multiple_of(128 * half, 128), 128)]
 
     def panel_skip(n):
@@ -247,14 +267,14 @@
 
     def panel_top(act):
         def step(m):
-            n = 2 * m + k
-            act(panel_skip(n))
-            act(panel_back(n))
+            act(panel_skip(8 * k + m))
+            act(panel_back(8 * k + m))
 
         loop(0, 8, step)
-        loop(0, 8, lambda m: act(panel_pair(2 * m + k)))
-
-    def panel_line(n):
+        loop(0, 8, lambda m: act(panel_pair(8 * k + m)))
+
+    def panel_line(t):
+        n = lax.rem(t + jnp.where(r == 0, 8, 0), 16)
         panel_skip(n).wait_recv()
         when(has_skip, lambda: panel_skip(n).start())
         when(has_back, lambda: panel_back(n).start())
@@ -270,14 +290,15 @@
         return brow.at[s, j, kc, pl.ds(pl.multiple_of(128 * half, 128), 128)]
 
     def mirror_copy(s, m, way, row):
-        return remote(mirror_chunk(s, m), mirror_chunk(s, m), m_send.at[8 * s + m, way], m_recv.at[8 * s + m], row, c)
+        chunk = mirror_chunk(s, m)
+        return remote(chunk, chunk, m_send.at[8 * s + m, way], m_recv.at[8 * s + m], row, 2 * z + hub_core(row))
 
     def mirror_pair(s, m):
         n = 8 * s + m
         return remote(mirror_chunk(s, m), mirror_chunk(s, m), m_sib_send.at[n], m_sib_recv.at[n], r, sibling)
 
     def mirror_feed(j, half):
-        m = 4 * j + half
+        m = 4 * j + 2 * k + half
         n = 8 * r + m
         return remote(mirror_chunk(r, m), mirror_chunk(r, m), m_sib_send.at[n], m_recv.at[n], r, sibling)
 
@@ -290,18 +311,18 @@
         ring_down = both(ring, jnp.logical_or(rel == 0, both(s == 0, rel == 3)))
         line_up = both(line, jnp.logical_or(x == 0, both(s == 0, x == 1)))
         line_down = both(line, jnp.logical_or(x == 0, both(s == 1, x == 3)))
-        when(ring_up, lambda: act(mirror_copy(s, m, 0, x * 4 + lax.rem(y + 1, 4))))
-        when(ring_down, lambda: act(mirror_copy(s, m, 1, x * 4 + lax.rem(y + 3, 4))))
-        when(line_up, lambda: act(mirror_copy(s, m, 2, lax.rem(x + 1, 4) * 4 + y)))
-        when(line_down, lambda: act(mirror_copy(s, m, 3, lax.rem(x + 3, 4) * 4 + y)))
-        when(both(kc == 0, r != s), lambda: act(mirror_pair(s, m)))
+        when(ring_up, lambda: act(mirror_copy(s, m, 0, peer((0, 1)))))
+        when(ring_down, lambda: act(mirror_copy(s, m, 1, peer((0, 3)))))
+        when(line_up, lambda: act(mirror_copy(s, m, 2, peer((1, 0)))))
+        when(line_down, lambda: act(mirror_copy(s, m, 3, peer((3, 0)))))
+        when(both(kc != k, r != s), lambda: act(mirror_pair(s, m)))
 
     def mirror_step(n):
         nearer = jnp.where(jnp.logical_or(y == 0, y == 3), 0, 1)
         s = lax.rem(lax.div(n, 8) + nearer, 2)
         m = lax.rem(n, 8)
         kc = lax.rem(lax.div(m, 2), 2)
-        when(jnp.logical_or(r != s, kc == 0), lambda: mirror_copy(s, m, 0, r).wait_recv())
+        when(jnp.logical_or(r != s, kc != k), lambda: mirror_copy(s, m, 0, r).wait_recv())
         mirror_each(s, m, start)
 
     def mirror_sent(n):
@@ -318,71 +339,102 @@
             def take(s=s):
                 for j in range(2):
                     for half in range(2):
-                        mirror_pair(s, 4 * j + half).wait_recv()
+                        mirror_pair(s, 4 * j + 2 * k + half).wait_recv()
 
             when(r != s, take)
 
-    def lead_from(src, n, p):
-        rows = pl.ds(pl.multiple_of(16 * p, 16), 16)
-        return remote(src.at[rows], lead_stage.at[n], gs_send.at[n, p], gh_recv.at[n], p, jnp.int32(2 * HEAD))
-
-    own_block = kern.at[0, 0, 0, 0]
-
-    def lead_scatter(src, n, act):
-        loop(0, 16, lambda p: act(lead_from(src, n, p)))
-
-    def down(buf, which, d):
-        to = lax.rem(HEAD + d, 16)
-        stage = lead_stage if which == 0 else inv_stage
-        return remote(stage, buf.at[r], gd_send.at[which, d], gd_recv.at[which], r, 2 * to + 1)
-
-    def across(buf, which, d):
-        return remote(
-            buf.at[r], buf.at[r], ga_send.at[which, d], ga_recv.at[which, r], lax.rem(r + d, 16), c
-        )
-
-    def piece_from(buf, which, p):
-        return remote(buf.at[p], buf.at[p], ga_send.at[which, 0], ga_recv.at[which, p], r, sibling)
-
-    def pair(buf, which):
+    def lead_from(n, p):
+        rows = own_block.at[pl.ds(16 * p, 16)]
+        to = lead.at[0, n] if p == 0 else lead_stage.at[n]
+        return remote(rows, to, gs_send.at[p], gh_recv.at[n], jnp.int32(p), one)
+
+    def lead_scatter(n, act):
+        for p in range(16):
+            if p != n:
+                act(lead_from(n, p))
+
+    def head_copies(buf, stage, send, recv):
+        out = []
+        for d in LINE:
+            out.append((None, remote(stage, buf, send.at[d], recv, r, jnp.int32(2 * d + 1))))
+        out.append((r != 0, remote(stage, buf, send.at[0], recv, r, zero)))
+        return out
+
+    def each(copies, act):
+        for cond, copy in copies:
+            if cond is None:
+                act(copy)
+            else:
+                when(cond, lambda copy=copy: act(copy))
+
+    def down(which, act):
+        buf, stage = ((lead, lead_stage), (inv0, inv_stage))[which]
+        send, recv = gd_send.at[which], gd_recv.at[which]
+        when(r != 0, lambda: each(head_copies(buf.at[r], stage, send, recv), act))
+        when(r == 0, lambda: each(head_copies(buf.at[0], buf.at[0], send, recv), act))
+
+    def down_taken(which):
+        buf = (lead, inv0)[which]
+        remote(buf.at[r], buf.at[r], gd_send.at[which, 0], gd_recv.at[which], r, sibling).wait_recv()
+
+    def across(which, act):
+        buf = (lead, inv0)[which]
+        for n, d in enumerate(PLANE):
+            row = peer(d)
+            act(remote(buf.at[r], buf.at[r], ga_send.at[which, n], ga_recv.at[which, r], row, 2 * z + hub_core(row)))
+
+    def pair(which):
+        buf = (lead, inv0)[which]
         return remote(buf, buf, gx_send.at[which], gx_recv.at[which], r, sibling)
 
-    def head_down(buf, which):
-        loop(0, 16, lambda d: down(buf, which, lax.rem(d + 8, 16)).start())
-
-    def spread(buf, which):
-        down(buf, which, 0).wait_recv()
-        loop(1, 16, lambda d: across(buf, which, lax.rem(d + 9, 15) + 1).start())
-
-    def collect(buf, which):
-        loop(1, 16, lambda d: piece_from(buf, which, lax.rem(r + d, 16)).wait_recv())
-        pair(buf, which).start()
+    def spread(which):
+        when(neither(aide), lambda: down_taken(which))
+        across(which, start)
+
+    def collect(which):
+        buf = (lead, inv0)[which]
+
+        def take(d):
+            p = lax.rem(r + d, 16)
+            remote(buf.at[p], buf.at[p], ga_send.at[which, 0], ga_recv.at[which, p], r, sibling).wait_recv()
+
+        loop(1, 16, take)
+        pair(which).start()
 
     def inverse_piece(p):
-        return remote(inv_src.at[p], inv_stage, xr_send.at[0, p], xh_recv.at[0], p, jnp.int32(2 * HEAD))
-
-    def inverse_block(n):
+        to = inv0.at[0] if p == 0 else inv_stage
+        return remote(inv_src.at[p], to, xr_send.at[0, p], xh_recv.at[0], jnp.int32(p), one)
+
+    def inverse_first(n, p):
         lo, hi = GROUPS[n]
-        return pl.ds(lo, hi - lo)
-
-    def inverse_first(n, p):
-        rows = inverse_block(n)
-        return remote(x_src.at[rows], xs_stage.at[rows], xr_send.at[1 + n, p], xh_recv.at[1 + n], p, jnp.int32(2 * HEAD))
-
-    def inverse_down(n, d):
-        rows = inverse_block(n)
-        to = lax.rem(HEAD + d, 16)
-        return remote(xs_stage.at[rows], xs.at[rows], xd_send.at[n, d], xd_recv.at[n], r, 2 * to + 1)
+        rows = pl.ds(lo, hi - lo)
+        to = xs if p == 0 else xs_stage
+        return remote(x_src.at[rows], to.at[rows], xr_send.at[1 + n, p], xh_recv.at[1 + n], jnp.int32(p), one)
+
+    def from_root(act, copy):
+        for d in PLANE:
+            act(copy(4 * d[0] + d[1]))
+        act(copy(0))
+
+    def first_all(n, act):
+        from_root(act, lambda p: inverse_first(n, p))
+
+    def inverse_down(n, act):
+        lo, hi = GROUPS[n]
+        rows = pl.ds(lo, hi - lo)
+        send, recv = xd_send.at[n], xd_recv.at[n]
+        when(r != 0, lambda: each(head_copies(xs.at[rows], xs_stage.at[rows], send, recv), act))
+        when(r == 0, lambda: each(head_copies(xs.at[rows], xs.at[rows], send, recv), act))
+
+    def inverse_taken(n):
+        lo, hi = GROUPS[n]
+        rows = xs.at[pl.ds(lo, hi - lo)]
+        remote(rows, rows, xd_send.at[n, 0], xd_recv.at[n], r, sibling).wait_recv()
 
     def inverse_pair(n):
-        block = xs.at[inverse_block(n)]
-        return remote(block, block, xx_send.at[n], xx_recv.at[n], r, sibling)
-
-    def first_all(n, act):
-        loop(0, 16, lambda p: act(inverse_first(n, lax.rem(p + 10, 16))))
-
-    def down_all(n, act):
-        loop(0, 16, lambda d: act(inverse_down(n, lax.rem(d + 8, 16))))
+        lo, hi = GROUPS[n]
+        rows = xs.at[pl.ds(lo, hi - lo)]
+        return remote(rows, rows, xx_send.at[n], xx_recv.at[n], r, sibling)
 
     def lead_copy(n):
         return remote(own_block, gbuf.at[n + 1], lead_send.at[n], lead_recv.at[n], zero, zero)
@@ -394,13 +446,15 @@
         g[64:320, 0:256] = gbuf[0].astype(jnp.float32)
         set_identity(g)
 
-        def second_half():
+        def bulk():
             arrive()
             feeds(start)
             panel_top(start)
+
+        def second_half():
             for p in range(16):
                 inv_src[p] = g[64 + 16 * p : 80 + 16 * p, 256:512]
-            loop(0, 16, lambda p: inverse_piece(p).start())
+            from_root(start, inverse_piece)
             lead_copy(0).wait_recv()
             lead_copy(1).wait_recv()
             side = dot32(g[64:320, 256:512], gbuf[1].astype(jnp.float32), ((1,), (0,)))
@@ -408,69 +462,79 @@
             set_identity(g)
 
         def phase(it):
-            when(it == 1, second_half)
-
             def store(n, packed):
                 x_src[n] = packed
                 for which, (lo, hi) in enumerate(GROUPS):
                     if hi == n + 1:
                         when(it == 1, lambda which=which: first_all(which, start))
 
-            factor_phase(g, store)
+            factor_phase(g, store, lambda: when(it == 0, bulk))
+            when(it == 0, second_half)
 
         loop(0, 2, phase)
 
     when(root, root_main)
-    when(jnp.logical_not(root), arrive)
-
-    def zero_top():
+    when(neither(root), arrive)
+
+    def top_sends():
         when(aide, lambda: lead_copy(0).start())
         when(helper, lambda: lead_copy(1).start())
         panel_top(start)
-        when(both(core0, r < 2), lambda: feeds(start))
-
-    when(both(top, jnp.logical_not(root)), zero_top)
-    when(both(both(core0, r < 2), inner), lambda: feeds(start))
-
-    when(aide, lambda: lead_scatter(own_block, 0, start))
-    when(helper, lambda: lead_scatter(own_block, 1, start))
-
-    def core1_main():
+        when(aide, lambda: lead_scatter(0, start))
+        when(helper, lambda: lead_scatter(1, start))
+
+    when(both(top, neither(root)), top_sends)
+    when(both(both(mate, r < 2), neither(root)), lambda: feeds(start))
+
+    def hub_main():
         loop(0, 16, mirror_step)
-        spread(lead, 0)
-        spread(inv0, 1)
-        collect(lead, 0)
-        collect(inv0, 1)
-
-    when(core1, core1_main)
+
+        def aide_down():
+            lead_from(1, 0).wait_recv()
+            down(0, start)
+            inverse_piece(0).wait_recv()
+            down(1, start)
+
+        when(aide, aide_down)
+        spread(0)
+        spread(1)
+        collect(0)
+        collect(1)
+
+    when(hub, hub_main)
 
     def head_main():
-        for n in range(2):
-            lead_from(own_block, n, 0).wait_recv()
-        head_down(lead, 0)
-        inverse_piece(0).wait_recv()
-        head_down(inv0, 1)
+        lead_from(0, 1).wait_recv()
+        when(neither(helper), lambda: lead_from(1, 2).wait_recv())
+        down(0, start)
+        inverse_piece(1).wait_recv()
+        down(1, start)
         for n in range(3):
-            inverse_first(n, 0).wait_recv()
-            down_all(n, start)
+            inverse_first(n, 1).wait_recv()
+            inverse_down(n, start)
 
     when(head, head_main)
     when(runner, lambda: loop(0, 16, panel_line))
 
-    def core0_take():
-        pair(lead, 0).wait_recv()
-        pair(inv0, 1).wait_recv()
-
-    when(core0, core0_take)
+    def mate_take():
+        pair(0).wait_recv()
+        pair(1).wait_recv()
+
+    when(mate, mate_take)
     take = {lo: n for n, (lo, hi) in enumerate(GROUPS)}
 
     def inverse_take(n):
-        def first():
-            inverse_down(n, 0).wait_recv()
+        def as_hub():
+            def as_aide():
+                inverse_first(n, 0).wait_recv()
+                inverse_down(n, start)
+
+            when(aide, as_aide)
+            when(neither(aide), lambda: inverse_taken(n))
             inverse_pair(n).start()
 
-        when(core1, first)
-        when(core0, lambda: inverse_pair(n).wait_recv())
+        when(hub, as_hub)
+        when(mate, lambda: inverse_pair(n).wait_recv())
 
     def put(lo, hi, left, values):
         high = values.astype(jnp.bfloat16)
@@ -501,46 +565,46 @@
         if n < 3:
             work[hi:256, :] = work[hi:256, :] - dot32(lines[:, hi:256], lines, ((0,), (0,)))
 
-    when(core0, mirror_take)
-    when(both(core1, inner), lambda: loop(0, 16, lambda n: panel_pair(n).wait_recv()))
-    when(top, lambda: loop(0, 8, lambda m: panel_pair(2 * m + 1 - k).wait_recv()))
+    when(mate, mirror_take)
+    when(both(hub, inner), lambda: loop(0, 16, lambda n: panel_pair(n).wait_recv()))
+    when(top, lambda: loop(0, 8, lambda m: panel_pair(8 * (1 - k) + m).wait_recv()))
 
     when(runner, lambda: loop(0, 16, panel_line_sent))
     when(top, lambda: panel_top(sent))
-    when(both(core0, r < 2), lambda: feeds(sent))
-
-    def core1_drain():
+    when(both(mate, r < 2), lambda: feeds(sent))
+
+    def hub_drain():
         loop(0, 16, mirror_sent)
-        for which, buf in ((0, lead), (1, inv0)):
-            loop(1, 16, lambda d, which=which, buf=buf: across(buf, which, d).wait_send())
-            pair(buf, which).wait_send()
+        for which in range(2):
+            across(which, sent)
+            pair(which).wait_send()
         for n in range(3):
             inverse_pair(n).wait_send()
 
-    when(core1, core1_drain)
-
-    def head_drain():
-        for which, buf in ((0, lead), (1, inv0)):
-            loop(0, 16, lambda d, which=which, buf=buf: down(buf, which, d).wait_send())
+    when(hub, hub_drain)
+
+    def line_drain():
+        for which in range(2):
+            down(which, sent)
         for n in range(3):
-            down_all(n, sent)
-
-    when(head, head_drain)
+            inverse_down(n, sent)
+
+    when(c == 1, line_drain)
 
     def aide_drain():
         lead_copy(0).wait_send()
-        lead_scatter(own_block, 0, sent)
+        lead_scatter(0, sent)
 
     when(aide, aide_drain)
 
     def helper_drain():
         lead_copy(1).wait_send()
-        lead_scatter(own_block, 1, sent)
+        lead_scatter(1, sent)
 
     when(helper, helper_drain)
 
     def root_drain():
-        loop(0, 16, lambda p: inverse_piece(p).wait_send())
+        from_root(sent, inverse_piece)
         for n in range(3):
             first_all(n, sent)
 
@@ -578,7 +642,7 @@
             dma((16, 2)), dma((16,)), dma((16,)), dma((16,)),
             dma((16, 4)), dma((16,)), dma((16,)), dma((16,)),
             dma((2,)), dma((2,)),
-            dma((2, 16)), dma((2,)), dma((2, 16)), dma((2,)), dma((2, 16)), dma((2, 16)), dma((2,)), dma((2,)),
+            dma((16,)), dma((2,)), dma((2, 16)), dma((2,)), dma((2, 16)), dma((2, 16)), dma((2,)), dma((2,)),
             dma((4, 16)), dma((4,)), dma((3, 16)), dma((3,)), dma((3,)), dma((3,)), dma((3,)),
         ],
         compiler_params=pltpu.CompilerParams(
@@ -670,6 +734,7 @@
 
 
 def per_device(kernel):
+    kernel = pltpu.with_memory_space_constraint(kernel, pltpu.HBM)
     return update(kernel, *gather(kernel))
 
 

time: 57 us -> 62.3 us (1.093)
  the two profiles are of different devices: /device:TPU:13 before, /device:TPU:32 now
where the time goes in v4:
time: 62.3 us; the launch traced here: 62.1 us
  Pallas kernels  61.3 us (98%)
  between operations  0.8 us (1%)
    pallas_call x1, Pallas kernels, gather(): pl.pallas_call(gather_kernel, out_shape=(jax.ShapeDtypeStruct((4, 2, 256,...  56.9 us
    pallas_call x1, Pallas kernels, update(): pl.pallas_call(update_kernel, out_shape=(jax.ShapeDtypeStruct((1, 4, 2, 2...  4.48 us

profile of v4, /device:TPU:32, one launch (start us, length us, event | category | flops | bytes accessed | tf_op | source)
XLA Modules:
  0.0 62.1 jit_solution(14230026198959423411)
XLA Ops:
  0.6 56.9 %gather_and_factor.1 = (bf16[4,2,256,256]{3,2,1,0:T(8,128)(2,1)S(1)}, bf16[2,2,2,256,256]{4,3,2,1,0:T(8,128)(2,1)S(1)}, bf16[2,512,512]{2,1,0:T(8,128)(2,1)S(1)}) custom-call(bf16[1,4,1,2,256,256]{5,4,3,2,1,0:T(8,128)(2,1)} %kern.3), custom_call_target="tpu_custom_call" | custom-call | tf_op jit(solution)/shard_map/gather_and_factor/pallas_call | solution.py:617
  57.5 4.5 %solve_and_update.1 = (f32[1,4,2,256,256]{4,3,2,1,0:T(8,128)}, bf16[1,4,1,2,256,256]{5,4,3,2,1,0:T(8,128)(2,1)}) custom-call(bf16[1,4,1,2,256,256]{5,4,3,2,1,0:T(8,128)(2,1)} %kern.3, bf16[4,2,256,256]{3,2,1,0:T(8,128)(2,1)S(1)} %get-tuple-element.5.acol, bf16[2,2,2,256,256]{4,3,2,1,0:T(8,128)(2,1)S(1)} %get-tuple-element.6.brow, ...), custom_call_target="tpu_custom_call" | custom-call | tf_op jit(solution)/shard_map/solve_and_update/pallas_call | solution.py:717

commit v5 on v4

--- a/solution.py
+++ b/solution.py
@@ -9,8 +9,9 @@
 
 MESH = pl.DeviceIdType.MESH
 HI = lax.Precision.HIGHEST
-GROUPS = ((0, 2), (2, 3), (3, 4))
+GROUPS = ((0, 3), (3, 4))
 PLANE = sorted(((a, b) for a in range(4) for b in range(4) if a or b), key=lambda d: -min(d[0], 4 - d[0]) - min(d[1], 4 - d[1]))
+NEAR = ((0, 1), (0, 3), (1, 0), (3, 0))
 LINE = sorted(range(1, 16), key=lambda d: -min(d, 16 - d))
 SKIP = {0: 3, 3: 6, 6: 8, 13: 10, 10: 9}
 BACK = {0: 13, 3: 2, 2: 1, 6: 5, 5: 4, 8: 7, 13: 14, 14: 15, 10: 11, 11: 12}
@@ -109,7 +110,7 @@
         turned = pltpu.roll(wide, 64, 1)
         low = wide if odd else turned
         high = turned if odd else wide
-        if b == 1:
+        if b == 2:
             middle()
         store(b, jnp.where(lax.broadcasted_iota(jnp.int32,(32,128),1) < 64, low[32:], high[:32]))
         base = lo if odd else lo - 64
@@ -144,7 +145,7 @@
 
 def gather_kernel(
     kern, acol, brow, parts,
-    lead, inv0, xs, gbuf, g, x_src, inv_src, lead_stage, inv_stage, xs_stage, work,
+    lead, inv0, xs, gbuf, g, x_src, inv_src, work,
     p_send, p_recv, p_sib_send, p_sib_recv, m_send, m_recv, m_sib_send, m_sib_recv,
     lead_send, lead_recv, gs_send, gh_recv, gd_send, gd_recv, ga_send, ga_recv, gx_send, gx_recv,
     xr_send, xh_recv, xd_send, xd_recv, xx_send, xx_recv, loc,
@@ -211,7 +212,7 @@
     own_rows = pltpu.make_async_copy(kern.at[0, 0, 0], brow.at[lax.rem(r, 2), :, k], loc.at[1])
     own_lead = pltpu.make_async_copy(own_block, gbuf.at[0], loc.at[2])
     aide_piece = pltpu.make_async_copy(own_block.at[pl.ds(0, 16)], lead.at[0, 0], loc.at[2])
-    helper_piece = pltpu.make_async_copy(own_block.at[pl.ds(16, 16)], lead_stage.at[1], loc.at[2])
+    helper_piece = pltpu.make_async_copy(own_block.at[pl.ds(16, 16)], lead.at[1, 1], loc.at[2])
     when(root, lambda: own_lead.start())
     when(aide, lambda: aide_piece.start())
     when(helper, lambda: helper_piece.start())
@@ -228,10 +229,17 @@
 
     def greet_plane():
         for d in PLANE:
-            signal(peer(d), 2 * z + hub_core(peer(d)))
+            signal(peer(d), c)
         when(inner, lambda: signal(r, one))
-
-    when(hub, greet_plane)
+        when(both(inner, r == 0), lambda: signal(r, zero))
+
+    when(k == 1, greet_plane)
+
+    def greet_mirror():
+        for d in NEAR:
+            signal(peer(d), hub_core(peer(d)))
+
+    when(both(hub, top), greet_mirror)
 
     def greet_sources():
         signal(zero, zero)
@@ -242,10 +250,10 @@
     when(jnp.logical_or(root, aide), lambda: signal(one, one))
 
     def arrive():
-        plane = jnp.where(hub, 15, 0)
+        plane = jnp.where(k == 1, 15, 0) + jnp.where(both(hub, top), 4, 0)
         line = jnp.where(top, 2, jnp.where(k == 0, children, 0))
         down = jnp.where(c == 1, 15, 0)
-        more = jnp.where(root, 15, 0) + jnp.where(aide, 15, 0) + jnp.where(helper, 16, 0)
+        more = jnp.where(root, 30, 0) + jnp.where(aide, 15, 0) + jnp.where(helper, 16, 0)
         pl.semaphore_wait(barrier, 1 + plane + line + down + more)
         when(top, lambda: own_panel.wait())
         when(r < 2, lambda: own_rows.wait())
@@ -345,51 +353,30 @@
 
     def lead_from(n, p):
         rows = own_block.at[pl.ds(16 * p, 16)]
-        to = lead.at[0, n] if p == 0 else lead_stage.at[n]
-        return remote(rows, to, gs_send.at[p], gh_recv.at[n], jnp.int32(p), one)
+        return remote(rows, lead.at[p, n], gs_send.at[p], gh_recv.at[n], jnp.int32(p), one)
 
     def lead_scatter(n, act):
         for p in range(16):
             if p != n:
                 act(lead_from(n, p))
 
-    def head_copies(buf, stage, send, recv):
-        out = []
+    def down(which, act):
+        piece = (lead, inv0)[which].at[r]
         for d in LINE:
-            out.append((None, remote(stage, buf, send.at[d], recv, r, jnp.int32(2 * d + 1))))
-        out.append((r != 0, remote(stage, buf, send.at[0], recv, r, zero)))
-        return out
-
-    def each(copies, act):
-        for cond, copy in copies:
-            if cond is None:
-                act(copy)
-            else:
-                when(cond, lambda copy=copy: act(copy))
-
-    def down(which, act):
-        buf, stage = ((lead, lead_stage), (inv0, inv_stage))[which]
-        send, recv = gd_send.at[which], gd_recv.at[which]
-        when(r != 0, lambda: each(head_copies(buf.at[r], stage, send, recv), act))
-        when(r == 0, lambda: each(head_copies(buf.at[0], buf.at[0], send, recv), act))
-
-    def down_taken(which):
-        buf = (lead, inv0)[which]
-        remote(buf.at[r], buf.at[r], gd_send.at[which, 0], gd_recv.at[which], r, sibling).wait_recv()
+            act(remote(piece, piece, gd_send.at[which, d], gd_recv.at[which], r, jnp.int32(2 * d + 1)))
 
     def across(which, act):
-        buf = (lead, inv0)[which]
+        piece = (lead, inv0)[which].at[r]
         for n, d in enumerate(PLANE):
-            row = peer(d)
-            act(remote(buf.at[r], buf.at[r], ga_send.at[which, n], ga_recv.at[which, r], row, 2 * z + hub_core(row)))
+            act(remote(piece, piece, ga_send.at[which, n], ga_recv.at[which, r], peer(d), c))
 
     def pair(which):
         buf = (lead, inv0)[which]
         return remote(buf, buf, gx_send.at[which], gx_recv.at[which], r, sibling)
 
-    def spread(which):
-        when(neither(aide), lambda: down_taken(which))
-        across(which, start)
+    def piece_taken(which):
+        piece = (lead, inv0)[which].at[r]
+        remote(piece, piece, gd_send.at[which, 0], gd_recv.at[which], r, sibling).wait_recv()
 
     def collect(which):
         buf = (lead, inv0)[which]
@@ -402,38 +389,38 @@
         pair(which).start()
 
     def inverse_piece(p):
-        to = inv0.at[0] if p == 0 else inv_stage
-        return remote(inv_src.at[p], to, xr_send.at[0, p], xh_recv.at[0], jnp.int32(p), one)
+        return remote(inv_src.at[p], inv0.at[p], xr_send.at[0, p], xh_recv.at[0], jnp.int32(p), one)
+
+    def inverse_rows(buf, n):
+        lo, hi = GROUPS[n]
+        return buf.at[pl.ds(lo, hi - lo)]
 
     def inverse_first(n, p):
-        lo, hi = GROUPS[n]
-        rows = pl.ds(lo, hi - lo)
-        to = xs if p == 0 else xs_stage
-        return remote(x_src.at[rows], to.at[rows], xr_send.at[1 + n, p], xh_recv.at[1 + n], jnp.int32(p), one)
+        return remote(
+            inverse_rows(x_src, n), inverse_rows(xs, n), xr_send.at[1 + n, p], xh_recv.at[1 + n], jnp.int32(p), one
+        )
 
     def from_root(act, copy):
         for d in PLANE:
             act(copy(4 * d[0] + d[1]))
         act(copy(0))
 
+    def inverse_down(n, act, src):
+        for d in LINE:
+            act(remote(
+                inverse_rows(src, n), inverse_rows(xs, n), xd_send.at[n, d], xd_recv.at[n], r, jnp.int32(2 * d + 1)
+            ))
+
     def first_all(n, act):
+        inverse_down(n, act, x_src)
         from_root(act, lambda p: inverse_first(n, p))
 
-    def inverse_down(n, act):
-        lo, hi = GROUPS[n]
-        rows = pl.ds(lo, hi - lo)
-        send, recv = xd_send.at[n], xd_recv.at[n]
-        when(r != 0, lambda: each(head_copies(xs.at[rows], xs_stage.at[rows], send, recv), act))
-        when(r == 0, lambda: each(head_copies(xs.at[rows], xs.at[rows], send, recv), act))
-
     def inverse_taken(n):
-        lo, hi = GROUPS[n]
-        rows = xs.at[pl.ds(lo, hi - lo)]
+        rows = inverse_rows(xs, n)
         remote(rows, rows, xd_send.at[n, 0], xd_recv.at[n], r, sibling).wait_recv()
 
     def inverse_pair(n):
-        lo, hi = GROUPS[n]
-        rows = xs.at[pl.ds(lo, hi - lo)]
+        rows = inverse_rows(xs, n)
         return remote(rows, rows, xx_send.at[n], xx_recv.at[n], r, sibling)
 
     def lead_copy(n):
@@ -486,55 +473,62 @@
     when(both(top, neither(root)), top_sends)
     when(both(both(mate, r < 2), neither(root)), lambda: feeds(start))
 
-    def hub_main():
-        loop(0, 16, mirror_step)
-
-        def aide_down():
-            lead_from(1, 0).wait_recv()
-            down(0, start)
-            inverse_piece(0).wait_recv()
-            down(1, start)
-
-        when(aide, aide_down)
-        spread(0)
-        spread(1)
-        collect(0)
-        collect(1)
-
-    when(hub, hub_main)
+    def top_spread(which):
+        down(which, start)
+        across(which, start)
+
+    def aide_main():
+        loop(0, 8, mirror_step)
+        lead_from(1, 0).wait_recv()
+        top_spread(0)
+        inverse_piece(0).wait_recv()
+        top_spread(1)
+        loop(8, 16, mirror_step)
+
+    when(aide, aide_main)
+    when(both(hub, neither(aide)), lambda: loop(0, 16, mirror_step))
 
     def head_main():
         lead_from(0, 1).wait_recv()
         when(neither(helper), lambda: lead_from(1, 2).wait_recv())
-        down(0, start)
+        top_spread(0)
         inverse_piece(1).wait_recv()
-        down(1, start)
-        for n in range(3):
+        top_spread(1)
+        for n in range(2):
             inverse_first(n, 1).wait_recv()
-            inverse_down(n, start)
+            inverse_down(n, start, xs)
 
     when(head, head_main)
+
+    def line_spread():
+        for which in range(2):
+            piece_taken(which)
+            across(which, start)
+
+    when(both(k == 1, inner), line_spread)
+
+    def core1_collect():
+        collect(0)
+        collect(1)
+
+    when(k == 1, core1_collect)
     when(runner, lambda: loop(0, 16, panel_line))
 
-    def mate_take():
+    def core0_take():
         pair(0).wait_recv()
         pair(1).wait_recv()
 
-    when(mate, mate_take)
+    when(k == 0, core0_take)
     take = {lo: n for n, (lo, hi) in enumerate(GROUPS)}
 
     def inverse_take(n):
-        def as_hub():
-            def as_aide():
-                inverse_first(n, 0).wait_recv()
-                inverse_down(n, start)
-
-            when(aide, as_aide)
-            when(neither(aide), lambda: inverse_taken(n))
+        def first():
+            when(aide, lambda: inverse_first(n, 0).wait_recv())
+            when(inner, lambda: inverse_taken(n))
             inverse_pair(n).start()
 
-        when(hub, as_hub)
-        when(mate, lambda: inverse_pair(n).wait_recv())
+        when(k == 1, first)
+        when(k == 0, lambda: inverse_pair(n).wait_recv())
 
     def put(lo, hi, left, values):
         high = values.astype(jnp.bfloat16)
@@ -566,30 +560,35 @@
             work[hi:256, :] = work[hi:256, :] - dot32(lines[:, hi:256], lines, ((0,), (0,)))
 
     when(mate, mirror_take)
-    when(both(hub, inner), lambda: loop(0, 16, lambda n: panel_pair(n).wait_recv()))
+    when(both(k == 1, inner), lambda: loop(0, 16, lambda n: panel_pair(n).wait_recv()))
     when(top, lambda: loop(0, 8, lambda m: panel_pair(8 * (1 - k) + m).wait_recv()))
 
     when(runner, lambda: loop(0, 16, panel_line_sent))
     when(top, lambda: panel_top(sent))
     when(both(mate, r < 2), lambda: feeds(sent))
 
-    def hub_drain():
-        loop(0, 16, mirror_sent)
+    when(hub, lambda: loop(0, 16, mirror_sent))
+
+    def core1_drain():
         for which in range(2):
             across(which, sent)
             pair(which).wait_send()
-        for n in range(3):
+        for n in range(2):
             inverse_pair(n).wait_send()
 
-    when(hub, hub_drain)
+    when(k == 1, core1_drain)
 
     def line_drain():
         for which in range(2):
             down(which, sent)
-        for n in range(3):
-            inverse_down(n, sent)
 
     when(c == 1, line_drain)
+
+    def head_drain():
+        for n in range(2):
+            inverse_down(n, sent, xs)
+
+    when(head, head_drain)
 
     def aide_drain():
         lead_copy(0).wait_send()
@@ -605,7 +604,7 @@
 
     def root_drain():
         from_root(sent, inverse_piece)
-        for n in range(3):
+        for n in range(2):
             first_all(n, sent)
 
     when(root, root_drain)
@@ -635,15 +634,12 @@
             pltpu.VMEM((384, 512), f32),
             pltpu.VMEM((4, 32, 128), f32),
             pltpu.VMEM((16, 16, 256), f32),
-            pltpu.VMEM((2, 16, 256), bf16),
-            pltpu.VMEM((16, 256), f32),
-            pltpu.VMEM((4, 32, 128), f32),
             pltpu.VMEM((256, 768), f32),
             dma((16, 2)), dma((16,)), dma((16,)), dma((16,)),
             dma((16, 4)), dma((16,)), dma((16,)), dma((16,)),
             dma((2,)), dma((2,)),
             dma((16,)), dma((2,)), dma((2, 16)), dma((2,)), dma((2, 16)), dma((2, 16)), dma((2,)), dma((2,)),
-            dma((4, 16)), dma((4,)), dma((3, 16)), dma((3,)), dma((3,)), dma((3,)), dma((3,)),
+            dma((3, 16)), dma((3,)), dma((2, 16)), dma((2,)), dma((2,)), dma((2,)), dma((3,)),
         ],
         compiler_params=pltpu.CompilerParams(
             collective_id=0, has_side_effects=True, vmem_limit_bytes=24 * 1024 * 1024

time: 62.3 us -> 58.2 us (0.934)
  the two profiles are of different devices: /device:TPU:32 before, /device:TPU:128 now
where the time goes in v5:
time: 58.2 us; the launch traced here: 58 us
  Pallas kernels  57.2 us (98%)
  between operations  0.8 us (1%)
    pallas_call x1, Pallas kernels, gather(): pl.pallas_call(gather_kernel, out_shape=(jax.ShapeDtypeStruct((4, 2, 256,...  52.8 us
    pallas_call x1, Pallas kernels, update(): pl.pallas_call(update_kernel, out_shape=(jax.ShapeDtypeStruct((1, 4, 2, 2...  4.48 us

profile of v5, /device:TPU:128, one launch (start us, length us, event | category | flops | bytes accessed | tf_op | source)
XLA Modules:
  0.0 58.0 jit_solution(14572992026310428530)
XLA Ops:
  0.6 52.8 %gather_and_factor.1 = (bf16[4,2,256,256]{3,2,1,0:T(8,128)(2,1)S(1)}, bf16[2,2,2,256,256]{4,3,2,1,0:T(8,128)(2,1)S(1)}, bf16[2,512,512]{2,1,0:T(8,128)(2,1)S(1)}) custom-call(bf16[1,4,1,2,256,256]{5,4,3,2,1,0:T(8,128)(2,1)} %kern.3), custom_call_target="tpu_custom_call" | custom-call | tf_op jit(solution)/shard_map/gather_and_factor/pallas_call | solution.py:616
  53.4 4.5 %solve_and_update.1 = (f32[1,4,2,256,256]{4,3,2,1,0:T(8,128)}, bf16[1,4,1,2,256,256]{5,4,3,2,1,0:T(8,128)(2,1)}) custom-call(bf16[1,4,1,2,256,256]{5,4,3,2,1,0:T(8,128)(2,1)} %kern.3, bf16[4,2,256,256]{3,2,1,0:T(8,128)(2,1)S(1)} %get-tuple-element.5.acol, bf16[2,2,2,256,256]{4,3,2,1,0:T(8,128)(2,1)S(1)} %get-tuple-element.6.brow, ...), custom_call_target="tpu_custom_call" | custom-call | tf_op jit(solution)/shard_map/solve_and_update/pallas_call | solution.py:713

commit v6 on v5

--- a/solution.py
+++ b/solution.py
@@ -9,7 +9,6 @@
 
 MESH = pl.DeviceIdType.MESH
 HI = lax.Precision.HIGHEST
-GROUPS = ((0, 3), (3, 4))
 PLANE = sorted(((a, b) for a in range(4) for b in range(4) if a or b), key=lambda d: -min(d[0], 4 - d[0]) - min(d[1], 4 - d[1]))
 NEAR = ((0, 1), (0, 3), (1, 0), (3, 0))
 LINE = sorted(range(1, 16), key=lambda d: -min(d, 16 - d))
@@ -110,7 +109,7 @@
         turned = pltpu.roll(wide, 64, 1)
         low = wide if odd else turned
         high = turned if odd else wide
-        if b == 2:
+        if b == 1:
             middle()
         store(b, jnp.where(lax.broadcasted_iota(jnp.int32,(32,128),1) < 64, low[32:], high[:32]))
         base = lo if odd else lo - 64
@@ -145,10 +144,10 @@
 
 def gather_kernel(
     kern, acol, brow, parts,
-    lead, inv0, xs, gbuf, g, x_src, inv_src, work,
+    lead, inv0, inv1, xs, gbuf, g, x_src, inv_src, inv1_src, work,
     p_send, p_recv, p_sib_send, p_sib_recv, m_send, m_recv, m_sib_send, m_sib_recv,
-    lead_send, lead_recv, gs_send, gh_recv, gd_send, gd_recv, ga_send, ga_recv, gx_send, gx_recv,
-    xr_send, xh_recv, xd_send, xd_recv, xx_send, xx_recv, loc,
+    lead_send, lead_recv, gs_send, gh_recv, gd_send, gd_recv, ga_send, ga_recv, parts_send, parts_recv,
+    xr_send, xh_recv, xd_send, xd_recv, loc,
 ):
     r = lax.axis_index("row")
     c = lax.axis_index("col")
@@ -231,7 +230,6 @@
         for d in PLANE:
             signal(peer(d), c)
         when(inner, lambda: signal(r, one))
-        when(both(inner, r == 0), lambda: signal(r, zero))
 
     when(k == 1, greet_plane)
 
@@ -253,7 +251,7 @@
         plane = jnp.where(k == 1, 15, 0) + jnp.where(both(hub, top), 4, 0)
         line = jnp.where(top, 2, jnp.where(k == 0, children, 0))
         down = jnp.where(c == 1, 15, 0)
-        more = jnp.where(root, 30, 0) + jnp.where(aide, 15, 0) + jnp.where(helper, 16, 0)
+        more = jnp.where(root, 15, 0) + jnp.where(aide, 15, 0) + jnp.where(helper, 16, 0)
         pl.semaphore_wait(barrier, 1 + plane + line + down + more)
         when(top, lambda: own_panel.wait())
         when(r < 2, lambda: own_rows.wait())
@@ -261,8 +259,8 @@
         when(helper, lambda: helper_piece.wait())
 
     def panel_chunk(n):
-        col, i, half = lax.div(n, 8), lax.rem(lax.div(n, 2), 4), lax.rem(n, 2)
-        return acol.at[i, col, pl.ds(pl.multiple_of(128 * half, 128), 128)]
+        col, i, quarter = lax.div(n, 16), lax.rem(lax.div(n, 4), 4), lax.rem(n, 4)
+        return acol.at[i, col, pl.ds(pl.multiple_of(64 * quarter, 64), 64)]
 
     def panel_skip(n):
         return remote(panel_chunk(n), panel_chunk(n), p_send.at[n, 0], p_recv.at[n], r, 2 * skip_to)
@@ -275,14 +273,14 @@
 
     def panel_top(act):
         def step(m):
-            act(panel_skip(8 * k + m))
-            act(panel_back(8 * k + m))
-
-        loop(0, 8, step)
-        loop(0, 8, lambda m: act(panel_pair(8 * k + m)))
+            act(panel_skip(16 * k + m))
+            act(panel_back(16 * k + m))
+
+        loop(0, 16, step)
+        loop(0, 16, lambda m: act(panel_pair(16 * k + m)))
 
     def panel_line(t):
-        n = lax.rem(t + jnp.where(r == 0, 8, 0), 16)
+        n = t
         panel_skip(n).wait_recv()
         when(has_skip, lambda: panel_skip(n).start())
         when(has_back, lambda: panel_back(n).start())
@@ -360,68 +358,68 @@
             if p != n:
                 act(lead_from(n, p))
 
+    def view(which, p):
+        if which < 2:
+            return (lead, inv0)[which].at[p]
+        return inv1.at[lax.div(p, 2)]
+
+    def takes_part(which, row):
+        return row >= 0 if which < 2 else lax.rem(row, 2) == 0
+
     def down(which, act):
-        piece = (lead, inv0)[which].at[r]
-        for d in LINE:
-            act(remote(piece, piece, gd_send.at[which, d], gd_recv.at[which], r, jnp.int32(2 * d + 1)))
+        def go():
+            for d in LINE:
+                act(remote(
+                    view(which, r), view(which, r), gd_send.at[which, d], gd_recv.at[which], r, jnp.int32(2 * d + 1)
+                ))
+
+        when(takes_part(which, r), go)
 
     def across(which, act):
-        piece = (lead, inv0)[which].at[r]
-        for n, d in enumerate(PLANE):
-            act(remote(piece, piece, ga_send.at[which, n], ga_recv.at[which, r], peer(d), c))
-
-    def pair(which):
-        buf = (lead, inv0)[which]
-        return remote(buf, buf, gx_send.at[which], gx_recv.at[which], r, sibling)
+        def go():
+            for n, d in enumerate(PLANE):
+                act(remote(view(which, r), view(which, r), ga_send.at[which, n], ga_recv.at[which, r], peer(d), c))
+
+        when(takes_part(which, r), go)
 
     def piece_taken(which):
-        piece = (lead, inv0)[which].at[r]
-        remote(piece, piece, gd_send.at[which, 0], gd_recv.at[which], r, sibling).wait_recv()
+        copy = remote(view(which, r), view(which, r), gd_send.at[which, 0], gd_recv.at[which], r, sibling)
+        when(takes_part(which, r), lambda: copy.wait_recv())
 
     def collect(which):
-        buf = (lead, inv0)[which]
-
         def take(d):
             p = lax.rem(r + d, 16)
-            remote(buf.at[p], buf.at[p], ga_send.at[which, 0], ga_recv.at[which, p], r, sibling).wait_recv()
+            copy = remote(view(which, p), view(which, p), ga_send.at[which, 0], ga_recv.at[which, p], r, sibling)
+            when(takes_part(which, p), lambda: copy.wait_recv())
 
         loop(1, 16, take)
-        pair(which).start()
 
     def inverse_piece(p):
         return remote(inv_src.at[p], inv0.at[p], xr_send.at[0, p], xh_recv.at[0], jnp.int32(p), one)
 
-    def inverse_rows(buf, n):
-        lo, hi = GROUPS[n]
-        return buf.at[pl.ds(lo, hi - lo)]
+    def next_piece(p):
+        return remote(inv1_src.at[p // 2], inv1.at[p // 2], xr_send.at[1, p], xh_recv.at[1], jnp.int32(p), one)
 
     def inverse_first(n, p):
-        return remote(
-            inverse_rows(x_src, n), inverse_rows(xs, n), xr_send.at[1 + n, p], xh_recv.at[1 + n], jnp.int32(p), one
-        )
-
-    def from_root(act, copy):
+        return remote(x_src.at[n], xs.at[n], xr_send.at[2 + n, p], xh_recv.at[2 + n], jnp.int32(p), one)
+
+    def from_root(act, copy, step=1):
         for d in PLANE:
-            act(copy(4 * d[0] + d[1]))
+            p = 4 * d[0] + d[1]
+            if p % step == 0:
+                act(copy(p))
         act(copy(0))
 
-    def inverse_down(n, act, src):
+    def inverse_down(n, act):
         for d in LINE:
-            act(remote(
-                inverse_rows(src, n), inverse_rows(xs, n), xd_send.at[n, d], xd_recv.at[n], r, jnp.int32(2 * d + 1)
-            ))
-
-    def first_all(n, act):
-        inverse_down(n, act, x_src)
-        from_root(act, lambda p: inverse_first(n, p))
+            act(remote(xs.at[n], xs.at[n], xd_send.at[n, d], xd_recv.at[n], r, jnp.int32(2 * d + 1)))
 
     def inverse_taken(n):
-        rows = inverse_rows(xs, n)
-        remote(rows, rows, xd_send.at[n, 0], xd_recv.at[n], r, sibling).wait_recv()
-
-    def inverse_pair(n):
-        rows = inverse_rows(xs, n)
-        return remote(rows, rows, xx_send.at[n], xx_recv.at[n], r, sibling)
+        remote(xs.at[n], xs.at[n], xd_send.at[n, 0], xd_recv.at[n], r, sibling).wait_recv()
+
+    def parts_pair(n):
+        block = parts.at[0] if n == 0 else parts.at[pl.ds(1, 2)]
+        return remote(block, block, parts_send.at[n], parts_recv.at[n], r, sibling)
 
     def lead_copy(n):
         return remote(own_block, gbuf.at[n + 1], lead_send.at[n], lead_recv.at[n], zero, zero)
@@ -450,10 +448,14 @@
 
         def phase(it):
             def store(n, packed):
-                x_src[n] = packed
-                for which, (lo, hi) in enumerate(GROUPS):
-                    if hi == n + 1:
-                        when(it == 1, lambda which=which: first_all(which, start))
+                if n < 2:
+                    for part in range(4):
+                        inv1_src[4 * n + part] = packed[8 * part : 8 * part + 8]
+                    if n == 1:
+                        when(it == 1, lambda: from_root(start, next_piece, 2))
+                else:
+                    x_src[n - 2] = packed
+                    when(it == 1, lambda: from_root(start, lambda p: inverse_first(n - 2, p)))
 
             factor_phase(g, store, lambda: when(it == 0, bulk))
             when(it == 0, second_half)
@@ -476,6 +478,13 @@
     def top_spread(which):
         down(which, start)
         across(which, start)
+
+    def head_inverses(p):
+        when(takes_part(2, r), lambda: next_piece(p).wait_recv())
+        top_spread(2)
+        for n in range(2):
+            inverse_first(n, p).wait_recv()
+            inverse_down(n, start)
 
     def aide_main():
         loop(0, 8, mirror_step)
@@ -484,6 +493,7 @@
         inverse_piece(0).wait_recv()
         top_spread(1)
         loop(8, 16, mirror_step)
+        head_inverses(0)
 
     when(aide, aide_main)
     when(both(hub, neither(aide)), lambda: loop(0, 16, mirror_step))
@@ -494,101 +504,86 @@
         top_spread(0)
         inverse_piece(1).wait_recv()
         top_spread(1)
-        for n in range(2):
-            inverse_first(n, 1).wait_recv()
-            inverse_down(n, start, xs)
+        head_inverses(2)
 
     when(head, head_main)
 
     def line_spread():
-        for which in range(2):
+        for which in range(3):
             piece_taken(which)
             across(which, start)
 
     when(both(k == 1, inner), line_spread)
-
-    def core1_collect():
+    when(runner, lambda: loop(0, 32, panel_line))
+
+    def put(block, lo, hi, values):
+        high = values.astype(jnp.bfloat16)
+        parts[block, 0, lo:hi] = high
+        parts[block, 1, lo:hi] = (values - high.astype(jnp.float32)).astype(jnp.bfloat16)
+
+    def assemble():
+        def block(n):
+            return jnp.concatenate([lead[p, n] for p in range(16)], axis=0).astype(jnp.float32)
+
         collect(0)
         collect(1)
-
-    when(k == 1, core1_collect)
-    when(runner, lambda: loop(0, 16, panel_line))
-
-    def core0_take():
-        pair(0).wait_recv()
-        pair(1).wait_recv()
-
-    when(k == 0, core0_take)
-    take = {lo: n for n, (lo, hi) in enumerate(GROUPS)}
-
-    def inverse_take(n):
-        def first():
-            when(aide, lambda: inverse_first(n, 0).wait_recv())
-            when(inner, lambda: inverse_taken(n))
-            inverse_pair(n).start()
-
-        when(k == 1, first)
-        when(k == 0, lambda: inverse_pair(n).wait_recv())
-
-    def put(lo, hi, left, values):
-        high = values.astype(jnp.bfloat16)
-        parts[0, lo:hi, left : left + 256] = high
-        parts[1, lo:hi, left : left + 256] = (values - high.astype(jnp.float32)).astype(jnp.bfloat16)
-
-    def block(n):
-        return jnp.concatenate([lead[p, n] for p in range(16)], axis=0).astype(jnp.float32)
-
-    first_inverse = jnp.concatenate([inv0[p] for p in range(16)], axis=0)
-    put(0, 256, 0, first_inverse)
-    put(0, 256, 256, jnp.zeros((256, 256), jnp.float32))
-    side = dot32(first_inverse, block(0), ((1,), (0,)))
-    work[:, 0:256] = block(1) - dot32(side, side, ((0,), (0,)))
-    work[:, 256:512] = -dot32(side, first_inverse, ((0,), (0,)))
-    rows = lax.broadcasted_iota(jnp.int32, (256, 256), 0)
-    cols = lax.broadcasted_iota(jnp.int32, (256, 256), 1)
-    work[:, 512:768] = jnp.where(rows == cols, 1.0, 0.0)
-    for n in range(4):
-        if n in take:
-            inverse_take(take[n])
-        packed = xs[n]
-        inverse = jnp.concatenate([packed[:, 64:128], packed[:, 0:64]], axis=0)
-        lo, hi = 64 * n, 64 * n + 64
-        lines = dot32(inverse, work[lo:hi, :], ((1,), (0,)))
-        put(256 + lo, 256 + hi, 0, lines[:, 256:512])
-        put(256 + lo, 256 + hi, 256, lines[:, 512:768])
-        if n < 3:
-            work[hi:256, :] = work[hi:256, :] - dot32(lines[:, hi:256], lines, ((0,), (0,)))
-
+        first_inverse = jnp.concatenate([inv0[p] for p in range(16)], axis=0)
+        put(0, 0, 256, first_inverse)
+        parts_pair(0).start()
+        side = dot32(first_inverse, block(0), ((1,), (0,)))
+        work[:, 0:256] = block(1) - dot32(side, side, ((0,), (0,)))
+        work[:, 256:512] = -dot32(side, first_inverse, ((0,), (0,)))
+        rows = lax.broadcasted_iota(jnp.int32, (256, 256), 0)
+        cols = lax.broadcasted_iota(jnp.int32, (256, 256), 1)
+        work[:, 512:768] = jnp.where(rows == cols, 1.0, 0.0)
+        collect(2)
+        for n in range(4):
+            if n < 2:
+                packed = jnp.concatenate([inv1[4 * n + p] for p in range(4)], axis=0)
+            else:
+                when(inner, lambda: inverse_taken(n - 2))
+                packed = xs[n - 2]
+            inverse = jnp.concatenate([packed[:, 64:128], packed[:, 0:64]], axis=0)
+            lo, hi = 64 * n, 64 * n + 64
+            lines = dot32(inverse, work[lo:hi, :], ((1,), (0,)))
+            put(1, lo, hi, lines[:, 256:512])
+            put(2, lo, hi, lines[:, 512:768])
+            if n < 3:
+                work[hi:256, :] = work[hi:256, :] - dot32(lines[:, hi:256], lines, ((0,), (0,)))
+        parts_pair(1).start()
+
+    when(k == 1, assemble)
+
+    def parts_take():
+        parts_pair(0).wait_recv()
+        parts_pair(1).wait_recv()
+
+    when(k == 0, parts_take)
     when(mate, mirror_take)
-    when(both(k == 1, inner), lambda: loop(0, 16, lambda n: panel_pair(n).wait_recv()))
-    when(top, lambda: loop(0, 8, lambda m: panel_pair(8 * (1 - k) + m).wait_recv()))
-
-    when(runner, lambda: loop(0, 16, panel_line_sent))
+    when(both(k == 1, inner), lambda: loop(0, 32, lambda n: panel_pair(n).wait_recv()))
+    when(top, lambda: loop(0, 16, lambda m: panel_pair(16 * (1 - k) + m).wait_recv()))
+
+    when(runner, lambda: loop(0, 32, panel_line_sent))
     when(top, lambda: panel_top(sent))
     when(both(mate, r < 2), lambda: feeds(sent))
 
     when(hub, lambda: loop(0, 16, mirror_sent))
 
     def core1_drain():
-        for which in range(2):
+        for which in range(3):
             across(which, sent)
-            pair(which).wait_send()
         for n in range(2):
-            inverse_pair(n).wait_send()
+            parts_pair(n).wait_send()
 
     when(k == 1, core1_drain)
 
     def line_drain():
-        for which in range(2):
+        for which in range(3):
             down(which, sent)
+        for n in range(2):
+            inverse_down(n, sent)
 
     when(c == 1, line_drain)
-
-    def head_drain():
-        for n in range(2):
-            inverse_down(n, sent, xs)
-
-    when(head, head_drain)
 
     def aide_drain():
         lead_copy(0).wait_send()
@@ -604,8 +599,9 @@
 
     def root_drain():
         from_root(sent, inverse_piece)
+        from_root(sent, next_piece, 2)
         for n in range(2):
-            first_all(n, sent)
+            from_root(sent, lambda p, n=n: inverse_first(n, p))
 
     when(root, root_drain)
 
@@ -618,7 +614,7 @@
         out_shape=(
             jax.ShapeDtypeStruct((4, 2, 256, 256), bf16),
             jax.ShapeDtypeStruct((2, 2, 2, 256, 256), bf16),
-            jax.ShapeDtypeStruct((2, 512, 512), bf16),
+            jax.ShapeDtypeStruct((3, 2, 256, 256), bf16),
         ),
         in_specs=[pl.BlockSpec(memory_space=pltpu.HBM)],
         out_specs=(
@@ -629,17 +625,19 @@
         scratch_shapes=[
             pltpu.VMEM((16, 2, 16, 256), bf16),
             pltpu.VMEM((16, 16, 256), f32),
-            pltpu.VMEM((4, 32, 128), f32),
+            pltpu.VMEM((8, 8, 128), f32),
+            pltpu.VMEM((2, 32, 128), f32),
             pltpu.VMEM((3, 256, 256), bf16),
             pltpu.VMEM((384, 512), f32),
-            pltpu.VMEM((4, 32, 128), f32),
+            pltpu.VMEM((2, 32, 128), f32),
             pltpu.VMEM((16, 16, 256), f32),
+            pltpu.VMEM((8, 8, 128), f32),
             pltpu.VMEM((256, 768), f32),
-            dma((16, 2)), dma((16,)), dma((16,)), dma((16,)),
+            dma((32, 2)), dma((32,)), dma((32,)), dma((32,)),
             dma((16, 4)), dma((16,)), dma((16,)), dma((16,)),
             dma((2,)), dma((2,)),
-            dma((16,)), dma((2,)), dma((2, 16)), dma((2,)), dma((2, 16)), dma((2, 16)), dma((2,)), dma((2,)),
-            dma((3, 16)), dma((3,)), dma((2, 16)), dma((2,)), dma((2,)), dma((2,)), dma((3,)),
+            dma((16,)), dma((2,)), dma((3, 16)), dma((3,)), dma((3, 16)), dma((3, 16)), dma((2,)), dma((2,)),
+            dma((4, 16)), dma((4,)), dma((2, 16)), dma((2,)), dma((3,)),
         ],
         compiler_params=pltpu.CompilerParams(
             collective_id=0, has_side_effects=True, vmem_limit_bytes=24 * 1024 * 1024
@@ -662,7 +660,7 @@
             for s in range(n + 1):
                 for t in range(2):
                     term = jnp.dot(
-                        parts[t, 256 * n : 256 * n + 256, 256 * s : 256 * s + 256],
+                        parts[n + s, t],
                         brow[s, j, k],
                         preferred_element_type=jnp.float32,
                     )
@@ -680,7 +678,7 @@
                 for t in range(2):
                     term = lax.dot_general(
                         acol[i, s],
-                        parts[t, 256 * n : 256 * n + 256, 256 * s : 256 * s + 256],
+                        parts[n + s, t],
                         (((1,), (1,)), ((), ())),
                         preferred_element_type=jnp.float32,
                     )

time: 58.2 us -> 51.3 us (0.88)
  the two profiles are of different devices: /device:TPU:128 before, /device:TPU:145 now
where the time goes in v6:
time: 51.3 us; the launch traced here: 51.1 us
  Pallas kernels  50.3 us (98%)
  between operations  0.8 us (2%)
    pallas_call x1, Pallas kernels, gather(): pl.pallas_call(gather_kernel, out_shape=(jax.ShapeDtypeStruct((4, 2, 256,...  45.8 us
    pallas_call x1, Pallas kernels, update(): pl.pallas_call(update_kernel, out_shape=(jax.ShapeDtypeStruct((1, 4, 2, 2...  4.48 us

profile of v6, /device:TPU:145, one launch (start us, length us, event | category | flops | bytes accessed | tf_op | source)
XLA Modules:
  0.0 51.1 jit_solution(4280266211604011633)
XLA Ops:
  0.6 45.8 %gather_and_factor.1 = (bf16[4,2,256,256]{3,2,1,0:T(8,128)(2,1)S(1)}, bf16[2,2,2,256,256]{4,3,2,1,0:T(8,128)(2,1)S(1)}, bf16[3,2,256,256]{3,2,1,0:T(8,128)(2,1)S(1)}) custom-call(bf16[1,4,1,2,256,256]{5,4,3,2,1,0:T(8,128)(2,1)} %kern.3), custom_call_target="tpu_custom_call" | custom-call | tf_op jit(solution)/shard_map/gather_and_factor/pallas_call | solution.py:612
  46.4 4.5 %solve_and_update.1 = (f32[1,4,2,256,256]{4,3,2,1,0:T(8,128)}, bf16[1,4,1,2,256,256]{5,4,3,2,1,0:T(8,128)(2,1)}) custom-call(bf16[1,4,1,2,256,256]{5,4,3,2,1,0:T(8,128)(2,1)} %kern.3, bf16[4,2,256,256]{3,2,1,0:T(8,128)(2,1)S(1)} %get-tuple-element.5.acol, bf16[2,2,2,256,256]{4,3,2,1,0:T(8,128)(2,1)S(1)} %get-tuple-element.6.brow, ...), custom_call_target="tpu_custom_call" | custom-call | tf_op jit(solution)/shard_map/solve_and_update/pallas_call | solution.py:711

commit v7 on v6

--- a/solution.py
+++ b/solution.py
@@ -12,6 +12,8 @@
 PLANE = sorted(((a, b) for a in range(4) for b in range(4) if a or b), key=lambda d: -min(d[0], 4 - d[0]) - min(d[1], 4 - d[1]))
 NEAR = ((0, 1), (0, 3), (1, 0), (3, 0))
 LINE = sorted(range(1, 16), key=lambda d: -min(d, 16 - d))
+FIRST = (8, 4, 12, 1, 15)
+RELAY = {4: (2, 6, 3, 5), 8: (7, 9), 12: (10, 14, 11, 13)}
 SKIP = {0: 3, 3: 6, 6: 8, 13: 10, 10: 9}
 BACK = {0: 13, 3: 2, 2: 1, 6: 5, 5: 4, 8: 7, 13: 14, 14: 15, 10: 11, 11: 12}
 
@@ -175,6 +177,7 @@
     has_back = member(z, list(BACK))
     parent = lookup(z, {v: q for q, v in list(SKIP.items()) + list(BACK.items())})
     children = has_skip.astype(jnp.int32) + has_back.astype(jnp.int32)
+    relay_of = lookup(z, {v: q for q, vs in RELAY.items() for v in vs})
     barrier = pltpu.get_barrier_semaphore()
 
     def remote(src, dst, send, recv, row, col):
@@ -230,6 +233,7 @@
         for d in PLANE:
             signal(peer(d), c)
         when(inner, lambda: signal(r, one))
+        when(relay_of != 0, lambda: signal(r, 2 * relay_of + 1))
 
     when(k == 1, greet_plane)
 
@@ -251,6 +255,8 @@
         plane = jnp.where(k == 1, 15, 0) + jnp.where(both(hub, top), 4, 0)
         line = jnp.where(top, 2, jnp.where(k == 0, children, 0))
         down = jnp.where(c == 1, 15, 0)
+        relays = jnp.where(jnp.logical_or(z == 4, z == 12), 4, jnp.where(z == 8, 2, 0))
+        down = down + jnp.where(k == 1, relays, 0)
         more = jnp.where(root, 15, 0) + jnp.where(aide, 15, 0) + jnp.where(helper, 16, 0)
         pl.semaphore_wait(barrier, 1 + plane + line + down + more)
         when(top, lambda: own_panel.wait())
@@ -366,14 +372,28 @@
     def takes_part(which, row):
         return row >= 0 if which < 2 else lax.rem(row, 2) == 0
 
+    def line_copy(which, d):
+        piece = view(which, r)
+        return remote(piece, piece, gd_send.at[which, d], gd_recv.at[which], r, jnp.int32(2 * d + 1))
+
     def down(which, act):
         def go():
-            for d in LINE:
-                act(remote(
-                    view(which, r), view(which, r), gd_send.at[which, d], gd_recv.at[which], r, jnp.int32(2 * d + 1)
-                ))
+            for d in FIRST:
+                act(line_copy(which, d))
 
         when(takes_part(which, r), go)
+
+    def relay(act, copy):
+        for q, targets in RELAY.items():
+
+            def go(targets=targets):
+                for d in targets:
+                    act(copy(d))
+
+            when(z == q, go)
+
+    def relay_piece(which, act):
+        when(takes_part(which, r), lambda: relay(act, lambda d: line_copy(which, d)))
 
     def across(which, act):
         def go():
@@ -410,9 +430,16 @@
                 act(copy(p))
         act(copy(0))
 
+    def inverse_copy(n, d):
+        return remote(xs.at[n], xs.at[n], xd_send.at[n, d], xd_recv.at[n], r, jnp.int32(2 * d + 1))
+
     def inverse_down(n, act):
-        for d in LINE:
-            act(remote(xs.at[n], xs.at[n], xd_send.at[n, d], xd_recv.at[n], r, jnp.int32(2 * d + 1)))
+        for d in FIRST if n == 0 else LINE:
+            act(inverse_copy(n, d))
+
+    def inverse_relay(n, act):
+        if n == 0:
+            relay(act, lambda d: inverse_copy(n, d))
 
     def inverse_taken(n):
         remote(xs.at[n], xs.at[n], xd_send.at[n, 0], xd_recv.at[n], r, sibling).wait_recv()
@@ -511,6 +538,7 @@
     def line_spread():
         for which in range(3):
             piece_taken(which)
+            relay_piece(which, start)
             across(which, start)
 
     when(both(k == 1, inner), line_spread)
@@ -541,7 +569,12 @@
             if n < 2:
                 packed = jnp.concatenate([inv1[4 * n + p] for p in range(4)], axis=0)
             else:
-                when(inner, lambda: inverse_taken(n - 2))
+
+                def arrived(n=n - 2):
+                    inverse_taken(n)
+                    inverse_relay(n, start)
+
+                when(inner, arrived)
                 packed = xs[n - 2]
             inverse = jnp.concatenate([packed[:, 64:128], packed[:, 0:64]], axis=0)
             lo, hi = 64 * n, 64 * n + 64
@@ -584,6 +617,13 @@
             inverse_down(n, sent)
 
     when(c == 1, line_drain)
+
+    def relay_drain():
+        for which in range(3):
+            relay_piece(which, sent)
+        inverse_relay(0, sent)
+
+    when(both(k == 1, inner), relay_drain)
 
     def aide_drain():
         lead_copy(0).wait_send()
@@ -652,58 +692,60 @@
     k = lax.rem(c, 2)
     load = pltpu.make_async_copy(kern.at[0, :, 0], old, sems.at[0])
     load.start()
-    mirror = []
-    for j in range(2):
-        halves = []
-        for n in range(2):
-            total = None
-            for s in range(n + 1):
-                for t in range(2):
-                    term = jnp.dot(
-                        parts[n + s, t],
-                        brow[s, j, k],
-                        preferred_element_type=jnp.float32,
-                    )
-                    total = term if total is None else total + term
-            halves.append(total.astype(jnp.bfloat16))
-        mirror.append(jnp.concatenate(halves, axis=0))
+    f32 = jnp.float32
     tri = lax.broadcasted_iota(jnp.int32, (256, 256), 0) >= lax.broadcasted_iota(jnp.int32, (256, 256), 1)
     stores = []
+
+    def store(src, dst):
+        stores.append(pltpu.make_async_copy(src, dst, sems.at[1 + len(stores)]))
+        stores[-1].start()
+
+    def rows(a, b):
+        return lax.dot_general(a, b, (((1,), (1,)), ((), ())), preferred_element_type=f32)
+
+    lefts = []
+    for h in range(2):
+        a, b = (jnp.concatenate([acol[2 * h, s], acol[2 * h + 1, s]], axis=0) for s in range(2))
+        first = rows(a, parts[0, 0]) + rows(a, parts[0, 1])
+        second = rows(a, parts[1, 0]) + rows(a, parts[1, 1]) + rows(b, parts[2, 0]) + rows(b, parts[2, 1])
+        lefts.append(jnp.concatenate([first.astype(jnp.bfloat16), second.astype(jnp.bfloat16)], axis=1))
+        for e in range(2):
+            i = 2 * h + e
+            for n, solved in enumerate((first, second)):
+                part = solved[256 * e : 256 * e + 256]
+                if i == 0:
+                    whole = jnp.logical_or(r > n, jnp.logical_and(r == n, tri))
+                    part = jnp.where(whole, part, 0.0)
+                pan[i, n] = part
+            store(pan.at[i], panels.at[0, i])
+    columns = []
+    for j in range(2):
+        a, b = brow[0, j, k], brow[1, j, k]
+        upper = jnp.dot(parts[0, 0], a, preferred_element_type=f32) + jnp.dot(
+            parts[0, 1], a, preferred_element_type=f32
+        )
+        lower = jnp.dot(parts[1, 0], a, preferred_element_type=f32) + jnp.dot(
+            parts[1, 1], a, preferred_element_type=f32
+        )
+        lower = lower + jnp.dot(parts[2, 0], b, preferred_element_type=f32)
+        lower = lower + jnp.dot(parts[2, 1], b, preferred_element_type=f32)
+        columns.append(jnp.concatenate([upper, lower], axis=0).astype(jnp.bfloat16))
+    mirror = jnp.concatenate(columns, axis=1)
     load.wait()
-    for i in range(4):
-        solved = []
-        for n in range(2):
-            total = None
-            for s in range(n + 1):
-                for t in range(2):
-                    term = lax.dot_general(
-                        acol[i, s],
-                        parts[n + s, t],
-                        (((1,), (1,)), ((), ())),
-                        preferred_element_type=jnp.float32,
-                    )
-                    total = term if total is None else total + term
-            solved.append(total)
-        left = jnp.concatenate([a.astype(jnp.bfloat16) for a in solved], axis=1)
-        if i == 0:
-            solved[0] = jnp.where(jnp.logical_or(r != 0, tri), solved[0], 0.0)
-            solved[1] = jnp.where(jnp.logical_or(r > 1, jnp.logical_and(r == 1, tri)), solved[1], 0.0)
-        for n in range(2):
-            pan[i, n] = solved[n]
-        stores.append(pltpu.make_async_copy(pan.at[i], panels.at[0, i], sems.at[1 + 2 * i]))
-        stores[-1].start()
-        for j in range(2):
-            change = jnp.dot(left, mirror[j], preferred_element_type=jnp.float32)
-            out = (old[i, j].astype(jnp.float32) - change).astype(jnp.bfloat16)
-            if i == 0:
-                out = jnp.where(r >= 2, out, jnp.zeros_like(out))
-            if j == 0:
-                out = jnp.where(c >= 2, out, jnp.zeros_like(out))
-            new[i, j] = out
-        stores.append(pltpu.make_async_copy(new.at[i], schur.at[0, i, 0], sems.at[2 + 2 * i]))
-        stores[-1].start()
-    for store in stores:
-        store.wait()
+    for h in range(2):
+        change = jnp.dot(lefts[h], mirror, preferred_element_type=f32)
+        for e in range(2):
+            i = 2 * h + e
+            for j in range(2):
+                out = old[i, j].astype(f32) - change[256 * e : 256 * e + 256, 256 * j : 256 * j + 256]
+                if i == 0:
+                    out = jnp.where(r >= 2, out, 0.0)
+                if j == 0:
+                    out = jnp.where(c >= 2, out, 0.0)
+                new[i, j] = out.astype(jnp.bfloat16)
+            store(new.at[i], schur.at[0, i, 0])
+    for copy in stores:
+        copy.wait()
 
 
 def update(kernel, *gathered):

time: 51.3 us -> 52.9 us (1.031)
  the two profiles are of different devices: /device:TPU:145 before, /device:TPU:160 now
where the time goes in v7:
time: 52.9 us; the launch traced here: 52.8 us
  Pallas kernels  52 us (98%)
  between operations  0.8 us (2%)
    pallas_call x1, Pallas kernels, gather(): pl.pallas_call(gather_kernel, out_shape=(jax.ShapeDtypeStruct((4, 2, 256,...  49 us
    pallas_call x1, Pallas kernels, update(): pl.pallas_call(update_kernel, out_shape=(jax.ShapeDtypeStruct((1, 4, 2, 2...  3.01 us

profile of v7, /device:TPU:160, one launch (start us, length us, event | category | flops | bytes accessed | tf_op | source)
XLA Modules:
  0.0 52.8 jit_solution(16793631278674230261)
XLA Ops:
  0.6 49.0 %gather_and_factor.1 = (bf16[4,2,256,256]{3,2,1,0:T(8,128)(2,1)S(1)}, bf16[2,2,2,256,256]{4,3,2,1,0:T(8,128)(2,1)S(1)}, bf16[3,2,256,256]{3,2,1,0:T(8,128)(2,1)S(1)}) custom-call(bf16[1,4,1,2,256,256]{5,4,3,2,1,0:T(8,128)(2,1)} %kern.3), custom_call_target="tpu_custom_call" | custom-call | tf_op jit(solution)/shard_map/gather_and_factor/pallas_call | solution.py:652
  49.6 3.0 %solve_and_update.1 = (f32[1,4,2,256,256]{4,3,2,1,0:T(8,128)}, bf16[1,4,1,2,256,256]{5,4,3,2,1,0:T(8,128)(2,1)}) custom-call(bf16[1,4,1,2,256,256]{5,4,3,2,1,0:T(8,128)(2,1)} %kern.3, bf16[4,2,256,256]{3,2,1,0:T(8,128)(2,1)S(1)} %get-tuple-element.5.acol, bf16[2,2,2,256,256]{4,3,2,1,0:T(8,128)(2,1)S(1)} %get-tuple-element.6.brow, ...), custom_call_target="tpu_custom_call" | custom-call | tf_op jit(solution)/shard_map/solve_and_update/pallas_call | solution.py:753

commit v8 on v7

--- a/solution.py
+++ b/solution.py
@@ -224,7 +224,7 @@
     signal(r, sibling)
 
     def greet_panel():
-        signal(r, 2 * parent)
+        when(jnp.logical_or(parent != 0, r != 0), lambda: signal(r, 2 * parent))
         when(parent == 0, lambda: signal(r, one))
 
     when(runner, greet_panel)
@@ -253,7 +253,7 @@
 
     def arrive():
         plane = jnp.where(k == 1, 15, 0) + jnp.where(both(hub, top), 4, 0)
-        line = jnp.where(top, 2, jnp.where(k == 0, children, 0))
+        line = jnp.where(root, 0, jnp.where(top, 2, jnp.where(k == 0, children, 0)))
         down = jnp.where(c == 1, 15, 0)
         relays = jnp.where(jnp.logical_or(z == 4, z == 12), 4, jnp.where(z == 8, 2, 0))
         down = down + jnp.where(k == 1, relays, 0)
@@ -264,42 +264,37 @@
         when(aide, lambda: aide_piece.wait())
         when(helper, lambda: helper_piece.wait())
 
-    def panel_chunk(n):
-        col, i, quarter = lax.div(n, 16), lax.rem(lax.div(n, 4), 4), lax.rem(n, 4)
-        return acol.at[i, col, pl.ds(pl.multiple_of(64 * quarter, 64), 64)]
-
-    def panel_skip(n):
-        return remote(panel_chunk(n), panel_chunk(n), p_send.at[n, 0], p_recv.at[n], r, 2 * skip_to)
-
-    def panel_back(n):
-        return remote(panel_chunk(n), panel_chunk(n), p_send.at[n, 1], p_recv.at[n], r, 2 * back_to)
-
-    def panel_pair(n):
-        return remote(panel_chunk(n), panel_chunk(n), p_sib_send.at[n], p_sib_recv.at[n], r, sibling)
-
-    def panel_top(act):
-        def step(m):
-            act(panel_skip(16 * k + m))
-            act(panel_back(16 * k + m))
-
-        loop(0, 16, step)
-        loop(0, 16, lambda m: act(panel_pair(16 * k + m)))
-
-    def panel_line(t):
-        n = t
-        panel_skip(n).wait_recv()
-        when(has_skip, lambda: panel_skip(n).start())
-        when(has_back, lambda: panel_back(n).start())
-        panel_pair(n).start()
-
-    def panel_line_sent(n):
-        when(has_skip, lambda: panel_skip(n).wait_send())
-        when(has_back, lambda: panel_back(n).wait_send())
-        panel_pair(n).wait_send()
+    CHUNKS = tuple((i, quarter) for i in range(4) for quarter in range(4))
+
+    def panel_copy(col, m, way):
+        i, quarter = CHUNKS[m]
+        chunk = acol.at[i, col, pl.ds(64 * quarter, 64)]
+        n = 16 * col + m
+        to = (r, 2 * skip_to) if way == 0 else (r, 2 * back_to) if way == 1 else (r, sibling)
+        send = p_sib_send.at[n] if way == 2 else p_send.at[n, way]
+        recv = p_sib_recv.at[n] if way == 2 else p_recv.at[n]
+        return remote(chunk, chunk, send, recv, *to)
+
+    def column_pair(col):
+        return remote(acol.at[:, col], acol.at[:, col], p_sib_send.at[32], p_sib_recv.at[32], r, sibling)
+
+    def panel_top(col, act):
+        for m in range(16):
+            act(panel_copy(col, m, 0))
+            act(panel_copy(col, m, 1))
+
+    def panel_line(t, act, arrive_first):
+        col = jnp.where(r == 0, 1 - t, t)
+        for m in range(16):
+            if arrive_first:
+                panel_copy(col, m, 0).wait_recv()
+            when(has_skip, lambda m=m: act(panel_copy(col, m, 0)))
+            when(has_back, lambda m=m: act(panel_copy(col, m, 1)))
+            act(panel_copy(col, m, 2))
 
     def mirror_chunk(s, m):
-        j, kc, half = lax.div(m, 4), lax.rem(lax.div(m, 2), 2), lax.rem(m, 2)
-        return brow.at[s, j, kc, pl.ds(pl.multiple_of(128 * half, 128), 128)]
+        j, half = m // 4, m % 2
+        return brow.at[s, j, (m // 2) % 2, pl.ds(128 * half, 128)]
 
     def mirror_copy(s, m, way, row):
         chunk = mirror_chunk(s, m)
@@ -310,35 +305,37 @@
         return remote(mirror_chunk(s, m), mirror_chunk(s, m), m_sib_send.at[n], m_sib_recv.at[n], r, sibling)
 
     def mirror_feed(j, half):
-        m = 4 * j + 2 * k + half
-        n = 8 * r + m
-        return remote(mirror_chunk(r, m), mirror_chunk(r, m), m_sib_send.at[n], m_recv.at[n], r, sibling)
+        n = 8 * r + 4 * j + 2 * k + half
+        chunk = brow.at[r, j, k, pl.ds(128 * half, 128)]
+        return remote(chunk, chunk, m_sib_send.at[n], m_recv.at[n], r, sibling)
 
     def mirror_each(s, m, act):
-        j, kc = lax.div(m, 4), lax.rem(lax.div(m, 2), 2)
+        j, kc = m // 4, (m // 2) % 2
         rel = lax.rem(y + 4 - s, 4)
-        ring = jnp.logical_or(j == 1, x == 0)
-        line = jnp.logical_or(j == 0, rel == 0)
-        ring_up = both(ring, jnp.logical_or(rel == 0, both(s == 1, rel == 1)))
-        ring_down = both(ring, jnp.logical_or(rel == 0, both(s == 0, rel == 3)))
-        line_up = both(line, jnp.logical_or(x == 0, both(s == 0, x == 1)))
-        line_down = both(line, jnp.logical_or(x == 0, both(s == 1, x == 3)))
+        ring_up = jnp.logical_or(rel == 0, both(s == 1, rel == 1))
+        ring_down = jnp.logical_or(rel == 0, both(s == 0, rel == 3))
+        line_up = jnp.logical_or(x == 0, both(s == 0, x == 1))
+        line_down = jnp.logical_or(x == 0, both(s == 1, x == 3))
+        if j == 0:
+            ring_up, ring_down = both(ring_up, x == 0), both(ring_down, x == 0)
+        else:
+            line_up, line_down = both(line_up, rel == 0), both(line_down, rel == 0)
         when(ring_up, lambda: act(mirror_copy(s, m, 0, peer((0, 1)))))
         when(ring_down, lambda: act(mirror_copy(s, m, 1, peer((0, 3)))))
         when(line_up, lambda: act(mirror_copy(s, m, 2, peer((1, 0)))))
         when(line_down, lambda: act(mirror_copy(s, m, 3, peer((3, 0)))))
         when(both(kc != k, r != s), lambda: act(mirror_pair(s, m)))
 
-    def mirror_step(n):
+    def mirror_half(t):
         nearer = jnp.where(jnp.logical_or(y == 0, y == 3), 0, 1)
-        s = lax.rem(lax.div(n, 8) + nearer, 2)
-        m = lax.rem(n, 8)
-        kc = lax.rem(lax.div(m, 2), 2)
-        when(jnp.logical_or(r != s, kc != k), lambda: mirror_copy(s, m, 0, r).wait_recv())
-        mirror_each(s, m, start)
-
-    def mirror_sent(n):
-        mirror_each(lax.div(n, 8), lax.rem(n, 8), sent)
+        s = jnp.where(nearer == t, 0, 1)
+        for m in range(8):
+            when(jnp.logical_or(r != s, k != (m // 2) % 2), lambda m=m: mirror_copy(s, m, 0, r).wait_recv())
+            mirror_each(s, m, start)
+
+    def mirror_sent(s):
+        for m in range(8):
+            mirror_each(s, m, sent)
 
     def feeds(act):
         for j in range(2):
@@ -349,9 +346,14 @@
         for s in range(2):
 
             def take(s=s):
-                for j in range(2):
-                    for half in range(2):
-                        mirror_pair(s, 4 * j + 2 * k + half).wait_recv()
+                for kc in range(2):
+
+                    def mine(kc=kc):
+                        for j in range(2):
+                            for half in range(2):
+                                mirror_pair(s, 4 * j + 2 * kc + half).wait_recv()
+
+                    when(k == kc, mine)
 
             when(r != s, take)
 
@@ -460,8 +462,8 @@
 
         def bulk():
             arrive()
+            column_pair(0).start()
             feeds(start)
-            panel_top(start)
 
         def second_half():
             for p in range(16):
@@ -495,7 +497,8 @@
     def top_sends():
         when(aide, lambda: lead_copy(0).start())
         when(helper, lambda: lead_copy(1).start())
-        panel_top(start)
+        panel_top(k, start)
+        column_pair(k).start()
         when(aide, lambda: lead_scatter(0, start))
         when(helper, lambda: lead_scatter(1, start))
 
@@ -514,16 +517,18 @@
             inverse_down(n, start)
 
     def aide_main():
-        loop(0, 8, mirror_step)
+        column_pair(0).wait_recv()
+        panel_top(0, start)
+        loop(0, 1, mirror_half)
         lead_from(1, 0).wait_recv()
         top_spread(0)
         inverse_piece(0).wait_recv()
         top_spread(1)
-        loop(8, 16, mirror_step)
+        loop(1, 2, mirror_half)
         head_inverses(0)
 
     when(aide, aide_main)
-    when(both(hub, neither(aide)), lambda: loop(0, 16, mirror_step))
+    when(both(hub, neither(aide)), lambda: loop(0, 2, mirror_half))
 
     def head_main():
         lead_from(0, 1).wait_recv()
@@ -542,7 +547,7 @@
             across(which, start)
 
     when(both(k == 1, inner), line_spread)
-    when(runner, lambda: loop(0, 32, panel_line))
+    when(runner, lambda: loop(0, 2, lambda t: panel_line(t, start, True)))
 
     def put(block, lo, hi, values):
         high = values.astype(jnp.bfloat16)
@@ -593,14 +598,25 @@
 
     when(k == 0, parts_take)
     when(mate, mirror_take)
-    when(both(k == 1, inner), lambda: loop(0, 32, lambda n: panel_pair(n).wait_recv()))
-    when(top, lambda: loop(0, 16, lambda m: panel_pair(16 * (1 - k) + m).wait_recv()))
-
-    when(runner, lambda: loop(0, 32, panel_line_sent))
-    when(top, lambda: panel_top(sent))
+
+    def column_taken(col):
+        for m in range(16):
+            panel_copy(col, m, 2).wait_recv()
+
+    when(both(k == 1, inner), lambda: loop(0, 2, column_taken))
+    when(both(top, neither(aide)), lambda: column_pair(1 - k).wait_recv())
+
+    when(runner, lambda: loop(0, 2, lambda t: panel_line(t, sent, False)))
+
+    def top_drain():
+        column_pair(k).wait_send()
+        when(neither(root), lambda: panel_top(k, sent))
+        when(aide, lambda: panel_top(0, sent))
+
+    when(top, top_drain)
     when(both(mate, r < 2), lambda: feeds(sent))
 
-    when(hub, lambda: loop(0, 16, mirror_sent))
+    when(hub, lambda: loop(0, 2, mirror_sent))
 
     def core1_drain():
         for which in range(3):
@@ -673,7 +689,7 @@
             pltpu.VMEM((16, 16, 256), f32),
             pltpu.VMEM((8, 8, 128), f32),
             pltpu.VMEM((256, 768), f32),
-            dma((32, 2)), dma((32,)), dma((32,)), dma((32,)),
+            dma((32, 2)), dma((32,)), dma((33,)), dma((33,)),
             dma((16, 4)), dma((16,)), dma((16,)), dma((16,)),
             dma((2,)), dma((2,)),
             dma((16,)), dma((2,)), dma((3, 16)), dma((3,)), dma((3, 16)), dma((3, 16)), dma((2,)), dma((2,)),

time: 52.9 us -> 52.6 us (level)
  no operation moved by 1% of the time
where the time goes in v8:
time: 52.6 us; the launch traced here: 52.5 us
  Pallas kernels  51.7 us (98%)
  between operations  0.8 us (2%)
    pallas_call x1, Pallas kernels, gather(): pl.pallas_call(gather_kernel, out_shape=(jax.ShapeDtypeStruct((4, 2, 256,...  48.7 us
    pallas_call x1, Pallas kernels, update(): pl.pallas_call(update_kernel, out_shape=(jax.ShapeDtypeStruct((1, 4, 2, 2...  3 us

profile of v8, /device:TPU:160, one launch (start us, length us, event | category | flops | bytes accessed | tf_op | source)
XLA Modules:
  0.0 52.5 jit_solution(6632885927526816879)
XLA Ops:
  0.6 48.7 %gather_and_factor.1 = (bf16[4,2,256,256]{3,2,1,0:T(8,128)(2,1)S(1)}, bf16[2,2,2,256,256]{4,3,2,1,0:T(8,128)(2,1)S(1)}, bf16[3,2,256,256]{3,2,1,0:T(8,128)(2,1)S(1)}) custom-call(bf16[1,4,1,2,256,256]{5,4,3,2,1,0:T(8,128)(2,1)} %kern.3), custom_call_target="tpu_custom_call" | custom-call | tf_op jit(solution)/shard_map/gather_and_factor/pallas_call | solution.py:668
  49.3 3.0 %solve_and_update.1 = (f32[1,4,2,256,256]{4,3,2,1,0:T(8,128)}, bf16[1,4,1,2,256,256]{5,4,3,2,1,0:T(8,128)(2,1)}) custom-call(bf16[1,4,1,2,256,256]{5,4,3,2,1,0:T(8,128)(2,1)} %kern.3, bf16[4,2,256,256]{3,2,1,0:T(8,128)(2,1)S(1)} %get-tuple-element.5.acol, bf16[2,2,2,256,256]{4,3,2,1,0:T(8,128)(2,1)S(1)} %get-tuple-element.6.brow, ...), custom_call_target="tpu_custom_call" | custom-call | tf_op jit(solution)/shard_map/solve_and_update/pallas_call | solution.py:769

commit v9 on v8

--- a/solution.py
+++ b/solution.py
@@ -12,8 +12,7 @@
 PLANE = sorted(((a, b) for a in range(4) for b in range(4) if a or b), key=lambda d: -min(d[0], 4 - d[0]) - min(d[1], 4 - d[1]))
 NEAR = ((0, 1), (0, 3), (1, 0), (3, 0))
 LINE = sorted(range(1, 16), key=lambda d: -min(d, 16 - d))
-FIRST = (8, 4, 12, 1, 15)
-RELAY = {4: (2, 6, 3, 5), 8: (7, 9), 12: (10, 14, 11, 13)}
+GROUPS = ((0, 2), (2, 3), (3, 4))
 SKIP = {0: 3, 3: 6, 6: 8, 13: 10, 10: 9}
 BACK = {0: 13, 3: 2, 2: 1, 6: 5, 5: 4, 8: 7, 13: 14, 14: 15, 10: 11, 11: 12}
 
@@ -146,7 +145,7 @@
 
 def gather_kernel(
     kern, acol, brow, parts,
-    lead, inv0, inv1, xs, gbuf, g, x_src, inv_src, inv1_src, work,
+    lead, inv0, xs, gbuf, g, x_src, inv_src, work,
     p_send, p_recv, p_sib_send, p_sib_recv, m_send, m_recv, m_sib_send, m_sib_recv,
     lead_send, lead_recv, gs_send, gh_recv, gd_send, gd_recv, ga_send, ga_recv, parts_send, parts_recv,
     xr_send, xh_recv, xd_send, xd_recv, loc,
@@ -177,7 +176,6 @@
     has_back = member(z, list(BACK))
     parent = lookup(z, {v: q for q, v in list(SKIP.items()) + list(BACK.items())})
     children = has_skip.astype(jnp.int32) + has_back.astype(jnp.int32)
-    relay_of = lookup(z, {v: q for q, vs in RELAY.items() for v in vs})
     barrier = pltpu.get_barrier_semaphore()
 
     def remote(src, dst, send, recv, row, col):
@@ -233,7 +231,6 @@
         for d in PLANE:
             signal(peer(d), c)
         when(inner, lambda: signal(r, one))
-        when(relay_of != 0, lambda: signal(r, 2 * relay_of + 1))
 
     when(k == 1, greet_plane)
 
@@ -255,8 +252,6 @@
         plane = jnp.where(k == 1, 15, 0) + jnp.where(both(hub, top), 4, 0)
         line = jnp.where(root, 0, jnp.where(top, 2, jnp.where(k == 0, children, 0)))
         down = jnp.where(c == 1, 15, 0)
-        relays = jnp.where(jnp.logical_or(z == 4, z == 12), 4, jnp.where(z == 8, 2, 0))
-        down = down + jnp.where(k == 1, relays, 0)
         more = jnp.where(root, 15, 0) + jnp.where(aide, 15, 0) + jnp.where(helper, 16, 0)
         pl.semaphore_wait(barrier, 1 + plane + line + down + more)
         when(top, lambda: own_panel.wait())
@@ -367,87 +362,54 @@
                 act(lead_from(n, p))
 
     def view(which, p):
-        if which < 2:
-            return (lead, inv0)[which].at[p]
-        return inv1.at[lax.div(p, 2)]
-
-    def takes_part(which, row):
-        return row >= 0 if which < 2 else lax.rem(row, 2) == 0
-
-    def line_copy(which, d):
+        return (lead, inv0)[which].at[p]
+
+    def down(which, act):
         piece = view(which, r)
-        return remote(piece, piece, gd_send.at[which, d], gd_recv.at[which], r, jnp.int32(2 * d + 1))
-
-    def down(which, act):
-        def go():
-            for d in FIRST:
-                act(line_copy(which, d))
-
-        when(takes_part(which, r), go)
-
-    def relay(act, copy):
-        for q, targets in RELAY.items():
-
-            def go(targets=targets):
-                for d in targets:
-                    act(copy(d))
-
-            when(z == q, go)
-
-    def relay_piece(which, act):
-        when(takes_part(which, r), lambda: relay(act, lambda d: line_copy(which, d)))
+        for d in LINE:
+            act(remote(piece, piece, gd_send.at[which, d], gd_recv.at[which], r, jnp.int32(2 * d + 1)))
 
     def across(which, act):
-        def go():
-            for n, d in enumerate(PLANE):
-                act(remote(view(which, r), view(which, r), ga_send.at[which, n], ga_recv.at[which, r], peer(d), c))
-
-        when(takes_part(which, r), go)
+        piece = view(which, r)
+        for n, d in enumerate(PLANE):
+            act(remote(piece, piece, ga_send.at[which, n], ga_recv.at[which, r], peer(d), c))
 
     def piece_taken(which):
-        copy = remote(view(which, r), view(which, r), gd_send.at[which, 0], gd_recv.at[which], r, sibling)
-        when(takes_part(which, r), lambda: copy.wait_recv())
+        piece = view(which, r)
+        remote(piece, piece, gd_send.at[which, 0], gd_recv.at[which], r, sibling).wait_recv()
 
     def collect(which):
         def take(d):
             p = lax.rem(r + d, 16)
-            copy = remote(view(which, p), view(which, p), ga_send.at[which, 0], ga_recv.at[which, p], r, sibling)
-            when(takes_part(which, p), lambda: copy.wait_recv())
+            piece = view(which, p)
+            remote(piece, piece, ga_send.at[which, 0], ga_recv.at[which, p], r, sibling).wait_recv()
 
         loop(1, 16, take)
 
     def inverse_piece(p):
         return remote(inv_src.at[p], inv0.at[p], xr_send.at[0, p], xh_recv.at[0], jnp.int32(p), one)
 
-    def next_piece(p):
-        return remote(inv1_src.at[p // 2], inv1.at[p // 2], xr_send.at[1, p], xh_recv.at[1], jnp.int32(p), one)
+    def group(buf, n):
+        lo, hi = GROUPS[n]
+        return buf.at[pl.ds(lo, hi - lo)]
 
     def inverse_first(n, p):
-        return remote(x_src.at[n], xs.at[n], xr_send.at[2 + n, p], xh_recv.at[2 + n], jnp.int32(p), one)
-
-    def from_root(act, copy, step=1):
+        return remote(group(x_src, n), group(xs, n), xr_send.at[1 + n, p], xh_recv.at[1 + n], jnp.int32(p), one)
+
+    def from_root(act, copy):
         for d in PLANE:
-            p = 4 * d[0] + d[1]
-            if p % step == 0:
-                act(copy(p))
+            act(copy(4 * d[0] + d[1]))
         act(copy(0))
 
-    def inverse_copy(n, d):
-        return remote(xs.at[n], xs.at[n], xd_send.at[n, d], xd_recv.at[n], r, jnp.int32(2 * d + 1))
-
     def inverse_down(n, act):
-        for d in FIRST if n == 0 else LINE:
-            act(inverse_copy(n, d))
-
-    def inverse_relay(n, act):
-        if n == 0:
-            relay(act, lambda d: inverse_copy(n, d))
+        for d in LINE:
+            act(remote(group(xs, n), group(xs, n), xd_send.at[n, d], xd_recv.at[n], r, jnp.int32(2 * d + 1)))
 
     def inverse_taken(n):
-        remote(xs.at[n], xs.at[n], xd_send.at[n, 0], xd_recv.at[n], r, sibling).wait_recv()
+        remote(group(xs, n), group(xs, n), xd_send.at[n, 0], xd_recv.at[n], r, sibling).wait_recv()
 
     def parts_pair(n):
-        block = parts.at[0] if n == 0 else parts.at[pl.ds(1, 2)]
+        block = parts.at[0] if n == 0 else parts.at[pl.ds(1, 2), :, pl.ds(64 * (n - 1), 64)]
         return remote(block, block, parts_send.at[n], parts_recv.at[n], r, sibling)
 
     def lead_copy(n):
@@ -477,14 +439,10 @@
 
         def phase(it):
             def store(n, packed):
-                if n < 2:
-                    for part in range(4):
-                        inv1_src[4 * n + part] = packed[8 * part : 8 * part + 8]
-                    if n == 1:
-                        when(it == 1, lambda: from_root(start, next_piece, 2))
-                else:
-                    x_src[n - 2] = packed
-                    when(it == 1, lambda: from_root(start, lambda p: inverse_first(n - 2, p)))
+                x_src[n] = packed
+                for which, (lo, hi) in enumerate(GROUPS):
+                    if hi == n + 1:
+                        when(it == 1, lambda which=which: from_root(start, lambda p: inverse_first(which, p)))
 
             factor_phase(g, store, lambda: when(it == 0, bulk))
             when(it == 0, second_half)
@@ -510,9 +468,7 @@
         across(which, start)
 
     def head_inverses(p):
-        when(takes_part(2, r), lambda: next_piece(p).wait_recv())
-        top_spread(2)
-        for n in range(2):
+        for n in range(3):
             inverse_first(n, p).wait_recv()
             inverse_down(n, start)
 
@@ -524,8 +480,8 @@
         top_spread(0)
         inverse_piece(0).wait_recv()
         top_spread(1)
+        head_inverses(0)
         loop(1, 2, mirror_half)
-        head_inverses(0)
 
     when(aide, aide_main)
     when(both(hub, neither(aide)), lambda: loop(0, 2, mirror_half))
@@ -541,9 +497,8 @@
     when(head, head_main)
 
     def line_spread():
-        for which in range(3):
+        for which in range(2):
             piece_taken(which)
-            relay_piece(which, start)
             across(which, start)
 
     when(both(k == 1, inner), line_spread)
@@ -569,32 +524,25 @@
         rows = lax.broadcasted_iota(jnp.int32, (256, 256), 0)
         cols = lax.broadcasted_iota(jnp.int32, (256, 256), 1)
         work[:, 512:768] = jnp.where(rows == cols, 1.0, 0.0)
-        collect(2)
+        take = {lo: n for n, (lo, hi) in enumerate(GROUPS)}
         for n in range(4):
-            if n < 2:
-                packed = jnp.concatenate([inv1[4 * n + p] for p in range(4)], axis=0)
-            else:
-
-                def arrived(n=n - 2):
-                    inverse_taken(n)
-                    inverse_relay(n, start)
-
-                when(inner, arrived)
-                packed = xs[n - 2]
+            if n in take:
+                when(inner, lambda n=n: inverse_taken(take[n]))
+            packed = xs[n]
             inverse = jnp.concatenate([packed[:, 64:128], packed[:, 0:64]], axis=0)
             lo, hi = 64 * n, 64 * n + 64
             lines = dot32(inverse, work[lo:hi, :], ((1,), (0,)))
             put(1, lo, hi, lines[:, 256:512])
             put(2, lo, hi, lines[:, 512:768])
+            parts_pair(1 + n).start()
             if n < 3:
                 work[hi:256, :] = work[hi:256, :] - dot32(lines[:, hi:256], lines, ((0,), (0,)))
-        parts_pair(1).start()
 
     when(k == 1, assemble)
 
     def parts_take():
-        parts_pair(0).wait_recv()
-        parts_pair(1).wait_recv()
+        for n in range(5):
+            parts_pair(n).wait_recv()
 
     when(k == 0, parts_take)
     when(mate, mirror_take)
@@ -619,27 +567,20 @@
     when(hub, lambda: loop(0, 2, mirror_sent))
 
     def core1_drain():
-        for which in range(3):
+        for which in range(2):
             across(which, sent)
-        for n in range(2):
+        for n in range(5):
             parts_pair(n).wait_send()
 
     when(k == 1, core1_drain)
 
     def line_drain():
-        for which in range(3):
+        for which in range(2):
             down(which, sent)
-        for n in range(2):
+        for n in range(3):
             inverse_down(n, sent)
 
     when(c == 1, line_drain)
-
-    def relay_drain():
-        for which in range(3):
-            relay_piece(which, sent)
-        inverse_relay(0, sent)
-
-    when(both(k == 1, inner), relay_drain)
 
     def aide_drain():
         lead_copy(0).wait_send()
@@ -655,8 +596,7 @@
 
     def root_drain():
         from_root(sent, inverse_piece)
-        from_root(sent, next_piece, 2)
-        for n in range(2):
+        for n in range(3):
             from_root(sent, lambda p, n=n: inverse_first(n, p))
 
     when(root, root_drain)
@@ -681,19 +621,17 @@
         scratch_shapes=[
             pltpu.VMEM((16, 2, 16, 256), bf16),
             pltpu.VMEM((16, 16, 256), f32),
-            pltpu.VMEM((8, 8, 128), f32),
-            pltpu.VMEM((2, 32, 128), f32),
+            pltpu.VMEM((4, 32, 128), f32),
             pltpu.VMEM((3, 256, 256), bf16),
             pltpu.VMEM((384, 512), f32),
-            pltpu.VMEM((2, 32, 128), f32),
+            pltpu.VMEM((4, 32, 128), f32),
             pltpu.VMEM((16, 16, 256), f32),
-            pltpu.VMEM((8, 8, 128), f32),
             pltpu.VMEM((256, 768), f32),
             dma((32, 2)), dma((32,)), dma((33,)), dma((33,)),
             dma((16, 4)), dma((16,)), dma((16,)), dma((16,)),
             dma((2,)), dma((2,)),
-            dma((16,)), dma((2,)), dma((3, 16)), dma((3,)), dma((3, 16)), dma((3, 16)), dma((2,)), dma((2,)),
-            dma((4, 16)), dma((4,)), dma((2, 16)), dma((2,)), dma((3,)),
+            dma((16,)), dma((2,)), dma((2, 16)), dma((2,)), dma((2, 16)), dma((2, 16)), dma((5,)), dma((5,)),
+            dma((4, 16)), dma((4,)), dma((3, 16)), dma((3,)), dma((3,)),
         ],
         compiler_params=pltpu.CompilerParams(
             collective_id=0, has_side_effects=True, vmem_limit_bytes=24 * 1024 * 1024

time: 52.6 us -> 50.6 us (0.962)
  the two profiles are of different devices: /device:TPU:160 before, /device:TPU:153 now
where the time goes in v9:
time: 50.6 us; the launch traced here: 50.5 us
  Pallas kernels  49.7 us (98%)
  between operations  0.8 us (2%)
    pallas_call x1, Pallas kernels, gather(): pl.pallas_call(gather_kernel, out_shape=(jax.ShapeDtypeStruct((4, 2, 256,...  46.7 us
    pallas_call x1, Pallas kernels, update(): pl.pallas_call(update_kernel, out_shape=(jax.ShapeDtypeStruct((1, 4, 2, 2...  3 us

profile of v9, /device:TPU:153, one launch (start us, length us, event | category | flops | bytes accessed | tf_op | source)
XLA Modules:
  0.0 50.5 jit_solution(11542222871083761774)
XLA Ops:
  0.6 46.7 %gather_and_factor.1 = (bf16[4,2,256,256]{3,2,1,0:T(8,128)(2,1)S(1)}, bf16[2,2,2,256,256]{4,3,2,1,0:T(8,128)(2,1)S(1)}, bf16[3,2,256,256]{3,2,1,0:T(8,128)(2,1)S(1)}) custom-call(bf16[1,4,1,2,256,256]{5,4,3,2,1,0:T(8,128)(2,1)} %kern.3), custom_call_target="tpu_custom_call" | custom-call | tf_op jit(solution)/shard_map/gather_and_factor/pallas_call | solution.py:608
  47.3 3.0 %solve_and_update.1 = (f32[1,4,2,256,256]{4,3,2,1,0:T(8,128)}, bf16[1,4,1,2,256,256]{5,4,3,2,1,0:T(8,128)(2,1)}) custom-call(bf16[1,4,1,2,256,256]{5,4,3,2,1,0:T(8,128)(2,1)} %kern.3, bf16[4,2,256,256]{3,2,1,0:T(8,128)(2,1)S(1)} %get-tuple-element.5.acol, bf16[2,2,2,256,256]{4,3,2,1,0:T(8,128)(2,1)S(1)} %get-tuple-element.6.brow, ...), custom_call_target="tpu_custom_call" | custom-call | tf_op jit(solution)/shard_map/solve_and_update/pallas_call | solution.py:707

commit v10 on v8

--- a/solution.py
+++ b/solution.py
@@ -12,10 +12,8 @@
 PLANE = sorted(((a, b) for a in range(4) for b in range(4) if a or b), key=lambda d: -min(d[0], 4 - d[0]) - min(d[1], 4 - d[1]))
 NEAR = ((0, 1), (0, 3), (1, 0), (3, 0))
 LINE = sorted(range(1, 16), key=lambda d: -min(d, 16 - d))
-FIRST = (8, 4, 12, 1, 15)
-RELAY = {4: (2, 6, 3, 5), 8: (7, 9), 12: (10, 14, 11, 13)}
-SKIP = {0: 3, 3: 6, 6: 8, 13: 10, 10: 9}
-BACK = {0: 13, 3: 2, 2: 1, 6: 5, 5: 4, 8: 7, 13: 14, 14: 15, 10: 11, 11: 12}
+SKIP = {0: 3, 3: 6, 6: 7, 7: 8, 13: 10, 10: 9}
+BACK = {0: 13, 3: 2, 2: 1, 6: 5, 5: 4, 13: 14, 14: 15, 10: 11, 11: 12}
 
 
 def lookup(key, pairs):
@@ -177,7 +175,6 @@
     has_back = member(z, list(BACK))
     parent = lookup(z, {v: q for q, v in list(SKIP.items()) + list(BACK.items())})
     children = has_skip.astype(jnp.int32) + has_back.astype(jnp.int32)
-    relay_of = lookup(z, {v: q for q, vs in RELAY.items() for v in vs})
     barrier = pltpu.get_barrier_semaphore()
 
     def remote(src, dst, send, recv, row, col):
@@ -233,7 +230,6 @@
         for d in PLANE:
             signal(peer(d), c)
         when(inner, lambda: signal(r, one))
-        when(relay_of != 0, lambda: signal(r, 2 * relay_of + 1))
 
     when(k == 1, greet_plane)
 
@@ -255,8 +251,6 @@
         plane = jnp.where(k == 1, 15, 0) + jnp.where(both(hub, top), 4, 0)
         line = jnp.where(root, 0, jnp.where(top, 2, jnp.where(k == 0, children, 0)))
         down = jnp.where(c == 1, 15, 0)
-        relays = jnp.where(jnp.logical_or(z == 4, z == 12), 4, jnp.where(z == 8, 2, 0))
-        down = down + jnp.where(k == 1, relays, 0)
         more = jnp.where(root, 15, 0) + jnp.where(aide, 15, 0) + jnp.where(helper, 16, 0)
         pl.semaphore_wait(barrier, 1 + plane + line + down + more)
         when(top, lambda: own_panel.wait())
@@ -374,44 +368,34 @@
     def takes_part(which, row):
         return row >= 0 if which < 2 else lax.rem(row, 2) == 0
 
-    def line_copy(which, d):
+    def down(which, act):
         piece = view(which, r)
-        return remote(piece, piece, gd_send.at[which, d], gd_recv.at[which], r, jnp.int32(2 * d + 1))
-
-    def down(which, act):
+
         def go():
-            for d in FIRST:
-                act(line_copy(which, d))
+            for d in LINE:
+                act(remote(piece, piece, gd_send.at[which, d], gd_recv.at[which], r, jnp.int32(2 * d + 1)))
 
         when(takes_part(which, r), go)
 
-    def relay(act, copy):
-        for q, targets in RELAY.items():
-
-            def go(targets=targets):
-                for d in targets:
-                    act(copy(d))
-
-            when(z == q, go)
-
-    def relay_piece(which, act):
-        when(takes_part(which, r), lambda: relay(act, lambda d: line_copy(which, d)))
-
     def across(which, act):
+        piece = view(which, r)
+
         def go():
             for n, d in enumerate(PLANE):
-                act(remote(view(which, r), view(which, r), ga_send.at[which, n], ga_recv.at[which, r], peer(d), c))
+                act(remote(piece, piece, ga_send.at[which, n], ga_recv.at[which, r], peer(d), c))
 
         when(takes_part(which, r), go)
 
     def piece_taken(which):
-        copy = remote(view(which, r), view(which, r), gd_send.at[which, 0], gd_recv.at[which], r, sibling)
+        piece = view(which, r)
+        copy = remote(piece, piece, gd_send.at[which, 0], gd_recv.at[which], r, sibling)
         when(takes_part(which, r), lambda: copy.wait_recv())
 
     def collect(which):
         def take(d):
             p = lax.rem(r + d, 16)
-            copy = remote(view(which, p), view(which, p), ga_send.at[which, 0], ga_recv.at[which, p], r, sibling)
+            piece = view(which, p)
+            copy = remote(piece, piece, ga_send.at[which, 0], ga_recv.at[which, p], r, sibling)
             when(takes_part(which, p), lambda: copy.wait_recv())
 
         loop(1, 16, take)
@@ -432,22 +416,15 @@
                 act(copy(p))
         act(copy(0))
 
-    def inverse_copy(n, d):
-        return remote(xs.at[n], xs.at[n], xd_send.at[n, d], xd_recv.at[n], r, jnp.int32(2 * d + 1))
-
     def inverse_down(n, act):
-        for d in FIRST if n == 0 else LINE:
-            act(inverse_copy(n, d))
-
-    def inverse_relay(n, act):
-        if n == 0:
-            relay(act, lambda d: inverse_copy(n, d))
+        for d in LINE:
+            act(remote(xs.at[n], xs.at[n], xd_send.at[n, d], xd_recv.at[n], r, jnp.int32(2 * d + 1)))
 
     def inverse_taken(n):
         remote(xs.at[n], xs.at[n], xd_send.at[n, 0], xd_recv.at[n], r, sibling).wait_recv()
 
     def parts_pair(n):
-        block = parts.at[0] if n == 0 else parts.at[pl.ds(1, 2)]
+        block = parts.at[0] if n == 0 else parts.at[pl.ds(1, 2), :, pl.ds(64 * (n - 1), 64)]
         return remote(block, block, parts_send.at[n], parts_recv.at[n], r, sibling)
 
     def lead_copy(n):
@@ -524,8 +501,8 @@
         top_spread(0)
         inverse_piece(0).wait_recv()
         top_spread(1)
+        head_inverses(0)
         loop(1, 2, mirror_half)
-        head_inverses(0)
 
     when(aide, aide_main)
     when(both(hub, neither(aide)), lambda: loop(0, 2, mirror_half))
@@ -543,7 +520,6 @@
     def line_spread():
         for which in range(3):
             piece_taken(which)
-            relay_piece(which, start)
             across(which, start)
 
     when(both(k == 1, inner), line_spread)
@@ -574,27 +550,22 @@
             if n < 2:
                 packed = jnp.concatenate([inv1[4 * n + p] for p in range(4)], axis=0)
             else:
-
-                def arrived(n=n - 2):
-                    inverse_taken(n)
-                    inverse_relay(n, start)
-
-                when(inner, arrived)
+                when(inner, lambda n=n: inverse_taken(n - 2))
                 packed = xs[n - 2]
             inverse = jnp.concatenate([packed[:, 64:128], packed[:, 0:64]], axis=0)
             lo, hi = 64 * n, 64 * n + 64
             lines = dot32(inverse, work[lo:hi, :], ((1,), (0,)))
             put(1, lo, hi, lines[:, 256:512])
             put(2, lo, hi, lines[:, 512:768])
+            parts_pair(1 + n).start()
             if n < 3:
                 work[hi:256, :] = work[hi:256, :] - dot32(lines[:, hi:256], lines, ((0,), (0,)))
-        parts_pair(1).start()
 
     when(k == 1, assemble)
 
     def parts_take():
-        parts_pair(0).wait_recv()
-        parts_pair(1).wait_recv()
+        for n in range(5):
+            parts_pair(n).wait_recv()
 
     when(k == 0, parts_take)
     when(mate, mirror_take)
@@ -621,7 +592,7 @@
     def core1_drain():
         for which in range(3):
             across(which, sent)
-        for n in range(2):
+        for n in range(5):
             parts_pair(n).wait_send()
 
     when(k == 1, core1_drain)
@@ -633,13 +604,6 @@
             inverse_down(n, sent)
 
     when(c == 1, line_drain)
-
-    def relay_drain():
-        for which in range(3):
-            relay_piece(which, sent)
-        inverse_relay(0, sent)
-
-    when(both(k == 1, inner), relay_drain)
 
     def aide_drain():
         lead_copy(0).wait_send()
@@ -692,7 +656,7 @@
             dma((32, 2)), dma((32,)), dma((33,)), dma((33,)),
             dma((16, 4)), dma((16,)), dma((16,)), dma((16,)),
             dma((2,)), dma((2,)),
-            dma((16,)), dma((2,)), dma((3, 16)), dma((3,)), dma((3, 16)), dma((3, 16)), dma((2,)), dma((2,)),
+            dma((16,)), dma((2,)), dma((3, 16)), dma((3,)), dma((3, 16)), dma((3, 16)), dma((5,)), dma((5,)),
             dma((4, 16)), dma((4,)), dma((2, 16)), dma((2,)), dma((3,)),
         ],
         compiler_params=pltpu.CompilerParams(

time: 52.6 us -> 49.3 us (0.937)
  the two profiles are of different devices: /device:TPU:160 before, /device:TPU:145 now
where the time goes in v10:
time: 49.3 us; the launch traced here: 49.2 us
  Pallas kernels  48.4 us (98%)
  between operations  0.8 us (2%)
    pallas_call x1, Pallas kernels, gather(): pl.pallas_call(gather_kernel, out_shape=(jax.ShapeDtypeStruct((4, 2, 256,...  45.4 us
    pallas_call x1, Pallas kernels, update(): pl.pallas_call(update_kernel, out_shape=(jax.ShapeDtypeStruct((1, 4, 2, 2...  3 us

profile of v10, /device:TPU:145, one launch (start us, length us, event | category | flops | bytes accessed | tf_op | source)
XLA Modules:
  0.0 49.2 jit_solution(15571825957940857349)
XLA Ops:
  0.6 45.4 %gather_and_factor.1 = (bf16[4,2,256,256]{3,2,1,0:T(8,128)(2,1)S(1)}, bf16[2,2,2,256,256]{4,3,2,1,0:T(8,128)(2,1)S(1)}, bf16[3,2,256,256]{3,2,1,0:T(8,128)(2,1)S(1)}) custom-call(bf16[1,4,1,2,256,256]{5,4,3,2,1,0:T(8,128)(2,1)} %kern.3), custom_call_target="tpu_custom_call" | custom-call | tf_op jit(solution)/shard_map/gather_and_factor/pallas_call | solution.py:632
  46.0 3.0 %solve_and_update.1 = (f32[1,4,2,256,256]{4,3,2,1,0:T(8,128)}, bf16[1,4,1,2,256,256]{5,4,3,2,1,0:T(8,128)(2,1)}) custom-call(bf16[1,4,1,2,256,256]{5,4,3,2,1,0:T(8,128)(2,1)} %kern.3, bf16[4,2,256,256]{3,2,1,0:T(8,128)(2,1)S(1)} %get-tuple-element.5.acol, bf16[2,2,2,256,256]{4,3,2,1,0:T(8,128)(2,1)S(1)} %get-tuple-element.6.brow, ...), custom_call_target="tpu_custom_call" | custom-call | tf_op jit(solution)/shard_map/solve_and_update/pallas_call | solution.py:733

commit v11 on v10

--- a/solution.py
+++ b/solution.py
@@ -12,6 +12,7 @@
 PLANE = sorted(((a, b) for a in range(4) for b in range(4) if a or b), key=lambda d: -min(d[0], 4 - d[0]) - min(d[1], 4 - d[1]))
 NEAR = ((0, 1), (0, 3), (1, 0), (3, 0))
 LINE = sorted(range(1, 16), key=lambda d: -min(d, 16 - d))
+GATE = 13
 SKIP = {0: 3, 3: 6, 6: 7, 7: 8, 13: 10, 10: 9}
 BACK = {0: 13, 3: 2, 2: 1, 6: 5, 5: 4, 13: 14, 14: 15, 10: 11, 11: 12}
 
@@ -272,8 +273,8 @@
     def column_pair(col):
         return remote(acol.at[:, col], acol.at[:, col], p_sib_send.at[32], p_sib_recv.at[32], r, sibling)
 
-    def panel_top(col, act):
-        for m in range(16):
+    def panel_top(col, act, lo=0, hi=16):
+        for m in range(lo, hi):
             act(panel_copy(col, m, 0))
             act(panel_copy(col, m, 1))
 
@@ -498,9 +499,11 @@
         panel_top(0, start)
         loop(0, 1, mirror_half)
         lead_from(1, 0).wait_recv()
+        inverse_piece(0).wait_recv()
+        panel_top(1, sent, 0, GATE)
+        panel_top(0, sent, 0, GATE)
+        top_spread(1)
         top_spread(0)
-        inverse_piece(0).wait_recv()
-        top_spread(1)
         head_inverses(0)
         loop(1, 2, mirror_half)
 
@@ -510,15 +513,16 @@
     def head_main():
         lead_from(0, 1).wait_recv()
         when(neither(helper), lambda: lead_from(1, 2).wait_recv())
+        inverse_piece(1).wait_recv()
+        panel_top(1, sent, 0, GATE)
+        top_spread(1)
         top_spread(0)
-        inverse_piece(1).wait_recv()
-        top_spread(1)
         head_inverses(2)
 
     when(head, head_main)
 
     def line_spread():
-        for which in range(3):
+        for which in (1, 0, 2):
             piece_taken(which)
             across(which, start)
 
@@ -581,8 +585,9 @@
 
     def top_drain():
         column_pair(k).wait_send()
-        when(neither(root), lambda: panel_top(k, sent))
-        when(aide, lambda: panel_top(0, sent))
+        when(both(k == 0, neither(root)), lambda: panel_top(0, sent))
+        when(k == 1, lambda: panel_top(1, sent, GATE))
+        when(aide, lambda: panel_top(0, sent, GATE))
 
     when(top, top_drain)
     when(both(mate, r < 2), lambda: feeds(sent))

time: 49.3 us -> 49.3 us (level)
  no operation moved by 1% of the time
where the time goes in v11:
time: 49.3 us; the launch traced here: 49.2 us
  Pallas kernels  48.4 us (98%)
  between operations  0.8 us (2%)
    pallas_call x1, Pallas kernels, gather(): pl.pallas_call(gather_kernel, out_shape=(jax.ShapeDtypeStruct((4, 2, 256,...  45.4 us
    pallas_call x1, Pallas kernels, update(): pl.pallas_call(update_kernel, out_shape=(jax.ShapeDtypeStruct((1, 4, 2, 2...  3 us

profile of v11, /device:TPU:145, one launch (start us, length us, event | category | flops | bytes accessed | tf_op | source)
XLA Modules:
  0.0 49.2 jit_solution(6929956609997510509)
XLA Ops:
  0.6 45.4 %gather_and_factor.1 = (bf16[4,2,256,256]{3,2,1,0:T(8,128)(2,1)S(1)}, bf16[2,2,2,256,256]{4,3,2,1,0:T(8,128)(2,1)S(1)}, bf16[3,2,256,256]{3,2,1,0:T(8,128)(2,1)S(1)}) custom-call(bf16[1,4,1,2,256,256]{5,4,3,2,1,0:T(8,128)(2,1)} %kern.3), custom_call_target="tpu_custom_call" | custom-call | tf_op jit(solution)/shard_map/gather_and_factor/pallas_call | solution.py:637
  46.0 3.0 %solve_and_update.1 = (f32[1,4,2,256,256]{4,3,2,1,0:T(8,128)}, bf16[1,4,1,2,256,256]{5,4,3,2,1,0:T(8,128)(2,1)}) custom-call(bf16[1,4,1,2,256,256]{5,4,3,2,1,0:T(8,128)(2,1)} %kern.3, bf16[4,2,256,256]{3,2,1,0:T(8,128)(2,1)S(1)} %get-tuple-element.5.acol, bf16[2,2,2,256,256]{4,3,2,1,0:T(8,128)(2,1)S(1)} %get-tuple-element.6.brow, ...), custom_call_target="tpu_custom_call" | custom-call | tf_op jit(solution)/shard_map/solve_and_update/pallas_call | solution.py:738

commit v12 on v10

--- a/solution.py
+++ b/solution.py
@@ -12,8 +12,8 @@
 PLANE = sorted(((a, b) for a in range(4) for b in range(4) if a or b), key=lambda d: -min(d[0], 4 - d[0]) - min(d[1], 4 - d[1]))
 NEAR = ((0, 1), (0, 3), (1, 0), (3, 0))
 LINE = sorted(range(1, 16), key=lambda d: -min(d, 16 - d))
-SKIP = {0: 3, 3: 6, 6: 7, 7: 8, 13: 10, 10: 9}
-BACK = {0: 13, 3: 2, 2: 1, 6: 5, 5: 4, 13: 14, 14: 15, 10: 11, 11: 12}
+SKIP = {0: 3, 3: 5, 5: 6, 6: 7, 13: 11, 11: 9, 9: 8}
+BACK = {0: 13, 3: 2, 2: 1, 5: 4, 13: 14, 14: 15, 11: 12, 9: 10}
 
 
 def lookup(key, pairs):

time: 49.3 us -> 48.5 us (0.984)
  the two profiles are of different devices: /device:TPU:145 before, /device:TPU:32 now
where the time goes in v12:
time: 48.5 us; the launch traced here: 48.4 us
  Pallas kernels  47.6 us (98%)
  between operations  0.8 us (2%)
    pallas_call x1, Pallas kernels, gather(): pl.pallas_call(gather_kernel, out_shape=(jax.ShapeDtypeStruct((4, 2, 256,...  44.6 us
    pallas_call x1, Pallas kernels, update(): pl.pallas_call(update_kernel, out_shape=(jax.ShapeDtypeStruct((1, 4, 2, 2...  3 us

profile of v12, /device:TPU:32, one launch (start us, length us, event | category | flops | bytes accessed | tf_op | source)
XLA Modules:
  0.0 48.4 jit_solution(4565564623653548309)
XLA Ops:
  0.6 44.6 %gather_and_factor.1 = (bf16[4,2,256,256]{3,2,1,0:T(8,128)(2,1)S(1)}, bf16[2,2,2,256,256]{4,3,2,1,0:T(8,128)(2,1)S(1)}, bf16[3,2,256,256]{3,2,1,0:T(8,128)(2,1)S(1)}) custom-call(bf16[1,4,1,2,256,256]{5,4,3,2,1,0:T(8,128)(2,1)} %kern.3), custom_call_target="tpu_custom_call" | custom-call | tf_op jit(solution)/shard_map/gather_and_factor/pallas_call | solution.py:632
  45.2 3.0 %solve_and_update.1 = (f32[1,4,2,256,256]{4,3,2,1,0:T(8,128)}, bf16[1,4,1,2,256,256]{5,4,3,2,1,0:T(8,128)(2,1)}) custom-call(bf16[1,4,1,2,256,256]{5,4,3,2,1,0:T(8,128)(2,1)} %kern.3, bf16[4,2,256,256]{3,2,1,0:T(8,128)(2,1)S(1)} %get-tuple-element.5.acol, bf16[2,2,2,256,256]{4,3,2,1,0:T(8,128)(2,1)S(1)} %get-tuple-element.6.brow, ...), custom_call_target="tpu_custom_call" | custom-call | tf_op jit(solution)/shard_map/solve_and_update/pallas_call | solution.py:733

commit v13 on v12

--- a/solution.py
+++ b/solution.py
@@ -12,8 +12,8 @@
 PLANE = sorted(((a, b) for a in range(4) for b in range(4) if a or b), key=lambda d: -min(d[0], 4 - d[0]) - min(d[1], 4 - d[1]))
 NEAR = ((0, 1), (0, 3), (1, 0), (3, 0))
 LINE = sorted(range(1, 16), key=lambda d: -min(d, 16 - d))
-SKIP = {0: 3, 3: 5, 5: 6, 6: 7, 13: 11, 11: 9, 9: 8}
-BACK = {0: 13, 3: 2, 2: 1, 5: 4, 13: 14, 14: 15, 11: 12, 9: 10}
+SKIP = {0: 2, 2: 4, 4: 6, 6: 7, 13: 11, 11: 9, 9: 8}
+BACK = {0: 13, 2: 1, 4: 3, 6: 5, 13: 14, 14: 15, 11: 12, 9: 10}
 
 
 def lookup(key, pairs):

time: 48.5 us -> 48.7 us (level)
  the two profiles are of different devices: /device:TPU:32 before, /device:TPU:177 now
where the time goes in v13:
time: 48.7 us; the launch traced here: 48.6 us
  Pallas kernels  47.8 us (98%)
  between operations  0.8 us (2%)
    pallas_call x1, Pallas kernels, gather(): pl.pallas_call(gather_kernel, out_shape=(jax.ShapeDtypeStruct((4, 2, 256,...  44.8 us
    pallas_call x1, Pallas kernels, update(): pl.pallas_call(update_kernel, out_shape=(jax.ShapeDtypeStruct((1, 4, 2, 2...  3 us

profile of v13, /device:TPU:177, one launch (start us, length us, event | category | flops | bytes accessed | tf_op | source)
XLA Modules:
  0.0 48.6 jit_solution(8226064986792167185)
XLA Ops:
  0.6 44.8 %gather_and_factor.1 = (bf16[4,2,256,256]{3,2,1,0:T(8,128)(2,1)S(1)}, bf16[2,2,2,256,256]{4,3,2,1,0:T(8,128)(2,1)S(1)}, bf16[3,2,256,256]{3,2,1,0:T(8,128)(2,1)S(1)}) custom-call(bf16[1,4,1,2,256,256]{5,4,3,2,1,0:T(8,128)(2,1)} %kern.3), custom_call_target="tpu_custom_call" | custom-call | tf_op jit(solution)/shard_map/gather_and_factor/pallas_call | solution.py:632
  45.4 3.0 %solve_and_update.1 = (f32[1,4,2,256,256]{4,3,2,1,0:T(8,128)}, bf16[1,4,1,2,256,256]{5,4,3,2,1,0:T(8,128)(2,1)}) custom-call(bf16[1,4,1,2,256,256]{5,4,3,2,1,0:T(8,128)(2,1)} %kern.3, bf16[4,2,256,256]{3,2,1,0:T(8,128)(2,1)S(1)} %get-tuple-element.5.acol, bf16[2,2,2,256,256]{4,3,2,1,0:T(8,128)(2,1)S(1)} %get-tuple-element.6.brow, ...), custom_call_target="tpu_custom_call" | custom-call | tf_op jit(solution)/shard_map/solve_and_update/pallas_call | solution.py:733
